TPU v7x, 256 devices: a whole 4x4x8 slice. The times are simulated.
256 devices in a mesh: grp: 32 (over z_hi, y, core), sp: 8 (over z_lo, x).
Axes of the slice: x: 4, y: 4, z: 8 (z_hi: 4, z_lo: 2; z = z_hi * 2 + z_lo), core: 2. Of those that a mesh axis runs over, the one named last changes fastest.
Arguments:
- queries: bfloat16 [32768, 2048], P(('grp', 'sp')), may hold values from -6 to 6
- keys: bfloat16 [32768, 256], P(('grp', 'sp')), may hold values from -32 to 32
- values: bfloat16 [32768, 256], P(('grp', 'sp')), may hold values from -6 to 6
- grad_out: bfloat16 [32768, 2048], P(('grp', 'sp')), may hold values from -6 to 6
- group_of_row: int32 [32768, 1], P(('grp', 'sp')), may hold values from 0 to 31; in each aligned block of 128 rows (0 to 127, 128 to 255, ...) at most 8 rows name the same one
- head_slot: int32 [16], replicated, may hold values from 0 to 15, each once
Outputs:
- grad_queries: bfloat16 [32768, 2048], P(('grp', 'sp'))
- grad_keys: bfloat16 [32768, 256], P(('grp', 'sp'))
- grad_values: bfloat16 [32768, 256], P(('grp', 'sp'))
Inputs may be any that keep to these rules, and one draw needn't show every extreme that they name: `group_of_row`: among the 128 rows of one device no plan group is named more than 8 times; on some device some group is named exactly 8 times. `head_slot`: each slot number appears once.
All inputs are finite; a program needn't handle non-finite values.
Results may differ from a plain program's by a relative error of at most 0.035.
Values may be sent and summed in bfloat16 or wider, within the bound.
No kernel may reach another device: no remote copies, remote signals or barrier semaphores. Data moves between devices by JAX's collectives and lax.ppermute only.
A program may use at most 64 MiB of HBM per device.

v0:
```python
import jax
import jax.numpy as jnp
from jax import lax
from jax.sharding import PartitionSpec as P

HD = 128
QH = 16
KVH = 2
GROUP_HEADS = 7


def head_rows(array, heads):
    return array.reshape(array.shape[0], heads, array.shape[1] // heads)


def contract_last(left, right):
    return lax.dot_general(
        left, right, (((1,), (1,)), ((), ())), preferred_element_type=jnp.float32
    )


def contract_first(left, right):
    return lax.dot_general(
        left, right, (((0,), (0,)), ((), ())), preferred_element_type=jnp.float32
    )


def per_device(queries, keys, values, grad_out, group_of_row, head_slot):
    tok_rows = queries.shape[0]
    groups = lax.axis_size("grp")
    shards = lax.axis_size("sp")
    capacity = 2 * tok_rows // groups
    slot_count = groups * capacity
    local_heads = QH // shards
    softmax_scale = HD ** (-0.5)
    width_q = QH * HD
    width_k = KVH * HD
    real_slot = head_slot < GROUP_HEADS * KVH
    kv_slot = jnp.minimum(head_slot // GROUP_HEADS, KVH - 1)
    masked = (head_rows(grad_out, QH) * real_slot.astype(jnp.bfloat16)[None, :, None]).reshape(
        tok_rows, width_q
    )
    row_group = group_of_row[:, 0]
    member = (row_group[:, None] == jnp.arange(groups, dtype=jnp.int32)[None, :]).astype(jnp.int32)
    before = jnp.sum((jnp.cumsum(member, axis=0) - member) * member, axis=1)
    target = row_group * capacity + before
    placed = target[None, :] == jnp.arange(slot_count, dtype=jnp.int32)[:, None]
    placer = placed.astype(jnp.bfloat16)
    packed = jnp.dot(
        placer,
        jnp.concatenate([queries, masked, keys, values], axis=1),
        preferred_element_type=jnp.float32,
    ).astype(jnp.bfloat16)
    sent_q = packed[:, :width_q]
    sent_g = packed[:, width_q : 2 * width_q]
    sent_k = packed[:, 2 * width_q : 2 * width_q + width_k]
    sent_v = packed[:, 2 * width_q + width_k :]
    sent_doc = jnp.sum(placed.astype(jnp.int32), axis=1) - 1
    slot_q, slot_g, slot_k, slot_v, slot_doc = (
        lax.all_to_all(sent_q, "grp", split_axis=0, concat_axis=0, tiled=True),
        lax.all_to_all(sent_g, "grp", split_axis=0, concat_axis=0, tiled=True),
        lax.all_to_all(sent_k, "grp", split_axis=0, concat_axis=0, tiled=True),
        lax.all_to_all(sent_v, "grp", split_axis=0, concat_axis=0, tiled=True),
        lax.all_to_all(sent_doc, "grp", split_axis=0, concat_axis=0, tiled=True),
    )
    head_q, head_g = (
        lax.all_to_all(slot_q, "sp", split_axis=1, concat_axis=0, tiled=True),
        lax.all_to_all(slot_g, "sp", split_axis=1, concat_axis=0, tiled=True),
    )
    all_k, all_v, all_doc = (
        lax.all_gather(slot_k, "sp", axis=0, tiled=True),
        lax.all_gather(slot_v, "sp", axis=0, tiled=True),
        lax.all_gather(slot_doc, "sp", axis=0, tiled=True),
    )
    group_rows = all_doc.shape[0]
    block_rows = min(512, group_rows)
    blocks = group_rows // block_rows
    first_head = lax.axis_index("sp") * local_heads
    my_kv = lax.dynamic_slice_in_dim(kv_slot, first_head, local_heads)
    kv_choice = (my_kv[:, None] == jnp.arange(KVH, dtype=jnp.int32)[None, :]).astype(jnp.bfloat16)
    key_local = jnp.einsum(
        "lcd,hc->lhd", head_rows(all_k, KVH), kv_choice, preferred_element_type=jnp.float32
    ).astype(jnp.bfloat16)
    value_local = jnp.einsum(
        "lcd,hc->lhd", head_rows(all_v, KVH), kv_choice, preferred_element_type=jnp.float32
    ).astype(jnp.bfloat16)
    query_heads = head_rows(head_q, local_heads)
    grad_heads = head_rows(head_g, local_heads)

    def one_step(step_index, carry):
        key_sum, value_sum, query_grad = carry
        row_start = step_index // local_heads * block_rows
        head_index = step_index % local_heads
        kv_now = my_kv[head_index]
        query_block = lax.dynamic_slice(
            query_heads, (row_start, head_index, 0), (block_rows, 1, HD)
        )[:, 0]
        grad_block = lax.dynamic_slice(grad_heads, (row_start, head_index, 0), (block_rows, 1, HD))[
            :, 0
        ]
        key_one = lax.dynamic_index_in_dim(key_local, head_index, 1, keepdims=False)
        value_one = lax.dynamic_index_in_dim(value_local, head_index, 1, keepdims=False)
        doc_block = lax.dynamic_slice_in_dim(all_doc, row_start, block_rows)
        scores = contract_last(query_block, key_one) * softmax_scale
        visible = doc_block[:, None] == all_doc[None, :]
        scores = jnp.where(visible, scores, -1e30)
        row_max = jnp.max(scores, axis=1, keepdims=True)
        shifted = jnp.exp(scores - row_max)
        attend = shifted / jnp.sum(shifted, axis=1, keepdims=True)
        grad_attend = contract_last(grad_block, value_one)
        row_dot = jnp.sum(attend * grad_attend, axis=1, keepdims=True)
        grad_score = (attend * (grad_attend - row_dot) * softmax_scale).astype(jnp.bfloat16)
        q_grad = jnp.dot(grad_score, key_one, preferred_element_type=jnp.float32).astype(
            jnp.bfloat16
        )
        k_part = contract_first(grad_score, query_block)
        v_part = contract_first(attend.astype(jnp.bfloat16), grad_block)
        key_sum = lax.dynamic_update_index_in_dim(
            key_sum,
            lax.dynamic_index_in_dim(key_sum, kv_now, 1, keepdims=False) + k_part,
            kv_now,
            1,
        )
        value_sum = lax.dynamic_update_index_in_dim(
            value_sum,
            lax.dynamic_index_in_dim(value_sum, kv_now, 1, keepdims=False) + v_part,
            kv_now,
            1,
        )
        query_grad = lax.dynamic_update_slice(
            query_grad, q_grad[:, None, :], (row_start, head_index, 0)
        )
        return (key_sum, value_sum, query_grad)

    start_state = (
        jnp.zeros((group_rows, KVH, HD), jnp.float32),
        jnp.zeros((group_rows, KVH, HD), jnp.float32),
        jnp.zeros((group_rows, local_heads, HD), jnp.bfloat16),
    )
    key_sum, value_sum, query_grad = lax.fori_loop(0, blocks * local_heads, one_step, start_state)
    key_total, value_total = (
        lax.psum_scatter(
            key_sum.reshape(group_rows, width_k).astype(jnp.bfloat16),
            "sp",
            scatter_dimension=0,
            tiled=True,
        ).astype(jnp.float32),
        lax.psum_scatter(
            value_sum.reshape(group_rows, width_k).astype(jnp.bfloat16),
            "sp",
            scatter_dimension=0,
            tiled=True,
        ).astype(jnp.float32),
    )
    home_k, home_v = (
        lax.all_to_all(
            key_total.astype(jnp.bfloat16), "grp", split_axis=0, concat_axis=0, tiled=True
        ),
        lax.all_to_all(
            value_total.astype(jnp.bfloat16), "grp", split_axis=0, concat_axis=0, tiled=True
        ),
    )
    flat_dq = query_grad.reshape(group_rows, local_heads * HD)
    slot_dq = lax.all_to_all(flat_dq, "sp", split_axis=0, concat_axis=1, tiled=True)
    rows_dq = lax.all_to_all(slot_dq, "grp", split_axis=0, concat_axis=0, tiled=True)
    gathered = jnp.concatenate([rows_dq, home_k, home_v], axis=1)
    unpacked = contract_first(placer, gathered).astype(jnp.bfloat16)
    return (
        unpacked[:, :width_q],
        unpacked[:, width_q : width_q + width_k],
        unpacked[:, width_q + width_k :],
    )


def solution(mesh):
    in_specs = (
        P(("grp", "sp"), None),
        P(("grp", "sp"), None),
        P(("grp", "sp"), None),
        P(("grp", "sp"), None),
        P(("grp", "sp"), None),
        P(),
    )
    out_specs = (P(("grp", "sp"), None), P(("grp", "sp"), None), P(("grp", "sp"), None))
    return jax.shard_map(
        per_device, mesh=mesh, in_specs=in_specs, out_specs=out_specs, check_vma=False
    )
```

profile of v0, /device:TPU:1, one launch (start us, length us, event | category | flops | bytes accessed | tf_op | source)
XLA Modules:
  0.0 643.8 jit_solution(5544983888455949380)
XLA Ops:
  10.4 12.8 %all-to-all-start = ((s32[32,8,1]{1,2,0:T(1,128)}), s32[32,8,1]{1,2,0:T(1,128)S(1)}, u32[]{:S(2)}, u32[]{:S(2)}) async-start(s32[32,8,1]{1,2,0:T(1,128)} %bitcast.11), calls=%async_computation | async-start | bytes 32768 | tf_op jit(solution)/shard_map/all_to_all | solution.py:64
  29.0 3.5 all-to-all-done
  32.5 17.2 %all_to_all.135 = bf16[32,8,256]{2,1,0:T(8,128)(2,1)} all-to-all(bf16[32,8,256]{2,1,0:T(8,128)(2,1)S(1)} %get-tuple-element.330), channel_id=1, replica_groups=mesh['grp'=32,'sp'=8] {'grp'}, dimensions={0} | all-to-all | bytes 262144 | tf_op jit(solution)/shard_map/all_to_all | solution.py:62
  49.7 3.7 all-to-all-start.6
  56.1 8.4 %all-to-all-done.6 = bf16[32,8,256]{2,1,0:T(8,128)(2,1)S(1)} async-done(((bf16[32,8,256]{2,1,0:T(8,128)(2,1)}), bf16[32,8,256]{2,1,0:T(8,128)(2,1)S(1)}, u32[]{:S(2)}, u32[]{:S(2)}) %all-to-all-start.6) | async-done | bytes 131104 | tf_op jit(solution)/shard_map/all_to_all | solution.py:63
  64.5 31.7 %all_to_all.136 = bf16[32,8,2048]{2,1,0:T(8,128)(2,1)S(1)} all-to-all(bf16[32,8,2048]{2,1,0:T(8,128)(2,1)S(1)} %get-tuple-element.332), channel_id=1, replica_groups=mesh['grp'=32,'sp'=8] {'grp'}, dimensions={0} | all-to-all | bytes 2097152 | tf_op jit(solution)/shard_map/all_to_all | solution.py:60
  96.2 5.6 all-to-all-start.4
  104.0 27.9 %all-to-all-done.4 = bf16[32,8,2048]{2,1,0:T(8,128)(2,1)S(1)} async-done(((bf16[32,8,2048]{2,1,0:T(8,128)(2,1)}), bf16[32,8,2048]{2,1,0:T(8,128)(2,1)S(1)}, u32[]{:S(2)}, u32[]{:S(2)}) %all-to-all-start.4) | async-done | bytes 1048608 | tf_op jit(solution)/shard_map/all_to_all | solution.py:61
  131.9 4.1 all-to-all-start.2
  138.3 15.2 %all-to-all-done.2 = bf16[256,8,256]{2,0,1:T(8,128)(2,1)S(1)} async-done(((bf16[256,8,256]{2,0,1:T(8,128)(2,1)}), bf16[256,8,256]{2,0,1:T(8,128)(2,1)S(1)}, u32[]{:S(2)}, u32[]{:S(2)}) %all-to-all-start.2) | async-done | bytes 1048608 | tf_op jit(solution)/shard_map/all_to_all | solution.py:67
  153.4 4.0 all-to-all-start.5
  158.9 21.0 %all-gather = s32[8,1,256]{2,1,0:T(1,128)S(1)} all-gather(s32[1,1,256]{2,1,0:T(1,128)S(1)} %reshape.88), channel_id=1, replica_groups=mesh['grp'=32,'sp'=8] {'sp'}, dimensions={0}, use_global_device_ids=true | all-gather | bytes 9216 | tf_op jit(solution)/shard_map/all_gather | solution.py:73
  183.8 13.1 %all-gather.6.cloned.1.call-done = bf16[2048,256]{1,0:T(8,128)(2,1)} async-done(((bf16[256,256]{1,0:T(8,128)(2,1)}), bf16[2048,256]{1,0:T(8,128)(2,1)}) %all-gather.6.cloned.1.call-update) | async-done | bytes 1048592 | tf_op jit(solution)/shard_map/all_gather | solution.py:72
  207.8 280.3 %while.19 = (s32[]{:T(128)}, f32[2048,2,128]{0,2,1:T(8,128)}, f32[2048,2,128]{0,2,1:T(8,128)}, bf16[2048,2,128]{0,2,1:T(8,128)(2,1)}, s32[2]{0:T(128)S(1)}, /*in...) while((s32[]{:T(128)}, f32[2048,2,128]{0,2,1:T(8,128)}, ...), condition=%wide.region_7.8_spmd, body=%wide.region_3.7_spmd.sunk | while | flops 1362688512 | bytes 76193216 | solution.py:140
  230.4 4.6 fusion.74
  245.7 2.8 multiply_reduce_fusion.2
  265.4 4.6 fusion.74
  300.5 4.6 fusion.74
  315.8 2.8 multiply_reduce_fusion.2
  335.5 4.6 fusion.74
  370.6 4.6 fusion.74
  405.6 4.6 fusion.74
  440.7 4.6 fusion.74
  475.7 4.6 fusion.74
  488.2 2.9 convert_element_type.83
  494.0 3.8 all-to-all-start.7
  497.8 36.4 %reduce-scatter.3.cloned.1.call-done = bf16[256,256]{0,1:T(8,128)(2,1)} async-done(((bf16[2048,256]{0,1:T(8,128)(2,1)}), bf16[256,256]{0,1:T(8,128)(2,1)}) %reduce-scatter.3.cloned.1.call-update) | async-done | bytes 131088 | tf_op jit(solution)/shard_map/reduce_scatter | solution.py:142
  535.9 13.3 %all-to-all-start.9 = ((bf16[32,8,256]{2,1,0:T(8,128)(2,1)}), bf16[32,8,256]{2,1,0:T(8,128)(2,1)S(1)}, u32[]{:S(2)}, u32[]{:S(2)}) async-start(bf16[32,8,256]{2,1,0:T(8,128)(2,1)} %bitcast.28), calls=%async_computation.10 | async-start | bytes 262144 | tf_op jit(solution)/shard_map/all_to_all | solution.py:156
  549.2 28.9 %reduce-scatter.5.cloned.1.call-done = bf16[256,256]{0,1:T(8,128)(2,1)} async-done(((bf16[2048,256]{0,1:T(8,128)(2,1)}), bf16[256,256]{0,1:T(8,128)(2,1)}) %reduce-scatter.5.cloned.1.call-update) | async-done | bytes 131088 | tf_op jit(solution)/shard_map/reduce_scatter | solution.py:148
  579.8 13.4 %all-to-all-start.10 = ((bf16[32,8,256]{2,1,0:T(8,128)(2,1)}), bf16[32,8,256]{2,1,0:T(8,128)(2,1)S(1)}, u32[]{:S(2)}, u32[]{:S(2)}) async-start(bf16[32,8,256]{2,1,0:T(8,128)(2,1)} %bitcast.31), calls=%async_computation.12 | async-start | bytes 262144 | tf_op jit(solution)/shard_map/all_to_all | solution.py:159
  594.8 9.8 %all-to-all-done.10 = bf16[32,8,256]{2,1,0:T(8,128)(2,1)S(1)} async-done(((bf16[32,8,256]{2,1,0:T(8,128)(2,1)}), bf16[32,8,256]{2,1,0:T(8,128)(2,1)S(1)}, u32[]{:S(2)}, u32[]{:S(2)}) %all-to-all-start.10) | async-done | bytes 131104 | tf_op jit(solution)/shard_map/all_to_all | solution.py:159
  604.6 30.8 %all_to_all.137 = bf16[32,8,2048]{2,1,0:T(8,128)(2,1)S(1)} all-to-all(bf16[32,8,2048]{2,1,0:T(8,128)(2,1)S(1)} %all_to_all.115), channel_id=1, replica_groups=mesh['grp'=32,'sp'=8] {'grp'}, dimensions={0} | all-to-all | bytes 2097152 | tf_op jit(solution)/shard_map/all_to_all | solution.py:165
  (217 shorter events, 263.5 us)
Async XLA Ops:
  10.4 22.1 %all-to-all-start = ((s32[32,8,1]{1,2,0:T(1,128)}), s32[32,8,1]{1,2,0:T(1,128)S(1)}, u32[]{:S(2)}, u32[]{:S(2)}) async-start(s32[32,8,1]{1,2,0:T(1,128)} %bitcast.11), calls=%async_computation | async-start | bytes 32768 | tf_op jit(solution)/shard_map/all_to_all | solution.py:64
  26.9 1.4 copy-start.3
  49.7 14.9 %all-to-all-start.6 = ((bf16[32,8,256]{2,1,0:T(8,128)(2,1)}), bf16[32,8,256]{2,1,0:T(8,128)(2,1)S(1)}, u32[]{:S(2)}, u32[]{:S(2)}) async-start(bf16[32,8,256]{2,1,0:T(8,128)(2,1)} %get-tuple-element.329), calls=%async_computation.6 | async-start | bytes 262144 | tf_op jit(solution)/shard_map/all_to_all | solution.py:63
  64.5 38.3 %copy-start.4 = (bf16[32,8,256]{2,1,0:T(8,128)(2,1)}, bf16[32,8,256]{2,1,0:T(8,128)(2,1)S(1)}, u32[]{:S(2)}) copy-start(bf16[32,8,256]{2,1,0:T(8,128)(2,1)S(1)} %all-to-all-done.6) | copy-start | bytes 393220
  96.2 35.7 %all-to-all-start.4 = ((bf16[32,8,2048]{2,1,0:T(8,128)(2,1)}), bf16[32,8,2048]{2,1,0:T(8,128)(2,1)S(1)}, u32[]{:S(2)}, u32[]{:S(2)}) async-start(bf16[32,8,2048]{2,1,0:T(8,128)(2,1)} %get-tuple-element.331), calls=%async_computation.4 | async-start | bytes 2097152 | tf_op jit(solution)/shard_map/all_to_all | solution.py:61
  101.8 78.1 %all-gather.4.cloned.1.call-start = ((), (), s32[]{:S(2)}) async-start(), calls=%async_computation.13 | async-start | bytes 1179648 | tf_op jit(solution)/shard_map/all_gather | solution.py:71
  131.9 21.6 %all-to-all-start.2 = ((bf16[256,8,256]{2,0,1:T(8,128)(2,1)}), bf16[256,8,256]{2,0,1:T(8,128)(2,1)S(1)}, u32[]{:S(2)}, u32[]{:S(2)}) async-start(bf16[256,8,256]{2,0,1:T(8,128)(2,1)} %copy.58), calls=%async_computation.2 | async-start | bytes 2097152 | tf_op jit(solution)/shard_map/all_to_all | solution.py:67
  136.0 60.9 %all-gather.6.cloned.1.call-start = ((), (), s32[]{:S(2)}) async-start(), calls=%async_computation.14 | async-start | bytes 1179648 | tf_op jit(solution)/shard_map/all_gather | solution.py:72
  137.1 20.5 %copy-start.5 = (s32[16]{0:T(128)S(1)}, s32[16]{0:T(128)}, u32[]{:S(2)}) copy-start(s32[16]{0:T(128)} %param.13) | copy-start | bytes 196
  153.4 48.6 %all-to-all-start.5 = ((bf16[256,8,256]{2,0,1:T(8,128)(2,1)}), bf16[256,8,256]{2,0,1:T(8,128)(2,1)S(1)}, u32[]{:S(2)}, u32[]{:S(2)}) async-start(bf16[256,8,256]{2,0,1:T(8,128)(2,1)} %copy.60), calls=%async_computation.5 | async-start | bytes 2097152 | tf_op jit(solution)/shard_map/all_to_all | solution.py:68
  157.5 376.7 %reduce-scatter.3.cloned.1.call-start = ((), (), s32[]{:S(2)}) async-start(), calls=%async_computation.15 | async-start | bytes 1179648 | tf_op jit(solution)/shard_map/reduce_scatter | solution.py:142
  209.9 3.5 copy-start
  245.0 3.5 copy-start
  280.0 3.5 copy-start
  315.1 3.5 copy-start
  350.1 3.5 copy-start
  385.1 3.5 copy-start
  420.2 3.5 copy-start
  455.2 3.5 copy-start
  488.2 3.0 copy-start.1
  491.1 1.4 copy-start.2
  491.1 87.0 %reduce-scatter.5.cloned.1.call-start = ((), (), s32[]{:S(2)}) async-start(), calls=%async_computation.16 | async-start | bytes 1179648 | tf_op jit(solution)/shard_map/reduce_scatter | solution.py:148
  494.0 41.8 %all-to-all-start.7 = ((bf16[8,256,256]{1,2,0:T(8,128)(2,1)}), bf16[8,256,256]{1,2,0:T(8,128)(2,1)S(1)}, u32[]{:S(2)}, u32[]{:S(2)}) async-start(bf16[8,256,256]{1,2,0:T(8,128)(2,1)} %copy.67), calls=%async_computation.7 | async-start | bytes 2097152 | tf_op jit(solution)/shard_map/all_to_all | solution.py:164
  535.9 43.9 %all-to-all-start.9 = ((bf16[32,8,256]{2,1,0:T(8,128)(2,1)}), bf16[32,8,256]{2,1,0:T(8,128)(2,1)S(1)}, u32[]{:S(2)}, u32[]{:S(2)}) async-start(bf16[32,8,256]{2,1,0:T(8,128)(2,1)} %bitcast.28), calls=%async_computation.10 | async-start | bytes 262144 | tf_op jit(solution)/shard_map/all_to_all | solution.py:156
  579.8 24.8 %all-to-all-start.10 = ((bf16[32,8,256]{2,1,0:T(8,128)(2,1)}), bf16[32,8,256]{2,1,0:T(8,128)(2,1)S(1)}, u32[]{:S(2)}, u32[]{:S(2)}) async-start(bf16[32,8,256]{2,1,0:T(8,128)(2,1)} %bitcast.31), calls=%async_computation.12 | async-start | bytes 262144 | tf_op jit(solution)/shard_map/all_to_all | solution.py:159
Sparse Core Ops, SparseCore 0:
  104.4 46.0 all-gather.3
  152.8 44.0 all-gather.5
  491.2 42.9 reduce-scatter.2
  536.6 41.4 reduce-scatter.4
where the time goes:
time: 648 us; the launch traced here: 644 us
  local copies, waits for them, and re-layouts  166 us (26%)
  waiting for transfers between devices  145 us (22%)
  matrix products  116 us (18%)
  blocking collectives  101 us (16%)
  starting transfers between devices  60.9 us (9%)
  other arithmetic  26.4 us (4%)
  loops' own time  16 us (2%)
  between operations  14 us (2%)
    dot_general x17, matrix products, contract_first(): lax.dot_general(left, right, (((0,), (0,)), ((), ())), preferred_element_...  58.7 us
    dynamic_update_slice x16, local copies, waits for them, and re-layouts, one_step(): lax.dynamic_update_index_in_dim(value_sum, lax.dynamic_index_in_dim(value...  42.2 us
    dynamic_slice x16, local copies, waits for them, and re-layouts, one_step(): lax.dynamic_index_in_dim(value_sum, kv_now, 1, keepdims=False) + v_part  38.8 us
    dot_general x16, matrix products, contract_last(): lax.dot_general(left, right, (((1,), (1,)), ((), ())), preferred_element_...  38.6 us
    reduce_scatter x1, waiting for transfers between devices, per_device(): lax.psum_scatter(key_sum.reshape(group_rows, width_k).astype(jnp.bfloat16...  36.4 us
    all_to_all x1, blocking collectives, per_device(): lax.all_to_all(sent_q, 'grp', split_axis=0, concat_axis=0, tiled=True)  31.7 us
    dynamic_slice x16, local copies, waits for them, and re-layouts, one_step(): lax.dynamic_index_in_dim(key_sum, kv_now, 1, keepdims=False) + k_part  30.9 us
    all_to_all x1, blocking collectives, per_device(): lax.all_to_all(slot_dq, 'grp', split_axis=0, concat_axis=0, tiled=True)  30.8 us
  transfers between devices with their start and end apart: 12, of which 8 were waited for; matrix products, arithmetic and copies ran while one was open for 4% of the time, Pallas kernels for 0%

commit v1 on v0

v1 whole, which is shorter than its diff:
```python
import math

import jax
import jax.numpy as jnp
from jax import lax
from jax.experimental import pallas as pl
from jax.experimental.pallas import tpu as pltpu
from jax.sharding import Mesh
from jax.sharding import PartitionSpec as P

HD = 128
QH = 16
KVH = 2
GROUP_HEADS = 7
CAP = 8
HALF = QH // KVH
EMPTY = 64.0
NEG = -1e30
AXES = ("zh", "y", "c", "zl", "x")
PLANE = ("y", "c", "x")
COLUMN = ("zh", "zl")
BF = jnp.bfloat16
F32 = jnp.float32
KEY_TILE = 256
VMEM = 56 * 1024 * 1024


def contract_last(left, right):
    return lax.dot_general(left, right, (((1,), (1,)), ((), ())), preferred_element_type=F32)


def dot(left, right):
    return jnp.dot(left, right, preferred_element_type=F32)


def row_slots(group_ref):
    rows = group_ref.shape[0]
    across = jnp.broadcast_to(group_ref[...].astype(F32), (rows, rows))
    along = across.T
    first = lax.broadcasted_iota(jnp.int32, (rows, rows), 0)
    second = lax.broadcasted_iota(jnp.int32, (rows, rows), 1)
    return across, along, across == along, first, second


def placer_of(group_ref, slots):
    rows = group_ref.shape[0]
    across, along, same, first, second = row_slots(group_ref)
    before = jnp.sum(jnp.where(same & (first < second), 1.0, 0.0), axis=0, keepdims=True)
    target = (along[:1] * CAP + before).astype(jnp.int32)
    return jnp.where(lax.broadcasted_iota(jnp.int32, (slots, rows), 0) == target, 1.0, 0.0).astype(BF)


def taker_of(group_ref, slots):
    rows = group_ref.shape[0]
    across, along, same, first, second = row_slots(group_ref)
    before = jnp.sum(jnp.where(same & (second < first), 1.0, 0.0), axis=1, keepdims=True)
    target = (across[:, :1] * CAP + before).astype(jnp.int32)
    return jnp.where(lax.broadcasted_iota(jnp.int32, (rows, slots), 1) == target, 1.0, 0.0).astype(BF)


def pack_kv_kernel(group_ref, key_ref, value_ref, out_ref):
    slots = out_ref.shape[0]
    placer = placer_of(group_ref, slots)
    filled = jnp.sum(placer.astype(F32), axis=1, keepdims=True)
    lane = lax.broadcasted_iota(jnp.int32, (slots, HD), 1)
    mark = jnp.where((lane == 0) & (filled < 0.5), EMPTY, 0.0)
    for c in range(KVH):
        cols = slice(c * HD, (c + 1) * HD)
        out_ref[:, 2 * c * HD : (2 * c + 1) * HD] = dot(placer, key_ref[:, cols]).astype(BF)
        out_ref[:, (2 * c + 1) * HD : (2 * c + 2) * HD] = (dot(placer, value_ref[:, cols]) + mark).astype(BF)


def pack_qg_kernel(order_ref, group_ref, query_ref, grad_ref, out_q_ref, out_g_ref, placer_ref):
    at = pl.program_id(0)

    @pl.when(at == 0)
    def _():
        placer_ref[...] = placer_of(group_ref, placer_ref.shape[0])

    placer = placer_ref[...]
    real = jnp.where(at % HALF < GROUP_HEADS, 1.0, 0.0)
    out_q_ref[...] = dot(placer, query_ref[...]).astype(BF)
    out_g_ref[...] = (dot(placer, grad_ref[...]) * real).astype(BF)


def attend_kernel(
    q_ref, g_ref, k_ref, v_ref, dkv_ref, dq_ref, s_ref, p_ref, dk_ref, dv_ref, bias_ref, kt_ref
):
    at = pl.program_id(0)
    keys = k_ref.shape[0]
    rows = q_ref.shape[0]
    tiles = keys // KEY_TILE
    scale = HD ** (-0.5)
    unit = scale * math.log2(math.e)

    @pl.when(at % HALF == 0)
    def _():
        dk_ref[...] = jnp.zeros_like(dk_ref)
        dv_ref[...] = jnp.zeros_like(dv_ref)
        empty = v_ref[:, :1].astype(F32) > 0.5 * EMPTY
        bias_ref[...] = jnp.broadcast_to(jnp.where(empty, NEG, 0.0), bias_ref.shape)
        kt_ref[...] = k_ref[...].T

    q = q_ref[...]
    g = g_ref[...]
    top = jnp.full((8, rows), -3e38, F32)
    for t in range(tiles):
        part = slice(t * KEY_TILE, (t + 1) * KEY_TILE)
        bias = bias_ref[part, :]
        s = contract_last(k_ref[part, :], q) + jnp.concatenate([bias] * (rows // HD), axis=1)
        s_ref[part, :] = s
        top = jnp.maximum(top, jnp.max(s.reshape(KEY_TILE // 8, 8, rows), axis=0))
    top = jnp.max(top, axis=0, keepdims=True)
    total = jnp.zeros((8, rows), F32)
    cross = jnp.zeros((8, rows), F32)
    for t in range(tiles):
        part = slice(t * KEY_TILE, (t + 1) * KEY_TILE)
        dp = contract_last(v_ref[part, :], g)
        e = jnp.exp2((s_ref[part, :] - top) * unit)
        s_ref[part, :] = e
        p_ref[part, :] = dp
        total = total + jnp.sum(e.reshape(KEY_TILE // 8, 8, rows), axis=0)
        cross = cross + jnp.sum((e * dp).reshape(KEY_TILE // 8, 8, rows), axis=0)
    share = 1.0 / jnp.sum(total, axis=0, keepdims=True)
    row_dot = jnp.sum(cross, axis=0, keepdims=True) * share
    dqt = jnp.zeros((HD, rows), F32)
    for t in range(tiles):
        part = slice(t * KEY_TILE, (t + 1) * KEY_TILE)
        p = s_ref[part, :] * share
        ds = (p * (p_ref[part, :] - row_dot)).astype(BF)
        dv_ref[part, :] += dot(p.astype(BF), g)
        dk_ref[part, :] += dot(ds, q)
        dqt += dot(kt_ref[:, part], ds)
    dq_ref[...] = (dqt * scale).T.astype(BF)

    @pl.when(at % HALF == HALF - 1)
    def _():
        dkv_ref[:, :HD] = (dk_ref[...] * scale).astype(BF)
        dkv_ref[:, HD:] = dv_ref[...].astype(BF)


def unpack_q_kernel(order_ref, group_ref, dq_ref, out_ref, taker_ref):
    @pl.when(pl.program_id(0) == 0)
    def _():
        taker_ref[...] = taker_of(group_ref, taker_ref.shape[1])

    out_ref[...] = dot(taker_ref[...], dq_ref[...]).astype(BF)


def unpack_kv_kernel(group_ref, dkv_ref, dk_ref, dv_ref):
    taker = taker_of(group_ref, dkv_ref.shape[0])
    for c in range(KVH):
        cols = slice(c * HD, (c + 1) * HD)
        dk_ref[:, cols] = dot(taker, dkv_ref[:, 2 * c * HD : (2 * c + 1) * HD]).astype(BF)
        dv_ref[:, cols] = dot(taker, dkv_ref[:, (2 * c + 1) * HD : (2 * c + 2) * HD]).astype(BF)


def struct(*shape):
    return jax.ShapeDtypeStruct(shape, BF)


def params():
    return pltpu.CompilerParams(vmem_limit_bytes=VMEM)


def per_device(queries, keys, values, grad_out, group_of_row, head_slot):
    rows = queries.shape[0]
    groups = lax.axis_size(PLANE)
    column = lax.axis_size(COLUMN)
    slots = groups * CAP
    width_q = QH * HD
    width_kv = 2 * KVH * HD
    all_keys = column * slots

    def over_plane(array):
        return lax.all_to_all(array, PLANE, split_axis=0, concat_axis=0, tiled=True)

    position = jnp.arange(QH, dtype=jnp.int32)
    head_at = jnp.where(
        position % HALF == GROUP_HEADS,
        KVH * GROUP_HEADS + position // HALF,
        position // HALF * GROUP_HEADS + position % HALF,
    )
    order = jnp.sum(
        jnp.where(head_at[:, None] == head_slot[None, :], position[None, :], 0), axis=1
    ).astype(jnp.int32)

    sent_kv = pl.pallas_call(
        pack_kv_kernel,
        out_shape=struct(slots, width_kv),
        compiler_params=params(),
        name="pack_kv",
    )(group_of_row, keys, values)
    home_kv = over_plane(sent_kv)
    all_kv = lax.all_gather(home_kv, COLUMN, axis=0, tiled=True)

    whole = pl.BlockSpec((rows, 1), lambda p, order: (0, 0))
    from_slot = pl.BlockSpec((rows, HD), lambda p, order: (0, order[p]))
    to_sorted = pl.BlockSpec((slots, HD), lambda p, order: (0, p))
    sent_q, sent_g = pl.pallas_call(
        pack_qg_kernel,
        out_shape=(struct(slots, width_q), struct(slots, width_q)),
        grid_spec=pltpu.PrefetchScalarGridSpec(
            num_scalar_prefetch=1,
            grid=(QH,),
            in_specs=[whole, from_slot, from_slot],
            out_specs=[to_sorted, to_sorted],
            scratch_shapes=[pltpu.VMEM((slots, rows), BF)],
        ),
        compiler_params=params(),
        name="pack_qg",
    )(order, group_of_row, queries, grad_out)
    home_q = over_plane(sent_q)
    home_g = over_plane(sent_g)

    one_head = pl.BlockSpec((slots, HD), lambda p: (0, p))
    pairs = QH * slots * all_keys
    grad_kv, grad_q = pl.pallas_call(
        attend_kernel,
        out_shape=(struct(all_keys, width_kv), struct(slots, width_q)),
        grid=(QH,),
        in_specs=[
            one_head,
            one_head,
            pl.BlockSpec((all_keys, HD), lambda p: (0, p // HALF * 2)),
            pl.BlockSpec((all_keys, HD), lambda p: (0, p // HALF * 2 + 1)),
        ],
        out_specs=[pl.BlockSpec((all_keys, 2 * HD), lambda p: (0, p // HALF)), one_head],
        scratch_shapes=[
            pltpu.VMEM((all_keys, slots), F32),
            pltpu.VMEM((all_keys, slots), F32),
            pltpu.VMEM((all_keys, HD), F32),
            pltpu.VMEM((all_keys, HD), F32),
            pltpu.VMEM((all_keys, HD), F32),
            pltpu.VMEM((HD, all_keys), BF),
        ],
        compiler_params=params(),
        cost_estimate=pl.CostEstimate(
            flops=10 * HD * pairs,
            bytes_accessed=2 * (3 * slots * width_q + 2 * all_keys * width_kv),
            transcendentals=pairs,
        ),
        name="attend",
    )(home_q, home_g, all_kv, all_kv)

    kv_total = lax.psum_scatter(grad_kv, COLUMN, scatter_dimension=0, tiled=True)
    back_q = over_plane(grad_q)
    back_kv = over_plane(kv_total)

    out_q = pl.pallas_call(
        unpack_q_kernel,
        out_shape=struct(rows, width_q),
        grid_spec=pltpu.PrefetchScalarGridSpec(
            num_scalar_prefetch=1,
            grid=(QH,),
            in_specs=[whole, to_sorted],
            out_specs=from_slot,
            scratch_shapes=[pltpu.VMEM((rows, slots), BF)],
        ),
        compiler_params=params(),
        name="unpack_q",
    )(order, group_of_row, back_q)
    out_k, out_v = pl.pallas_call(
        unpack_kv_kernel,
        out_shape=(struct(rows, KVH * HD), struct(rows, KVH * HD)),
        compiler_params=params(),
        name="unpack_kv",
    )(group_of_row, back_kv)
    return out_q, out_k, out_v


def solution(mesh):
    fine = Mesh(mesh.devices.reshape(4, 4, 2, 2, 4), AXES)
    split = P(AXES, None)
    return jax.shard_map(
        per_device,
        mesh=fine,
        in_specs=(split, split, split, split, split, P()),
        out_specs=(split, split, split),
        check_vma=False,
    )
```

time: 648 us -> 194 us (0.30)
  local copies, waits for them, and re-layouts: 166 us -> 3.28 us
  waiting for transfers between devices: 145 us -> 15.9 us
  matrix products: 116 us -> 0 us
  Pallas kernels: 0 us -> 64.6 us
  starting transfers between devices: 60.9 us -> 12 us
  other arithmetic: 26.4 us -> 1.36 us
  blocking collectives: 101 us -> 80.6 us
  loops' own time: 16 us -> 0 us
    dot_general x44 -> x0, matrix products: 116 us -> none  [the longest x17 58.7 us: contract_first(): lax.dot_general(left, right, (((0,), (0,)), ((), ())), preferred_element_...]
    dynamic_slice x49 -> x0, local copies, waits for them, and re-layouts: 75.1 us -> none  [the longest x16 38.8 us: one_step(): lax.dynamic_index_in_dim(value_sum, kv_now, 1, keepdims=False) + v_part]
    all_to_all x8 -> x1, waiting for transfers between devices: 64.8 us -> 0.01 us  [over_plane(): return lax.all_to_all(array, PLANE, split_axis=0, concat_axis=0, tiled=True)]
    pallas_call x0 -> x5, Pallas kernels: none -> 64.6 us  [the longest x1 39.1 us: per_device(): pl.pallas_call(attend_kernel, out_shape=(struct(all_keys, width_kv), stru...]
    dynamic_update_slice x40 -> x0, local copies, waits for them, and re-layouts: 61 us -> none  [the longest x16 42.2 us: one_step(): lax.dynamic_update_index_in_dim(value_sum, lax.dynamic_index_in_dim(value...]
    reduce_scatter x2 -> x1, waiting for transfers between devices: 65.3 us -> 15.8 us  [per_device(): lax.psum_scatter(grad_kv, COLUMN, scatter_dimension=0, tiled=True)]
    all_to_all x8 -> x1, starting transfers between devices: 60.7 us -> 11.9 us  [over_plane(): return lax.all_to_all(array, PLANE, split_axis=0, concat_axis=0, tiled=True)]
    all_gather x1 -> x0, blocking collectives: 21 us -> none  [per_device(): lax.all_gather(slot_doc, 'sp', axis=0, tiled=True)]
  transfers between devices with their start and end apart: 12 -> 3, of which waited for: 8 -> 1; matrix products, arithmetic and copies ran while one was open for 4% -> 1% of each run, Pallas kernels for 0% -> 11%
where the time goes in v1:
time: 194 us; the launch traced here: 192 us
  blocking collectives  80.6 us (42%)
  Pallas kernels  64.6 us (33%)
  waiting for transfers between devices  15.9 us (8%)
  between operations  14.1 us (7%)
  starting transfers between devices  12 us (6%)
  local copies, waits for them, and re-layouts  3.28 us (2%)
    all_to_all x4, blocking collectives, over_plane(): return lax.all_to_all(array, PLANE, split_axis=0, concat_axis=0, tiled=True)  80.6 us
    pallas_call x1, Pallas kernels, per_device(): pl.pallas_call(attend_kernel, out_shape=(struct(all_keys, width_kv), stru...  39.1 us
    reduce_scatter x1, waiting for transfers between devices, per_device(): lax.psum_scatter(grad_kv, COLUMN, scatter_dimension=0, tiled=True)  15.8 us
    all_to_all x1, starting transfers between devices, over_plane(): return lax.all_to_all(array, PLANE, split_axis=0, concat_axis=0, tiled=True)  11.9 us
    pallas_call x1, Pallas kernels, per_device(): pl.pallas_call(pack_qg_kernel, out_shape=(struct(slots, width_q), struct(...  10.8 us
    pallas_call x1, Pallas kernels, per_device(): pl.pallas_call(unpack_q_kernel, out_shape=struct(rows, width_q), grid_spe...  10.7 us
  transfers between devices with their start and end apart: 3, of which 1 were waited for; matrix products, arithmetic and copies ran while one was open for 1% of the time, Pallas kernels for 11%

profile of v1, /device:TPU:1, one launch (start us, length us, event | category | flops | bytes accessed | tf_op | source)
XLA Modules:
  0.0 191.8 jit_solution(5099205247882195228)
XLA Ops:
  7.2 0.0 all-gather.2.cloned.1.call-start
  7.2 1.4 copy.15.group_ref
  8.6 2.0 %pack_kv.1 = bf16[256,512]{1,0:T(8,128)(2,1)} custom-call(s32[128,1]{1,0:T(8,128)} %copy.15.group_ref, bf16[128,256]{1,0:T(8,128)(2,1)} %key_ref.1, bf16[128,256]{1,0:T(8,128)(2,1)} %value_ref.1), custom_call_target="tpu_custom_call" | custom-call | tf_op jit(solution)/shard_map/pack_kv/pallas_call | solution.py:188
  10.6 17.6 %all_to_all.56 = bf16[32,8,512]{2,1,0:T(8,128)(2,1)} all-to-all(bf16[32,8,512]{2,1,0:T(8,128)(2,1)} %bitcast.12), channel_id=1, replica_groups=mesh['zh'=4,'y'=4,'c'=2,'zl'=2,'x'=4] {'y','c','x'}, dimensions={0} | all-to-all | bytes 524288 | tf_op jit(solution)/shard_map/all_to_all | solution.py:176
  28.2 0.0 all-gather.2.cloned.1.call-update
  28.2 0.0 reduce-scatter.2.cloned.1.call-start
  28.3 1.4 select_reduce_fusion.order_ref
  29.6 10.8 %pack_qg.1 = (bf16[256,2048]{1,0:T(8,128)(2,1)}, bf16[256,2048]{1,0:T(8,128)(2,1)}) custom-call(s32[16]{0:T(128)} %select_reduce_fusion.order_ref, s32[128,1]{1,0:T(8,128)} %copy.15.group_ref, bf16[128,2048]{1,0:T(8,128)(2,1)} %query_ref.1, bf16[128,2048]{1,0:T(8,128)(2,1)} %grad_ref.1), custom_call_target="tpu_custom_call" | custom-call | tf_op jit(solution)/shard_map/pack_qg/pallas_call | solution.py:200
  40.4 0.0 copy-start.2
  40.4 20.6 %all_to_all.57 = bf16[32,8,2048]{2,1,0:T(8,128)(2,1)} all-to-all(bf16[32,8,2048]{2,1,0:T(8,128)(2,1)} %bitcast.17), channel_id=1, replica_groups=mesh['zh'=4,'y'=4,'c'=2,'zl'=2,'x'=4] {'y','c','x'}, dimensions={0} | all-to-all | bytes 2097152 | tf_op jit(solution)/shard_map/all_to_all | solution.py:176
  61.0 0.0 copy-done.2
  61.0 21.2 %all_to_all.58 = bf16[32,8,2048]{2,1,0:T(8,128)(2,1)} all-to-all(bf16[32,8,2048]{2,1,0:T(8,128)(2,1)S(1)} %bitcast.16), channel_id=1, replica_groups=mesh['zh'=4,'y'=4,'c'=2,'zl'=2,'x'=4] {'y','c','x'}, dimensions={0} | all-to-all | bytes 2097152 | tf_op jit(solution)/shard_map/all_to_all | solution.py:176
  82.2 0.0 all-gather.2.cloned.1.call-done.k_ref.v_ref
  82.2 39.1 %attend.1 = (bf16[2048,512]{1,0:T(8,128)(2,1)}, bf16[256,2048]{1,0:T(8,128)(2,1)}) custom-call(bf16[256,2048]{1,0:T(8,128)(2,1)} %bitcast.15, bf16[256,2048]{1,0:T(8,128)(2,1)} %bitcast.14, bf16[2048,512]{1,0:T(8,128)(2,1)} %all-gather.2.cloned.1.call-done.k_ref.v_ref, bf16[2048,512]{1,0:T(8,128)(2,1)} %all-gather.2.cloned.1.call-done.k_ref.v_ref), custom_call_target="tpu_custom_call" | custom-call | flops 10737418240 | bytes 7340032 | tf_op jit(solution)/shard_map/attend/pallas_call | solution.py:218
  121.3 0.0 copy-start.1
  121.3 0.0 reduce-scatter.2.cloned.1.call-update
  121.3 1.2 copy-done.1
  122.5 21.2 %all_to_all.59 = bf16[32,8,2048]{2,1,0:T(8,128)(2,1)} all-to-all(bf16[32,8,2048]{2,1,0:T(8,128)(2,1)S(1)} %bitcast.13), channel_id=1, replica_groups=mesh['zh'=4,'y'=4,'c'=2,'zl'=2,'x'=4] {'y','c','x'}, dimensions={0} | all-to-all | bytes 2097152 | tf_op jit(solution)/shard_map/all_to_all | solution.py:176
  143.7 15.8 %reduce-scatter.2.cloned.1.call-done = bf16[256,512]{1,0:T(8,128)(2,1)} async-done(((bf16[2048,512]{1,0:T(8,128)(2,1)}), bf16[256,512]{1,0:T(8,128)(2,1)}) %reduce-scatter.2.cloned.1.call-update) | async-done | bytes 262160 | tf_op jit(solution)/shard_map/reduce_scatter | solution.py:246
  159.5 11.9 %all-to-all-start.4 = ((bf16[32,8,512]{2,1,0:T(8,128)(2,1)}), bf16[32,8,512]{2,1,0:T(8,128)(2,1)S(1)}, u32[]{:S(2)}, u32[]{:S(2)}) async-start(bf16[32,8,512]{2,1,0:T(8,128)(2,1)} %bitcast.19), calls=%async_computation.5 | async-start | bytes 524288 | tf_op jit(solution)/shard_map/all_to_all | solution.py:176
  171.5 10.7 %unpack_q.1 = bf16[128,2048]{1,0:T(8,128)(2,1)} custom-call(s32[16]{0:T(128)} %select_reduce_fusion.order_ref, s32[128,1]{1,0:T(8,128)} %copy.15.group_ref, bf16[256,2048]{1,0:T(8,128)(2,1)} %bitcast.10), custom_call_target="tpu_custom_call" | custom-call | tf_op jit(solution)/shard_map/unpack_q/pallas_call | solution.py:250
  182.2 0.0 all-to-all-done.4
  182.2 0.0 copy-start
  182.2 0.7 copy-done
  182.9 2.1 %unpack_kv.1 = (bf16[128,256]{1,0:T(8,128)(2,1)}, bf16[128,256]{1,0:T(8,128)(2,1)}) custom-call(s32[128,1]{1,0:T(8,128)} %copy.15.group_ref, bf16[256,512]{1,0:T(8,128)(2,1)} %bitcast.11), custom_call_target="tpu_custom_call" | custom-call | tf_op jit(solution)/shard_map/unpack_kv/pallas_call | solution.py:263
  (1 shorter events, 0.0 us)
Async XLA Ops:
  7.2 75.1 %all-gather.2.cloned.1.call-start = ((), (), s32[]{:S(2)}) async-start(), calls=%async_computation.6 | async-start | bytes 2359296 | tf_op jit(solution)/shard_map/all_gather | solution.py:195
  28.2 131.3 %reduce-scatter.2.cloned.1.call-start = ((), (), s32[]{:S(2)}) async-start(), calls=%async_computation.7 | async-start | bytes 2359296 | tf_op jit(solution)/shard_map/reduce_scatter | solution.py:246
  40.4 20.6 %copy-start.2 = (bf16[256,2048]{1,0:T(8,128)(2,1)S(1)}, bf16[256,2048]{1,0:T(8,128)(2,1)}, u32[]{:S(2)}) copy-start(bf16[256,2048]{1,0:T(8,128)(2,1)} %get-tuple-element.9) | copy-start | bytes 3145732
  121.3 1.2 copy-start.1
  159.5 22.6 %all-to-all-start.4 = ((bf16[32,8,512]{2,1,0:T(8,128)(2,1)}), bf16[32,8,512]{2,1,0:T(8,128)(2,1)S(1)}, u32[]{:S(2)}, u32[]{:S(2)}) async-start(bf16[32,8,512]{2,1,0:T(8,128)(2,1)} %bitcast.19), calls=%async_computation.5 | async-start | bytes 524288 | tf_op jit(solution)/shard_map/all_to_all | solution.py:176
  182.2 0.7 copy-start
Sparse Core Ops, SparseCore 0:
  28.3 36.7 all-gather.1
  121.4 38.0 reduce-scatter.1

commit v2 on v1

v2 whole, which is shorter than its diff:
```python
import math

import jax
import jax.numpy as jnp
from jax import lax
from jax.experimental import pallas as pl
from jax.experimental.pallas import tpu as pltpu
from jax.sharding import Mesh
from jax.sharding import PartitionSpec as P

HD = 128
QH = 16
KVH = 2
GROUP_HEADS = 7
CAP = 8
HALF = QH // KVH
EMPTY = 64.0
NEG = -1e30
AXES = ("zh", "y", "c", "zl", "x")
PLANE = ("y", "c", "x")
COLUMN = ("zh", "zl")
BF = jnp.bfloat16
F32 = jnp.float32
KEY_TILE = 512
VMEM = 60 * 1024 * 1024


def contract_last(left, right):
    return lax.dot_general(left, right, (((1,), (1,)), ((), ())), preferred_element_type=F32)


def dot(left, right):
    return jnp.dot(left, right, preferred_element_type=F32)


def columns(at, width=HD):
    return pl.ds(pl.multiple_of(at * width, width), width)


def place_of(head):
    real = head < KVH * GROUP_HEADS
    return jnp.where(
        real,
        head + (head >= GROUP_HEADS).astype(jnp.int32),
        (head - KVH * GROUP_HEADS) * HALF + GROUP_HEADS,
    )


def row_groups(group_ref):
    rows = group_ref.shape[1]
    along = jnp.broadcast_to(group_ref[...].astype(F32), (rows, rows))
    across = along.T
    first = lax.broadcasted_iota(jnp.int32, (rows, rows), 0)
    second = lax.broadcasted_iota(jnp.int32, (rows, rows), 1)
    return along, across, along == across, first < second


def placer_of(group_ref, slots):
    rows = group_ref.shape[1]
    along, across, same, earlier = row_groups(group_ref)
    before = jnp.sum(jnp.where(same & earlier, 1.0, 0.0), axis=0, keepdims=True)
    target = (along[:1] * CAP + before).astype(jnp.int32)
    return jnp.where(lax.broadcasted_iota(jnp.int32, (slots, rows), 0) == target, 1.0, 0.0).astype(BF)


def taker_of(group_ref, slots):
    rows = group_ref.shape[1]
    along, across, same, earlier = row_groups(group_ref)
    later = lax.broadcasted_iota(jnp.int32, (rows, rows), 0) > lax.broadcasted_iota(
        jnp.int32, (rows, rows), 1
    )
    before = jnp.sum(jnp.where(same & later, 1.0, 0.0), axis=1, keepdims=True)
    target = (across[:, :1] * CAP + before).astype(jnp.int32)
    return jnp.where(lax.broadcasted_iota(jnp.int32, (rows, slots), 1) == target, 1.0, 0.0).astype(BF)


def pack_kv_kernel(group_ref, key_ref, value_ref, out_ref):
    slots = out_ref.shape[0]
    placer = placer_of(group_ref, slots)
    filled = jnp.sum(placer.astype(F32), axis=1, keepdims=True)
    lane = lax.broadcasted_iota(jnp.int32, (slots, HD), 1)
    mark = jnp.where((lane == 0) & (filled < 0.5), EMPTY, 0.0)
    for c in range(KVH):
        cols = slice(c * HD, (c + 1) * HD)
        out_ref[:, 2 * c * HD : (2 * c + 1) * HD] = dot(placer, key_ref[:, cols]).astype(BF)
        out_ref[:, (2 * c + 1) * HD : (2 * c + 2) * HD] = (dot(placer, value_ref[:, cols]) + mark).astype(BF)


def pack_qg_kernel(head_ref, group_ref, query_ref, grad_ref, out_ref):
    placer = placer_of(group_ref, out_ref.shape[0])
    for slot in range(QH):
        cols = slice(slot * HD, (slot + 1) * HD)
        head = head_ref[slot]
        place = place_of(head)
        real = (head < KVH * GROUP_HEADS).astype(F32)
        out_ref[:, columns(place)] = dot(placer, query_ref[:, cols]).astype(BF)
        out_ref[:, columns(QH + place)] = (dot(placer, grad_ref[:, cols]) * real).astype(BF)


def attend_kernel(qg_ref, kv_ref, dkv_ref, dq_ref, s_ref, p_ref, dk_ref, dv_ref, bias_ref, kt_ref):
    keys = kv_ref.shape[0]
    rows = qg_ref.shape[0]
    scale = HD ** (-0.5)
    unit = scale * math.log2(math.e)
    parts = [slice(t, t + KEY_TILE) for t in range(0, keys, KEY_TILE)]
    low = jnp.full((8, rows), -3e38, F32)

    def fold(tile):
        return tile.reshape(tile.shape[0] // 8, 8, rows)

    def one_key_head(c, _):
        k_cols, v_cols = columns(2 * c), columns(2 * c + 1)
        dk_ref[...] = jnp.zeros_like(dk_ref)
        dv_ref[...] = jnp.zeros_like(dv_ref)
        empty = kv_ref[:, v_cols][:, :1].astype(F32) > 0.5 * EMPTY
        bias_ref[...] = jnp.broadcast_to(jnp.where(empty, NEG, 0.0), bias_ref.shape)
        kt_ref[...] = kv_ref[:, k_cols].T

        def scores(buffer, q, part, top):
            bias = jnp.concatenate([bias_ref[part, :]] * (rows // HD), axis=1)
            s = contract_last(kv_ref[part, k_cols], q) + bias
            s_ref[buffer, part, :] = s
            return jnp.maximum(top, jnp.max(fold(s), axis=0))

        def one_head(h, top, here, there, last=False):
            at = c * HALF + h
            q = qg_ref[:, columns(at)]
            g = qg_ref[:, columns(QH + at)]
            top = jnp.max(top, axis=0, keepdims=True)
            total = jnp.zeros((8, rows), F32)
            cross = jnp.zeros((8, rows), F32)
            for part in parts:
                dp = contract_last(kv_ref[part, v_cols], g)
                e = jnp.exp2((s_ref[here, part, :] - top) * unit)
                s_ref[here, part, :] = e
                p_ref[part, :] = dp
                total = total + jnp.sum(fold(e), axis=0)
                cross = cross + jnp.sum(fold(e * dp), axis=0)
            share = 1.0 / jnp.sum(total, axis=0, keepdims=True)
            row_dot = jnp.sum(cross, axis=0, keepdims=True) * share
            dqt = jnp.zeros((HD, rows), F32)
            next_top = low
            if not last:
                next_q = qg_ref[:, columns(at + 1)]
            for part in parts:
                if not last:
                    next_top = scores(there, next_q, part, next_top)
                p = s_ref[here, part, :] * share
                ds = (p * (p_ref[part, :] - row_dot)).astype(BF)
                dv_ref[part, :] += dot(p.astype(BF), g)
                dk_ref[part, :] += dot(ds, q)
                dqt += dot(kt_ref[:, part], ds)
            dq_ref[:, columns(at)] = (dqt * scale).T.astype(BF)
            return next_top

        def two_heads(i, top):
            top = one_head(2 * i, top, 0, 1)
            return one_head(2 * i + 1, top, 1, 0)

        first_q = qg_ref[:, columns(c * HALF)]
        top = low
        for part in parts:
            top = scores(0, first_q, part, top)
        top = lax.fori_loop(0, HALF // 2 - 1, two_heads, top)
        top = one_head(HALF - 2, top, 0, 1)
        one_head(HALF - 1, top, 1, 0, last=True)
        dkv_ref[:, k_cols] = (dk_ref[...] * scale).astype(BF)
        dkv_ref[:, v_cols] = dv_ref[...].astype(BF)
        return 0

    lax.fori_loop(0, KVH, one_key_head, 0)


def unpack_q_kernel(head_ref, group_ref, dq_ref, out_ref):
    taker = taker_of(group_ref, dq_ref.shape[0])
    for slot in range(QH):
        place = place_of(head_ref[slot])
        out_ref[:, slot * HD : (slot + 1) * HD] = dot(taker, dq_ref[:, columns(place)]).astype(BF)


def unpack_kv_kernel(group_ref, dkv_ref, dk_ref, dv_ref):
    taker = taker_of(group_ref, dkv_ref.shape[0])
    for c in range(KVH):
        cols = slice(c * HD, (c + 1) * HD)
        dk_ref[:, cols] = dot(taker, dkv_ref[:, 2 * c * HD : (2 * c + 1) * HD]).astype(BF)
        dv_ref[:, cols] = dot(taker, dkv_ref[:, (2 * c + 1) * HD : (2 * c + 2) * HD]).astype(BF)


def struct(*shape):
    return jax.ShapeDtypeStruct(shape, BF)


def call(kernel, name, out_shape, scalars=0, inputs=1, scratch=(), cost=None):
    whole = pl.BlockSpec(memory_space=pltpu.VMEM)
    many = isinstance(out_shape, tuple)
    return pl.pallas_call(
        kernel,
        out_shape=out_shape,
        in_specs=[pl.BlockSpec(memory_space=pltpu.SMEM)] * scalars + [whole] * inputs,
        out_specs=(whole,) * len(out_shape) if many else whole,
        scratch_shapes=scratch,
        compiler_params=pltpu.CompilerParams(vmem_limit_bytes=VMEM),
        cost_estimate=cost,
        name=name,
    )


def per_device(queries, keys, values, grad_out, group_of_row, head_slot):
    rows = queries.shape[0]
    groups = lax.axis_size(PLANE)
    column = lax.axis_size(COLUMN)
    slots = groups * CAP
    width_q = QH * HD
    width_kv = 2 * KVH * HD
    all_keys = column * slots
    row_group = group_of_row.reshape(1, rows)

    def over_plane(array):
        return lax.all_to_all(array, PLANE, split_axis=0, concat_axis=0, tiled=True)

    sent_kv = call(pack_kv_kernel, "pack_kv", struct(slots, width_kv), inputs=3)(row_group, keys, values)
    home_kv = over_plane(sent_kv)
    all_kv = lax.all_gather(home_kv, COLUMN, axis=0, tiled=True)
    sent_qg = call(pack_qg_kernel, "pack_qg", struct(slots, 2 * width_q), scalars=1, inputs=3)(
        head_slot, row_group, queries, grad_out
    )
    home_qg = over_plane(sent_qg)

    pairs = QH * slots * all_keys
    grad_kv, grad_q = call(
        attend_kernel,
        "attend",
        (struct(all_keys, width_kv), struct(slots, width_q)),
        inputs=2,
        scratch=[
            pltpu.VMEM((2, all_keys, slots), F32),
            pltpu.VMEM((all_keys, slots), F32),
            pltpu.VMEM((all_keys, HD), F32),
            pltpu.VMEM((all_keys, HD), F32),
            pltpu.VMEM((all_keys, HD), F32),
            pltpu.VMEM((HD, all_keys), BF),
        ],
        cost=pl.CostEstimate(
            flops=10 * HD * pairs,
            bytes_accessed=2 * (3 * slots * width_q + 2 * all_keys * width_kv),
            transcendentals=pairs,
        ),
    )(home_qg, all_kv)

    kv_total = lax.psum_scatter(grad_kv, COLUMN, scatter_dimension=0, tiled=True)
    back_q = over_plane(grad_q)
    back_kv = over_plane(kv_total)
    out_q = call(unpack_q_kernel, "unpack_q", struct(rows, width_q), scalars=1, inputs=2)(
        head_slot, row_group, back_q
    )
    out_k, out_v = call(
        unpack_kv_kernel, "unpack_kv", (struct(rows, KVH * HD), struct(rows, KVH * HD)), inputs=2
    )(row_group, back_kv)
    return out_q, out_k, out_v


def solution(mesh):
    fine = Mesh(mesh.devices.reshape(4, 4, 2, 2, 4), AXES)
    split = P(AXES, None)
    return jax.shard_map(
        per_device,
        mesh=fine,
        in_specs=(split, split, split, split, split, P()),
        out_specs=(split, split, split),
        check_vma=False,
    )
```

time: 194 us -> 166 us (0.86); the launches traced: 192 us -> 166 us
  Pallas kernels: 64.6 us -> 42.2 us
  blocking collectives: 80.6 us -> 76.7 us
  waiting for transfers between devices: 15.9 us -> 19.3 us
    pallas_call x5, Pallas kernels: 64.6 us -> 42.2 us  [the longest x1 32 us: per_device(): call(attend_kernel, 'attend', (struct(all_keys, width_kv), struct(slots,...]
    all_to_all x1, waiting for transfers between devices: 0.01 us -> 6.2 us  [over_plane(): return lax.all_to_all(array, PLANE, split_axis=0, concat_axis=0, tiled=True)]
    reduce_scatter x1, waiting for transfers between devices: 15.8 us -> 11.6 us  [per_device(): lax.psum_scatter(grad_kv, COLUMN, scatter_dimension=0, tiled=True)]
    all_to_all x4 -> x3, blocking collectives: 80.6 us -> 76.7 us  [over_plane(): return lax.all_to_all(array, PLANE, split_axis=0, concat_axis=0, tiled=True)]
  transfers between devices with their start and end apart: 3 -> 3, of which waited for: 1 -> 3; matrix products, arithmetic and copies ran while one was open for 1% -> 0% of each run, Pallas kernels for 11% -> 4%
where the time goes in v2:
time: 166 us
  blocking collectives  76.7 us (46%)
  Pallas kernels  42.2 us (25%)
  waiting for transfers between devices  19.3 us (12%)
  between operations  14.1 us (8%)
  starting transfers between devices  11.8 us (7%)
  local copies, waits for them, and re-layouts  1.9 us (1%)
    all_to_all x3, blocking collectives, over_plane(): return lax.all_to_all(array, PLANE, split_axis=0, concat_axis=0, tiled=True)  76.7 us
    pallas_call x1, Pallas kernels, per_device(): call(attend_kernel, 'attend', (struct(all_keys, width_kv), struct(slots,...  32 us
    all_to_all x1, starting transfers between devices, over_plane(): return lax.all_to_all(array, PLANE, split_axis=0, concat_axis=0, tiled=True)  11.7 us
    reduce_scatter x1, waiting for transfers between devices, per_device(): lax.psum_scatter(grad_kv, COLUMN, scatter_dimension=0, tiled=True)  11.6 us
    all_to_all x1, waiting for transfers between devices, over_plane(): return lax.all_to_all(array, PLANE, split_axis=0, concat_axis=0, tiled=True)  6.2 us
    pallas_call x1, Pallas kernels, per_device(): call(pack_qg_kernel, 'pack_qg', struct(slots, 2 * width_q), scalars=1, in...  3.54 us
  transfers between devices with their start and end apart: 3, of which 3 were waited for; matrix products, arithmetic and copies ran while one was open for 0% of the time, Pallas kernels for 4%

profile of v2, /device:TPU:1, one launch (start us, length us, event | category | flops | bytes accessed | tf_op | source)
XLA Modules:
  0.0 165.9 jit_solution(17725654732855779972)
XLA Ops:
  7.2 0.0 all-gather.2.cloned.1.call-start
  7.2 1.9 %pack_kv.1 = bf16[256,512]{1,0:T(8,128)(2,1)} custom-call(s32[1,128]{1,0:T(1,128)} %bitcast.17, bf16[128,256]{1,0:T(8,128)(2,1)} %key_ref.1, bf16[128,256]{1,0:T(8,128)(2,1)} %value_ref.1), custom_call_target="tpu_custom_call" | custom-call | tf_op jit(solution)/shard_map/pack_kv/pallas_call | solution.py:221
  9.1 17.6 %all_to_all.45 = bf16[32,8,512]{2,1,0:T(8,128)(2,1)} all-to-all(bf16[32,8,512]{2,1,0:T(8,128)(2,1)} %bitcast.15), channel_id=1, replica_groups=mesh['zh'=4,'y'=4,'c'=2,'zl'=2,'x'=4] {'y','c','x'}, dimensions={0} | all-to-all | bytes 524288 | tf_op jit(solution)/shard_map/all_to_all | solution.py:219
  26.7 0.0 all-gather.2.cloned.1.call-update
  26.7 0.0 reduce-scatter.2.cloned.1.call-start
  26.8 3.5 %pack_qg.1 = bf16[256,4096]{1,0:T(8,128)(2,1)} custom-call(s32[16]{0:T(128)} %head_ref.3, s32[1,128]{1,0:T(1,128)} %bitcast.18, bf16[128,2048]{1,0:T(8,128)(2,1)} %query_ref.1, bf16[128,2048]{1,0:T(8,128)(2,1)} %grad_ref.1), custom_call_target="tpu_custom_call" | custom-call | tf_op jit(solution)/shard_map/pack_qg/pallas_call | solution.py:224
  30.3 31.8 %all_to_all.46 = bf16[32,8,4096]{2,1,0:T(8,128)(2,1)} all-to-all(bf16[32,8,4096]{2,1,0:T(8,128)(2,1)} %bitcast.9), channel_id=1, replica_groups=mesh['zh'=4,'y'=4,'c'=2,'zl'=2,'x'=4] {'y','c','x'}, dimensions={0} | all-to-all | bytes 4194304 | tf_op jit(solution)/shard_map/all_to_all | solution.py:219
  62.2 1.5 all-gather.2.cloned.1.call-done.kv_ref
  63.6 32.0 %attend.1 = (bf16[2048,512]{1,0:T(8,128)(2,1)}, bf16[256,2048]{1,0:T(8,128)(2,1)}) custom-call(bf16[256,4096]{1,0:T(8,128)(2,1)} %bitcast.11, bf16[2048,512]{1,0:T(8,128)(2,1)} %all-gather.2.cloned.1.call-done.kv_ref), custom_call_target="tpu_custom_call" | custom-call | flops 10737418240 | bytes 7340032 | tf_op jit(solution)/shard_map/attend/pallas_call | solution.py:230
  95.6 0.0 copy-start
  95.6 0.0 reduce-scatter.2.cloned.1.call-update
  95.7 1.2 copy-done
  96.9 27.3 %all_to_all.47 = bf16[32,8,2048]{2,1,0:T(8,128)(2,1)} all-to-all(bf16[32,8,2048]{2,1,0:T(8,128)(2,1)S(1)} %bitcast.12), channel_id=1, replica_groups=mesh['zh'=4,'y'=4,'c'=2,'zl'=2,'x'=4] {'y','c','x'}, dimensions={0} | all-to-all | bytes 2097152 | tf_op jit(solution)/shard_map/all_to_all | solution.py:219
  124.1 11.6 %reduce-scatter.2.cloned.1.call-done = bf16[256,512]{1,0:T(8,128)(2,1)} async-done(((bf16[2048,512]{1,0:T(8,128)(2,1)}), bf16[256,512]{1,0:T(8,128)(2,1)}) %reduce-scatter.2.cloned.1.call-update) | async-done | bytes 262160 | tf_op jit(solution)/shard_map/reduce_scatter | solution.py:250
  135.7 11.7 %all-to-all-start.3 = ((bf16[32,8,512]{2,1,0:T(8,128)(2,1)}), bf16[32,8,512]{2,1,0:T(8,128)(2,1)S(1)}, u32[]{:S(2)}, u32[]{:S(2)}) async-start(bf16[32,8,512]{2,1,0:T(8,128)(2,1)} %bitcast.16), calls=%async_computation.4 | async-start | bytes 524288 | tf_op jit(solution)/shard_map/all_to_all | solution.py:219
  147.5 2.7 %unpack_q.1 = bf16[128,2048]{1,0:T(8,128)(2,1)} custom-call(s32[16]{0:T(128)} %head_ref.3, s32[1,128]{1,0:T(1,128)} %bitcast.19, bf16[256,2048]{1,0:T(8,128)(2,1)} %bitcast.10), custom_call_target="tpu_custom_call" | custom-call | tf_op jit(solution)/shard_map/unpack_q/pallas_call | solution.py:253
  150.1 6.2 %all-to-all-done.3 = bf16[32,8,512]{2,1,0:T(8,128)(2,1)S(1)} async-done(((bf16[32,8,512]{2,1,0:T(8,128)(2,1)}), bf16[32,8,512]{2,1,0:T(8,128)(2,1)S(1)}, u32[]{:S(2)}, u32[]{:S(2)}) %all-to-all-start.3) | async-done | bytes 262176 | tf_op jit(solution)/shard_map/all_to_all | solution.py:219
  156.3 0.0 copy-start.1
  156.4 0.7 copy-done.1
  157.0 2.0 %unpack_kv.1 = (bf16[128,256]{1,0:T(8,128)(2,1)}, bf16[128,256]{1,0:T(8,128)(2,1)}) custom-call(s32[1,128]{1,0:T(1,128)} %bitcast.20, bf16[256,512]{1,0:T(8,128)(2,1)} %bitcast.14), custom_call_target="tpu_custom_call" | custom-call | tf_op jit(solution)/shard_map/unpack_kv/pallas_call | solution.py:256
Async XLA Ops:
  7.2 56.5 %all-gather.2.cloned.1.call-start = ((), (), s32[]{:S(2)}) async-start(), calls=%async_computation.5 | async-start | bytes 2359296 | tf_op jit(solution)/shard_map/all_gather | solution.py:223
  26.7 109.0 %reduce-scatter.2.cloned.1.call-start = ((), (), s32[]{:S(2)}) async-start(), calls=%async_computation.6 | async-start | bytes 2359296 | tf_op jit(solution)/shard_map/reduce_scatter | solution.py:250
  95.6 1.2 copy-start
  135.7 20.6 %all-to-all-start.3 = ((bf16[32,8,512]{2,1,0:T(8,128)(2,1)}), bf16[32,8,512]{2,1,0:T(8,128)(2,1)S(1)}, u32[]{:S(2)}, u32[]{:S(2)}) async-start(bf16[32,8,512]{2,1,0:T(8,128)(2,1)} %bitcast.16), calls=%async_computation.4 | async-start | bytes 524288 | tf_op jit(solution)/shard_map/all_to_all | solution.py:219
  156.3 0.7 copy-start.1
Sparse Core Ops, SparseCore 0:
  26.9 36.7 all-gather.1
  95.8 39.9 reduce-scatter.1

commit v3 on v2

--- a/solution.py
+++ b/solution.py
@@ -97,9 +97,12 @@
         out_ref[:, columns(QH + place)] = (dot(placer, grad_ref[:, cols]) * real).astype(BF)
 
 
-def attend_kernel(qg_ref, kv_ref, dkv_ref, dq_ref, s_ref, p_ref, dk_ref, dv_ref, bias_ref, kt_ref):
-    keys = kv_ref.shape[0]
+def attend_kernel(*refs):
+    qg_ref, kv_refs, dkv_refs, dq_ref = refs[0], refs[1:10], refs[10:19], refs[19]
+    k_ref, v_ref, s_ref, p_ref, dk_ref, dv_ref, bias_ref, kt_ref = refs[20:]
+    keys = k_ref.shape[0]
     rows = qg_ref.shape[0]
+    block = keys // 8
     scale = HD ** (-0.5)
     unit = scale * math.log2(math.e)
     parts = [slice(t, t + KEY_TILE) for t in range(0, keys, KEY_TILE)]
@@ -108,17 +111,21 @@
     def fold(tile):
         return tile.reshape(tile.shape[0] // 8, 8, rows)
 
-    def one_key_head(c, _):
-        k_cols, v_cols = columns(2 * c), columns(2 * c + 1)
+    def one_key_head(c):
+        for i in range(8):
+            here = slice(i * block, (i + 1) * block)
+            ref, first = (kv_refs[i], 2 * c * HD) if i < 7 else (kv_refs[7 + c], 0)
+            k_ref[here, :] = ref[:, first : first + HD]
+            v_ref[here, :] = ref[:, first + HD : first + 2 * HD]
         dk_ref[...] = jnp.zeros_like(dk_ref)
         dv_ref[...] = jnp.zeros_like(dv_ref)
-        empty = kv_ref[:, v_cols][:, :1].astype(F32) > 0.5 * EMPTY
+        empty = v_ref[:, :1].astype(F32) > 0.5 * EMPTY
         bias_ref[...] = jnp.broadcast_to(jnp.where(empty, NEG, 0.0), bias_ref.shape)
-        kt_ref[...] = kv_ref[:, k_cols].T
+        kt_ref[...] = k_ref[...].T
 
         def scores(buffer, q, part, top):
             bias = jnp.concatenate([bias_ref[part, :]] * (rows // HD), axis=1)
-            s = contract_last(kv_ref[part, k_cols], q) + bias
+            s = contract_last(k_ref[part, :], q) + bias
             s_ref[buffer, part, :] = s
             return jnp.maximum(top, jnp.max(fold(s), axis=0))
 
@@ -130,7 +137,7 @@
             total = jnp.zeros((8, rows), F32)
             cross = jnp.zeros((8, rows), F32)
             for part in parts:
-                dp = contract_last(kv_ref[part, v_cols], g)
+                dp = contract_last(v_ref[part, :], g)
                 e = jnp.exp2((s_ref[here, part, :] - top) * unit)
                 s_ref[here, part, :] = e
                 p_ref[part, :] = dp
@@ -164,11 +171,14 @@
         top = lax.fori_loop(0, HALF // 2 - 1, two_heads, top)
         top = one_head(HALF - 2, top, 0, 1)
         one_head(HALF - 1, top, 1, 0, last=True)
-        dkv_ref[:, k_cols] = (dk_ref[...] * scale).astype(BF)
-        dkv_ref[:, v_cols] = dv_ref[...].astype(BF)
-        return 0
-
-    lax.fori_loop(0, KVH, one_key_head, 0)
+        for i in range(8):
+            here = slice(i * block, (i + 1) * block)
+            ref, first = (dkv_refs[i], 2 * c * HD) if i < 7 else (dkv_refs[7 + c], 0)
+            ref[:, first : first + HD] = (dk_ref[here, :] * scale).astype(BF)
+            ref[:, first + HD : first + 2 * HD] = dv_ref[here, :].astype(BF)
+
+    for c in range(KVH):
+        one_key_head(c)
 
 
 def unpack_q_kernel(head_ref, group_ref, dq_ref, out_ref):
@@ -184,6 +194,39 @@
         cols = slice(c * HD, (c + 1) * HD)
         dk_ref[:, cols] = dot(taker, dkv_ref[:, 2 * c * HD : (2 * c + 1) * HD]).astype(BF)
         dv_ref[:, cols] = dot(taker, dkv_ref[:, (2 * c + 1) * HD : (2 * c + 2) * HD]).astype(BF)
+
+
+def ring_steps(axis):
+    size = lax.axis_size(axis)
+    up = [(i, (i + 1) % size) for i in range(size)]
+    down = [(i, (i - 1) % size) for i in range(size)]
+    return lambda x: lax.ppermute(x, axis, up), lambda x: lax.ppermute(x, axis, down)
+
+
+def gather_column(block):
+    up, down = ring_steps(COLUMN)
+    half = block.shape[1] // 2
+    below = above = block
+    blocks = [block]
+    for _ in range(3):
+        below, above = up(below), down(above)
+        blocks += [below, above]
+    return blocks + [up(below[:, :half]), down(above[:, half:])]
+
+
+def scatter_column(blocks):
+    up, down = ring_steps(COLUMN)
+
+    def plus(*terms):
+        return sum(term.astype(F32) for term in terms).astype(BF)
+
+    own, to_below, to_above = blocks[0], blocks[1:7:2], blocks[2:7:2]
+    zeros = jnp.zeros_like(blocks[7])
+    rising = plus(to_above[2], jnp.concatenate([up(blocks[7]), zeros], axis=1))
+    falling = plus(to_below[2], jnp.concatenate([zeros, down(blocks[8])], axis=1))
+    for i in (1, 0):
+        rising, falling = plus(to_above[i], up(rising)), plus(to_below[i], down(falling))
+    return plus(own, up(rising), down(falling))
 
 
 def struct(*shape):
@@ -220,19 +263,22 @@
 
     sent_kv = call(pack_kv_kernel, "pack_kv", struct(slots, width_kv), inputs=3)(row_group, keys, values)
     home_kv = over_plane(sent_kv)
-    all_kv = lax.all_gather(home_kv, COLUMN, axis=0, tiled=True)
+    all_kv = gather_column(home_kv)
     sent_qg = call(pack_qg_kernel, "pack_qg", struct(slots, 2 * width_q), scalars=1, inputs=3)(
         head_slot, row_group, queries, grad_out
     )
     home_qg = over_plane(sent_qg)
 
     pairs = QH * slots * all_keys
-    grad_kv, grad_q = call(
+    blocks = [struct(*block.shape) for block in all_kv]
+    *grad_kv, grad_q = call(
         attend_kernel,
         "attend",
-        (struct(all_keys, width_kv), struct(slots, width_q)),
-        inputs=2,
+        (*blocks, struct(slots, width_q)),
+        inputs=1 + len(all_kv),
         scratch=[
+            pltpu.VMEM((all_keys, HD), BF),
+            pltpu.VMEM((all_keys, HD), BF),
             pltpu.VMEM((2, all_keys, slots), F32),
             pltpu.VMEM((all_keys, slots), F32),
             pltpu.VMEM((all_keys, HD), F32),
@@ -245,9 +291,9 @@
             bytes_accessed=2 * (3 * slots * width_q + 2 * all_keys * width_kv),
             transcendentals=pairs,
         ),
-    )(home_qg, all_kv)
-
-    kv_total = lax.psum_scatter(grad_kv, COLUMN, scatter_dimension=0, tiled=True)
+    )(home_qg, *all_kv)
+
+    kv_total = scatter_column(grad_kv)
     back_q = over_plane(grad_q)
     back_kv = over_plane(kv_total)
     out_q = call(unpack_q_kernel, "unpack_q", struct(rows, width_q), scalars=1, inputs=2)(

time: 166 us -> 156 us (0.940)
  blocking collectives: 76.7 us -> 0 us
  starting transfers between devices: 11.8 us -> 57.8 us
  waiting for transfers between devices: 19.3 us -> 49.5 us
  between operations: 14.1 us -> 0.82 us
  other arithmetic: 0 us -> 4.08 us
    all_to_all x3 -> x0, blocking collectives: 76.7 us -> none  [over_plane(): return lax.all_to_all(array, PLANE, split_axis=0, concat_axis=0, tiled=True)]
    ppermute x0 -> x16, waiting for transfers between devices: none -> 33.8 us  [the longest x8 27.2 us: ring_steps(): lax.ppermute(x, axis, down)]
    ppermute x0 -> x16, starting transfers between devices: none -> 23.3 us  [the longest x8 20.7 us: ring_steps(): lax.ppermute(x, axis, down)]
    all_to_all x1 -> x4, starting transfers between devices: 11.7 us -> 34.5 us  [over_plane(): return lax.all_to_all(array, PLANE, split_axis=0, concat_axis=0, tiled=True)]
    reduce_scatter x1 -> x0, waiting for transfers between devices: 11.6 us -> none  [per_device(): lax.psum_scatter(grad_kv, COLUMN, scatter_dimension=0, tiled=True)]
    all_to_all x1 -> x4, waiting for transfers between devices: 6.2 us -> 15.7 us  [over_plane(): return lax.all_to_all(array, PLANE, split_axis=0, concat_axis=0, tiled=True)]
    convert_element_type x0 -> x6, other arithmetic: none -> 3.29 us  [plus(): return sum((term.astype(F32) for term in terms)).astype(BF)]
  transfers between devices with their start and end apart: 3 -> 20, of which waited for: 3 -> 12; matrix products, arithmetic and copies ran while one was open for 0% -> 3% of each run, Pallas kernels for 4% -> 4%
where the time goes in v3:
time: 156 us; the launch traced here: 155 us
  starting transfers between devices  57.8 us (37%)
  waiting for transfers between devices  49.5 us (32%)
  Pallas kernels  40.9 us (26%)
  other arithmetic  4.08 us (3%)
  local copies, waits for them, and re-layouts  2.08 us (1%)
    all_to_all x4, starting transfers between devices, over_plane(): return lax.all_to_all(array, PLANE, split_axis=0, concat_axis=0, tiled=True)  34.5 us
    pallas_call x1, Pallas kernels, per_device(): call(attend_kernel, 'attend', (*blocks, struct(slots, width_q)), inputs=1...  30.7 us
    ppermute x8, waiting for transfers between devices, ring_steps(): lax.ppermute(x, axis, down)  27.2 us
    ppermute x8, starting transfers between devices, ring_steps(): lax.ppermute(x, axis, down)  20.7 us
    all_to_all x4, waiting for transfers between devices, over_plane(): return lax.all_to_all(array, PLANE, split_axis=0, concat_axis=0, tiled=True)  15.7 us
    ppermute x8, waiting for transfers between devices, ring_steps(): lax.ppermute(x, axis, up)  6.64 us
    pallas_call x1, Pallas kernels, per_device(): call(pack_qg_kernel, 'pack_qg', struct(slots, 2 * width_q), scalars=1, in...  3.58 us
    convert_element_type x6, other arithmetic, plus(): return sum((term.astype(F32) for term in terms)).astype(BF)  3.29 us
  transfers between devices with their start and end apart: 20, of which 12 were waited for; matrix products, arithmetic and copies ran while one was open for 3% of the time, Pallas kernels for 4%

profile of v3, /device:TPU:1, one launch (start us, length us, event | category | flops | bytes accessed | tf_op | source)
XLA Modules:
  0.0 155.2 jit_solution(10185530175490325211)
XLA Ops:
  0.6 1.9 %pack_kv.1 = bf16[256,512]{1,0:T(8,128)(2,1)} custom-call(s32[1,128]{1,0:T(1,128)} %bitcast.18, bf16[128,256]{1,0:T(8,128)(2,1)} %key_ref.1, bf16[128,256]{1,0:T(8,128)(2,1)} %value_ref.1), custom_call_target="tpu_custom_call" | custom-call | tf_op jit(solution)/shard_map/pack_kv/pallas_call | solution.py:264
  2.5 8.6 %all-to-all-start.1 = ((bf16[32,8,512]{2,1,0:T(8,128)(2,1)}), bf16[32,8,512]{2,1,0:T(8,128)(2,1)S(1)}, u32[]{:S(2)}, u32[]{:S(2)}) async-start(bf16[32,8,512]{2,1,0:T(8,128)(2,1)} %bitcast.14), calls=%async_computation.1 | async-start | bytes 524288 | tf_op jit(solution)/shard_map/all_to_all | solution.py:262
  11.1 3.6 %pack_qg.1 = bf16[256,4096]{1,0:T(8,128)(2,1)} custom-call(s32[16]{0:T(128)} %head_ref.3, s32[1,128]{1,0:T(1,128)} %bitcast.19, bf16[128,2048]{1,0:T(8,128)(2,1)} %query_ref.1, bf16[128,2048]{1,0:T(8,128)(2,1)} %grad_ref.1), custom_call_target="tpu_custom_call" | custom-call | tf_op jit(solution)/shard_map/pack_qg/pallas_call | solution.py:267
  14.7 5.3 %all-to-all-done.1 = bf16[32,8,512]{2,1,0:T(8,128)(2,1)S(1)} async-done(((bf16[32,8,512]{2,1,0:T(8,128)(2,1)}), bf16[32,8,512]{2,1,0:T(8,128)(2,1)S(1)}, u32[]{:S(2)}, u32[]{:S(2)}) %all-to-all-start.1) | async-done | bytes 262176 | tf_op jit(solution)/shard_map/all_to_all | solution.py:262
  20.0 4.1 %all-to-all-start = ((bf16[32,8,4096]{2,1,0:T(8,128)(2,1)}), bf16[32,8,4096]{2,1,0:T(8,128)(2,1)S(1)}, u32[]{:S(2)}, u32[]{:S(2)}) async-start(bf16[32,8,4096]{2,1,0:T(8,128)(2,1)} %bitcast.10), calls=%async_computation | async-start | bytes 4194304 | tf_op jit(solution)/shard_map/all_to_all | solution.py:262
  24.2 5.7 %collective-permute-start.1 = (bf16[256,512]{1,0:T(8,128)(2,1)S(1)}, bf16[256,512]{1,0:T(8,128)(2,1)S(1)}, u32[]{:S(2)}, u32[]{:S(2)}) collective-permute-start(bf16[256,512]{1,0:T(8,128)(2,1)S(1)} %bitcast.15), channel_id=1, source_target_pairs={{0,196},{4,0},{64,4},{68,64},{128,68},{132,128},{192,132},{196,192... | collective-permute-start | bytes 786440 | tf_op jit(solution)/shard_map/ppermute | solution.py:203
  29.8 5.5 %collective-permute-done.1.refs_3_ = bf16[256,512]{1,0:T(8,128)(2,1)S(1)} collective-permute-done((bf16[256,512]{1,0:T(8,128)(2,1)S(1)}, bf16[256,512]{1,0:T(8,128)(2,1)S(1)}, u32[]{:S(2)}, u32[]{:S(2)}) %collective-permute-start.1) | collective-permute-done | bytes 262176 | tf_op jit(solution)/shard_map/ppermute | solution.py:203
  35.3 3.4 %collective-permute-start.3 = (bf16[256,512]{1,0:T(8,128)(2,1)S(1)}, bf16[256,512]{1,0:T(8,128)(2,1)S(1)}, u32[]{:S(2)}, u32[]{:S(2)}) collective-permute-start(bf16[256,512]{1,0:T(8,128)(2,1)S(1)} %collective-permute-done.1.refs_3_), channel_id=1, source_target_pairs={{0,196},{4,0},{64,4},{68,64},{128,68},{132,128},{192,132},{196,192... | collective-permute-start | bytes 786440 | tf_op jit(solution)/shard_map/ppermute | solution.py:203
  38.7 4.5 %collective-permute-done.3.refs_5_ = bf16[256,512]{1,0:T(8,128)(2,1)S(1)} collective-permute-done((bf16[256,512]{1,0:T(8,128)(2,1)S(1)}, bf16[256,512]{1,0:T(8,128)(2,1)S(1)}, u32[]{:S(2)}, u32[]{:S(2)}) %collective-permute-start.3) | collective-permute-done | bytes 262176 | tf_op jit(solution)/shard_map/ppermute | solution.py:203
  43.3 3.4 %collective-permute-start.5 = (bf16[256,512]{1,0:T(8,128)(2,1)S(1)}, bf16[256,512]{1,0:T(8,128)(2,1)S(1)}, u32[]{:S(2)}, u32[]{:S(2)}) collective-permute-start(bf16[256,512]{1,0:T(8,128)(2,1)S(1)} %collective-permute-done.3.refs_5_), channel_id=1, source_target_pairs={{0,196},{4,0},{64,4},{68,64},{128,68},{132,128},{192,132},{196,192... | collective-permute-start | bytes 786440 | tf_op jit(solution)/shard_map/ppermute | solution.py:203
  46.7 3.6 %collective-permute-done.5.refs_7_ = bf16[256,512]{1,0:T(8,128)(2,1)S(1)} collective-permute-done((bf16[256,512]{1,0:T(8,128)(2,1)S(1)}, bf16[256,512]{1,0:T(8,128)(2,1)S(1)}, u32[]{:S(2)}, u32[]{:S(2)}) %collective-permute-start.5) | collective-permute-done | bytes 262176 | tf_op jit(solution)/shard_map/ppermute | solution.py:203
  50.3 3.5 %collective-permute-start.7 = (bf16[256,256]{1,0:T(8,128)(2,1)S(1)}, bf16[256,256]{1,0:T(8,128)(2,1)S(1)}, u32[]{:S(2)}, u32[]{:S(2)}) collective-permute-start(bf16[256,256]{1,0:T(8,128)(2,1)S(1)} %slice.9), channel_id=1, source_target_pairs={{0,196},{4,0},{64,4},{68,64},{128,68},{132,128},{192,132},{196,192... | collective-permute-start | bytes 393224 | tf_op jit(solution)/shard_map/ppermute | solution.py:203
  54.1 1.7 %collective-permute-done.7.refs_9_ = bf16[256,256]{1,0:T(8,128)(2,1)S(1)} collective-permute-done((bf16[256,256]{1,0:T(8,128)(2,1)S(1)}, bf16[256,256]{1,0:T(8,128)(2,1)S(1)}, u32[]{:S(2)}, u32[]{:S(2)}) %collective-permute-start.7) | collective-permute-done | bytes 131104 | tf_op jit(solution)/shard_map/ppermute | solution.py:203
  55.8 3.5 %collective-permute-done.6.refs_8_ = bf16[256,256]{1,0:T(8,128)(2,1)} collective-permute-done((bf16[256,256]{1,0:T(8,128)(2,1)S(1)}, bf16[256,256]{1,0:T(8,128)(2,1)}, u32[]{:S(2)}, u32[]{:S(2)}) %collective-permute-start.6) | collective-permute-done | bytes 131104 | tf_op jit(solution)/shard_map/ppermute | solution.py:203
  59.3 1.3 copy-done.1
  60.6 30.7 %attend.1 = (bf16[256,512]{1,0:T(8,128)(2,1)}, bf16[256,512]{1,0:T(8,128)(2,1)}, bf16[256,512]{1,0:T(8,128)(2,1)}, bf16[256,512]{1,0:T(8,128)(2,1)}, bf16[256,51...) custom-call(bf16[256,4096]{1,0:T(8,128)(2,1)} %bitcast.12, ...), custom_call_target="tpu_custom_call" | custom-call | flops 10737418240 | bytes 7340032 | tf_op jit(solution)/shard_map/attend/pallas_call | solution.py:274
  91.4 1.5 collective-permute-start.8
  92.8 2.6 %collective-permute-done.12 = bf16[256,256]{1,0:T(8,128)(2,1)S(1)} collective-permute-done((bf16[256,256]{1,0:T(8,128)(2,1)}, bf16[256,256]{1,0:T(8,128)(2,1)S(1)}, u32[]{:S(2)}, u32[]{:S(2)}) %collective-permute-start.12) | collective-permute-done | bytes 131104 | tf_op jit(solution)/shard_map/ppermute | solution.py:203
  96.4 1.3 collective-permute-start.13
  97.7 1.0 add_convert_fusion.6
  99.1 3.9 %collective-permute-done.13 = bf16[256,512]{1,0:T(8,128)(2,1)S(1)} collective-permute-done((bf16[256,512]{1,0:T(8,128)(2,1)S(1)}, bf16[256,512]{1,0:T(8,128)(2,1)S(1)}, u32[]{:S(2)}, u32[]{:S(2)}) %collective-permute-start.13) | collective-permute-done | bytes 262176 | tf_op jit(solution)/shard_map/ppermute | solution.py:203
  103.0 1.1 add_convert_fusion.2
  104.1 1.2 collective-permute-start.14
  105.8 16.5 %all-to-all-start.2 = ((bf16[32,8,2048]{2,1,0:T(8,128)(2,1)}), bf16[32,8,2048]{2,1,0:T(8,128)(2,1)S(1)}, u32[]{:S(2)}, u32[]{:S(2)}) async-start(bf16[32,8,2048]{2,1,0:T(8,128)(2,1)} %bitcast.5), calls=%async_computation.2 | async-start | bytes 2097152 | tf_op jit(solution)/shard_map/all_to_all | solution.py:262
  122.4 2.2 %collective-permute-start.15 = (bf16[256,512]{1,0:T(8,128)(2,1)S(1)}, bf16[256,512]{1,0:T(8,128)(2,1)S(1)}, u32[]{:S(2)}, u32[]{:S(2)}) collective-permute-start(bf16[256,512]{1,0:T(8,128)(2,1)S(1)} %add_convert_fusion.1), channel_id=1, source_target_pairs={{0,196},{4,0},{64,4},{68,64},{128,68},{132,128},{192,132},{196,192... | collective-permute-start | bytes 786440 | tf_op jit(solution)/shard_map/ppermute | solution.py:203
  124.8 5.4 %collective-permute-done.15 = bf16[256,512]{1,0:T(8,128)(2,1)S(1)} collective-permute-done((bf16[256,512]{1,0:T(8,128)(2,1)S(1)}, bf16[256,512]{1,0:T(8,128)(2,1)S(1)}, u32[]{:S(2)}, u32[]{:S(2)}) %collective-permute-start.15) | collective-permute-done | bytes 262176 | tf_op jit(solution)/shard_map/ppermute | solution.py:203
  130.2 3.2 %collective-permute-done.11 = bf16[256,512]{1,0:T(8,128)(2,1)S(1)} collective-permute-done((bf16[256,512]{1,0:T(8,128)(2,1)S(1)}, bf16[256,512]{1,0:T(8,128)(2,1)S(1)}, u32[]{:S(2)}, u32[]{:S(2)}) %collective-permute-start.11) | collective-permute-done | bytes 262176 | tf_op jit(solution)/shard_map/ppermute | solution.py:203
  134.1 4.2 %all-to-all-done.2 = bf16[32,8,2048]{2,1,0:T(8,128)(2,1)S(1)} async-done(((bf16[32,8,2048]{2,1,0:T(8,128)(2,1)}), bf16[32,8,2048]{2,1,0:T(8,128)(2,1)S(1)}, u32[]{:S(2)}, u32[]{:S(2)}) %all-to-all-start.2) | async-done | bytes 1048608 | tf_op jit(solution)/shard_map/all_to_all | solution.py:262
  138.3 5.3 %all-to-all-start.3 = ((bf16[32,8,512]{2,1,0:T(8,128)(2,1)}), bf16[32,8,512]{2,1,0:T(8,128)(2,1)S(1)}, u32[]{:S(2)}, u32[]{:S(2)}) async-start(bf16[32,8,512]{2,1,0:T(8,128)(2,1)} %fusion), calls=%async_computation.3 | async-start | bytes 524288 | tf_op jit(solution)/shard_map/all_to_all | solution.py:262
  143.6 2.7 %unpack_q.1 = bf16[128,2048]{1,0:T(8,128)(2,1)} custom-call(s32[16]{0:T(128)} %head_ref.3, s32[1,128]{1,0:T(1,128)} %bitcast.20, bf16[256,2048]{1,0:T(8,128)(2,1)} %bitcast.11), custom_call_target="tpu_custom_call" | custom-call | tf_op jit(solution)/shard_map/unpack_q/pallas_call | solution.py:299
  146.3 6.2 %all-to-all-done.3 = bf16[32,8,512]{2,1,0:T(8,128)(2,1)S(1)} async-done(((bf16[32,8,512]{2,1,0:T(8,128)(2,1)}), bf16[32,8,512]{2,1,0:T(8,128)(2,1)S(1)}, u32[]{:S(2)}, u32[]{:S(2)}) %all-to-all-start.3) | async-done | bytes 262176 | tf_op jit(solution)/shard_map/all_to_all | solution.py:262
  153.2 2.0 %unpack_kv.1 = (bf16[128,256]{1,0:T(8,128)(2,1)}, bf16[128,256]{1,0:T(8,128)(2,1)}) custom-call(s32[1,128]{1,0:T(1,128)} %bitcast.21, bf16[256,512]{1,0:T(8,128)(2,1)} %bitcast.13), custom_call_target="tpu_custom_call" | custom-call | tf_op jit(solution)/shard_map/unpack_kv/pallas_call | solution.py:302
  (52 shorter events, 4.0 us)
Async XLA Ops:
  2.5 17.5 %all-to-all-start.1 = ((bf16[32,8,512]{2,1,0:T(8,128)(2,1)}), bf16[32,8,512]{2,1,0:T(8,128)(2,1)S(1)}, u32[]{:S(2)}, u32[]{:S(2)}) async-start(bf16[32,8,512]{2,1,0:T(8,128)(2,1)} %bitcast.14), calls=%async_computation.1 | async-start | bytes 524288 | tf_op jit(solution)/shard_map/all_to_all | solution.py:262
  20.0 9.8 %copy-start.6 = (bf16[32,8,512]{2,1,0:T(8,128)(2,1)}, bf16[32,8,512]{2,1,0:T(8,128)(2,1)S(1)}, u32[]{:S(2)}) copy-start(bf16[32,8,512]{2,1,0:T(8,128)(2,1)S(1)} %all-to-all-done.1) | copy-start | bytes 786436
  20.0 39.2 %all-to-all-start = ((bf16[32,8,4096]{2,1,0:T(8,128)(2,1)}), bf16[32,8,4096]{2,1,0:T(8,128)(2,1)S(1)}, u32[]{:S(2)}, u32[]{:S(2)}) async-start(bf16[32,8,4096]{2,1,0:T(8,128)(2,1)} %bitcast.10), calls=%async_computation | async-start | bytes 4194304 | tf_op jit(solution)/shard_map/all_to_all | solution.py:262
  24.2 11.1 %collective-permute-start.1 = (bf16[256,512]{1,0:T(8,128)(2,1)S(1)}, bf16[256,512]{1,0:T(8,128)(2,1)S(1)}, u32[]{:S(2)}, u32[]{:S(2)}) collective-permute-start(bf16[256,512]{1,0:T(8,128)(2,1)S(1)} %bitcast.15), channel_id=1, source_target_pairs={{0,196},{4,0},{64,4},{68,64},{128,68},{132,128},{192,132},{196,192... | collective-permute-start | bytes 786440 | tf_op jit(solution)/shard_map/ppermute | solution.py:203
  29.8 8.9 %collective-permute-start = (bf16[256,512]{1,0:T(8,128)(2,1)S(1)}, bf16[256,512]{1,0:T(8,128)(2,1)S(1)}, u32[]{:S(2)}, u32[]{:S(2)}) collective-permute-start(bf16[256,512]{1,0:T(8,128)(2,1)S(1)} %bitcast.16), channel_id=1, source_target_pairs={{0,4},{4,64},{64,68},{68,128},{128,132},{132,192},{192,196},{196,0... | collective-permute-start | bytes 786440 | tf_op jit(solution)/shard_map/ppermute | solution.py:203
  35.3 23.9 %copy-start.10 = (bf16[256,512]{1,0:T(8,128)(2,1)}, bf16[256,512]{1,0:T(8,128)(2,1)S(1)}, u32[]{:S(2)}) copy-start(bf16[256,512]{1,0:T(8,128)(2,1)S(1)} %collective-permute-done.1.refs_3_) | copy-start | bytes 786436
  35.3 8.0 %collective-permute-start.3 = (bf16[256,512]{1,0:T(8,128)(2,1)S(1)}, bf16[256,512]{1,0:T(8,128)(2,1)S(1)}, u32[]{:S(2)}, u32[]{:S(2)}) collective-permute-start(bf16[256,512]{1,0:T(8,128)(2,1)S(1)} %collective-permute-done.1.refs_3_), channel_id=1, source_target_pairs={{0,196},{4,0},{64,4},{68,64},{128,68},{132,128},{192,132},{196,192... | collective-permute-start | bytes 786440 | tf_op jit(solution)/shard_map/ppermute | solution.py:203
  38.7 20.5 %copy-start.11 = (bf16[256,512]{1,0:T(8,128)(2,1)}, bf16[256,512]{1,0:T(8,128)(2,1)S(1)}, u32[]{:S(2)}) copy-start(bf16[256,512]{1,0:T(8,128)(2,1)S(1)} %collective-permute-done.refs_2_) | copy-start | bytes 786436
  38.7 8.0 %collective-permute-start.2 = (bf16[256,512]{1,0:T(8,128)(2,1)S(1)}, bf16[256,512]{1,0:T(8,128)(2,1)S(1)}, u32[]{:S(2)}, u32[]{:S(2)}) collective-permute-start(bf16[256,512]{1,0:T(8,128)(2,1)S(1)} %collective-permute-done.refs_2_), channel_id=1, source_target_pairs={{0,4},{4,64},{64,68},{68,128},{128,132},{132,192},{192,196},{196,0... | collective-permute-start | bytes 786440 | tf_op jit(solution)/shard_map/ppermute | solution.py:203
  43.3 16.0 %copy-start.12 = (bf16[256,512]{1,0:T(8,128)(2,1)}, bf16[256,512]{1,0:T(8,128)(2,1)S(1)}, u32[]{:S(2)}) copy-start(bf16[256,512]{1,0:T(8,128)(2,1)S(1)} %collective-permute-done.3.refs_5_) | copy-start | bytes 786436
  43.3 7.0 %collective-permute-start.5 = (bf16[256,512]{1,0:T(8,128)(2,1)S(1)}, bf16[256,512]{1,0:T(8,128)(2,1)S(1)}, u32[]{:S(2)}, u32[]{:S(2)}) collective-permute-start(bf16[256,512]{1,0:T(8,128)(2,1)S(1)} %collective-permute-done.3.refs_5_), channel_id=1, source_target_pairs={{0,196},{4,0},{64,4},{68,64},{128,68},{132,128},{192,132},{196,192... | collective-permute-start | bytes 786440 | tf_op jit(solution)/shard_map/ppermute | solution.py:203
  46.7 7.1 %copy-start.13 = (bf16[256,512]{1,0:T(8,128)(2,1)}, bf16[256,512]{1,0:T(8,128)(2,1)S(1)}, u32[]{:S(2)}) copy-start(bf16[256,512]{1,0:T(8,128)(2,1)S(1)} %collective-permute-done.2.refs_4_) | copy-start | bytes 786436
  46.7 7.1 %collective-permute-start.4 = (bf16[256,512]{1,0:T(8,128)(2,1)S(1)}, bf16[256,512]{1,0:T(8,128)(2,1)S(1)}, u32[]{:S(2)}, u32[]{:S(2)}) collective-permute-start(bf16[256,512]{1,0:T(8,128)(2,1)S(1)} %collective-permute-done.2.refs_4_), channel_id=1, source_target_pairs={{0,4},{4,64},{64,68},{68,128},{128,132},{132,192},{192,196},{196,0... | collective-permute-start | bytes 786440 | tf_op jit(solution)/shard_map/ppermute | solution.py:203
  50.3 9.0 %copy-start.8 = (bf16[256,512]{1,0:T(8,128)(2,1)}, bf16[256,512]{1,0:T(8,128)(2,1)S(1)}, u32[]{:S(2)}) copy-start(bf16[256,512]{1,0:T(8,128)(2,1)S(1)} %collective-permute-done.5.refs_7_) | copy-start | bytes 786436
  50.3 5.4 %collective-permute-start.7 = (bf16[256,256]{1,0:T(8,128)(2,1)S(1)}, bf16[256,256]{1,0:T(8,128)(2,1)S(1)}, u32[]{:S(2)}, u32[]{:S(2)}) collective-permute-start(bf16[256,256]{1,0:T(8,128)(2,1)S(1)} %slice.9), channel_id=1, source_target_pairs={{0,196},{4,0},{64,4},{68,64},{128,68},{132,128},{192,132},{196,192... | collective-permute-start | bytes 393224 | tf_op jit(solution)/shard_map/ppermute | solution.py:203
  53.8 5.5 %copy-start.9 = (bf16[256,512]{1,0:T(8,128)(2,1)}, bf16[256,512]{1,0:T(8,128)(2,1)S(1)}, u32[]{:S(2)}) copy-start(bf16[256,512]{1,0:T(8,128)(2,1)S(1)} %collective-permute-done.4.refs_6_) | copy-start | bytes 786436
  53.8 5.4 %collective-permute-start.6 = (bf16[256,256]{1,0:T(8,128)(2,1)S(1)}, bf16[256,256]{1,0:T(8,128)(2,1)}, u32[]{:S(2)}, u32[]{:S(2)}) collective-permute-start(bf16[256,256]{1,0:T(8,128)(2,1)S(1)} %slice.8), channel_id=1, source_target_pairs={{0,4},{4,64},{64,68},{68,128},{128,132},{132,192},{192,196},{196,0... | collective-permute-start | bytes 393224 | tf_op jit(solution)/shard_map/ppermute | solution.py:203
  91.3 14.0 %copy-start.5 = (bf16[256,512]{1,0:T(8,128)(2,1)S(1)}, bf16[256,512]{1,0:T(8,128)(2,1)}, u32[]{:S(2)}) copy-start(bf16[256,512]{1,0:T(8,128)(2,1)} %get-tuple-element.18) | copy-start | bytes 786436
  91.3 4.1 %collective-permute-start.12 = (bf16[256,256]{1,0:T(8,128)(2,1)}, bf16[256,256]{1,0:T(8,128)(2,1)S(1)}, u32[]{:S(2)}, u32[]{:S(2)}) collective-permute-start(bf16[256,256]{1,0:T(8,128)(2,1)} %get-tuple-element.24), channel_id=1, source_target_pairs={{0,196},{4,0},{64,4},{68,64},{128,68},{132,128},{192,132},{196,192... | collective-permute-start | bytes 393224 | tf_op jit(solution)/shard_map/ppermute | solution.py:203
  91.4 6.3 %collective-permute-start.8 = (bf16[256,256]{1,0:T(8,128)(2,1)}, bf16[256,256]{1,0:T(8,128)(2,1)S(1)}, u32[]{:S(2)}, u32[]{:S(2)}) collective-permute-start(bf16[256,256]{1,0:T(8,128)(2,1)} %get-tuple-element.20), channel_id=1, source_target_pairs={{0,4},{4,64},{64,68},{68,128},{128,132},{132,192},{192,196},{196,0... | collective-permute-start | bytes 393224 | tf_op jit(solution)/shard_map/ppermute | solution.py:203
  96.4 6.6 %collective-permute-start.13 = (bf16[256,512]{1,0:T(8,128)(2,1)S(1)}, bf16[256,512]{1,0:T(8,128)(2,1)S(1)}, u32[]{:S(2)}, u32[]{:S(2)}) collective-permute-start(bf16[256,512]{1,0:T(8,128)(2,1)S(1)} %add_convert_fusion.3), channel_id=1, source_target_pairs={{0,196},{4,0},{64,4},{68,64},{128,68},{132,128},{192,132},{196,192... | collective-permute-start | bytes 786440 | tf_op jit(solution)/shard_map/ppermute | solution.py:203
  97.7 24.6 %copy-start.4 = (bf16[256,512]{1,0:T(8,128)(2,1)S(1)}, bf16[256,512]{1,0:T(8,128)(2,1)}, u32[]{:S(2)}) copy-start(bf16[256,512]{1,0:T(8,128)(2,1)} %get-tuple-element.21) | copy-start | bytes 786436
  98.7 6.5 %collective-permute-start.9 = (bf16[256,512]{1,0:T(8,128)(2,1)S(1)}, bf16[256,512]{1,0:T(8,128)(2,1)S(1)}, u32[]{:S(2)}, u32[]{:S(2)}) collective-permute-start(bf16[256,512]{1,0:T(8,128)(2,1)S(1)} %add_convert_fusion.6), channel_id=1, source_target_pairs={{0,4},{4,64},{64,68},{68,128},{128,132},{132,192},{192,196},{196,0... | collective-permute-start | bytes 786440 | tf_op jit(solution)/shard_map/ppermute | solution.py:203
  103.0 21.6 %copy-start.3 = (bf16[256,512]{1,0:T(8,128)(2,1)S(1)}, bf16[256,512]{1,0:T(8,128)(2,1)}, u32[]{:S(2)}) copy-start(bf16[256,512]{1,0:T(8,128)(2,1)} %get-tuple-element.17) | copy-start | bytes 786436
  104.1 18.3 %collective-permute-start.14 = (bf16[256,512]{1,0:T(8,128)(2,1)S(1)}, bf16[256,512]{1,0:T(8,128)(2,1)S(1)}, u32[]{:S(2)}, u32[]{:S(2)}) collective-permute-start(bf16[256,512]{1,0:T(8,128)(2,1)S(1)} %add_convert_fusion.2), channel_id=1, source_target_pairs={{0,196},{4,0},{64,4},{68,64},{128,68},{132,128},{192,132},{196,192... | collective-permute-start | bytes 786440 | tf_op jit(solution)/shard_map/ppermute | solution.py:203
  105.3 28.0 %copy-start.7 = (bf16[256,512]{1,0:T(8,128)(2,1)S(1)}, bf16[256,512]{1,0:T(8,128)(2,1)}, u32[]{:S(2)}) copy-start(bf16[256,512]{1,0:T(8,128)(2,1)} %get-tuple-element.16) | copy-start | bytes 786436
  105.3 19.2 %collective-permute-start.10 = (bf16[256,512]{1,0:T(8,128)(2,1)S(1)}, bf16[256,512]{1,0:T(8,128)(2,1)S(1)}, u32[]{:S(2)}, u32[]{:S(2)}) collective-permute-start(bf16[256,512]{1,0:T(8,128)(2,1)S(1)} %add_convert_fusion.5), channel_id=1, source_target_pairs={{0,4},{4,64},{64,68},{68,128},{128,132},{132,192},{192,196},{196,0... | collective-permute-start | bytes 786440 | tf_op jit(solution)/shard_map/ppermute | solution.py:203
  105.8 32.6 %all-to-all-start.2 = ((bf16[32,8,2048]{2,1,0:T(8,128)(2,1)}), bf16[32,8,2048]{2,1,0:T(8,128)(2,1)S(1)}, u32[]{:S(2)}, u32[]{:S(2)}) async-start(bf16[32,8,2048]{2,1,0:T(8,128)(2,1)} %bitcast.5), calls=%async_computation.2 | async-start | bytes 2097152 | tf_op jit(solution)/shard_map/all_to_all | solution.py:262
  122.4 7.8 %collective-permute-start.15 = (bf16[256,512]{1,0:T(8,128)(2,1)S(1)}, bf16[256,512]{1,0:T(8,128)(2,1)S(1)}, u32[]{:S(2)}, u32[]{:S(2)}) collective-permute-start(bf16[256,512]{1,0:T(8,128)(2,1)S(1)} %add_convert_fusion.1), channel_id=1, source_target_pairs={{0,196},{4,0},{64,4},{68,64},{128,68},{132,128},{192,132},{196,192... | collective-permute-start | bytes 786440 | tf_op jit(solution)/shard_map/ppermute | solution.py:203
  124.7 8.6 %collective-permute-start.11 = (bf16[256,512]{1,0:T(8,128)(2,1)S(1)}, bf16[256,512]{1,0:T(8,128)(2,1)S(1)}, u32[]{:S(2)}, u32[]{:S(2)}) collective-permute-start(bf16[256,512]{1,0:T(8,128)(2,1)S(1)} %add_convert_fusion.4), channel_id=1, source_target_pairs={{0,4},{4,64},{64,68},{68,128},{128,132},{132,192},{192,196},{196,0... | collective-permute-start | bytes 786440 | tf_op jit(solution)/shard_map/ppermute | solution.py:203
  138.3 5.3 %copy-start = (bf16[32,8,2048]{2,1,0:T(8,128)(2,1)}, bf16[32,8,2048]{2,1,0:T(8,128)(2,1)S(1)}, u32[]{:S(2)}) copy-start(bf16[32,8,2048]{2,1,0:T(8,128)(2,1)S(1)} %all-to-all-done.2) | copy-start | bytes 3145732
  138.3 14.2 %all-to-all-start.3 = ((bf16[32,8,512]{2,1,0:T(8,128)(2,1)}), bf16[32,8,512]{2,1,0:T(8,128)(2,1)S(1)}, u32[]{:S(2)}, u32[]{:S(2)}) async-start(bf16[32,8,512]{2,1,0:T(8,128)(2,1)} %fusion), calls=%async_computation.3 | async-start | bytes 524288 | tf_op jit(solution)/shard_map/all_to_all | solution.py:262
  (3 other events, 5.6 us)

commit v4 on v3

--- a/solution.py
+++ b/solution.py
@@ -99,133 +99,142 @@
 
 def attend_kernel(*refs):
     qg_ref, kv_refs, dkv_refs, dq_ref = refs[0], refs[1:10], refs[10:19], refs[19]
-    k_ref, v_ref, s_ref, p_ref, dk_ref, dv_ref, bias_ref, kt_ref = refs[20:]
-    keys = k_ref.shape[0]
+    kv_ref, x_ref, y_ref, p_ref, dk_ref, dv_ref, bias_ref, kt_ref = refs[20:]
+    keys = kv_ref.shape[0]
     rows = qg_ref.shape[0]
     block = keys // 8
     scale = HD ** (-0.5)
     unit = scale * math.log2(math.e)
     parts = [slice(t, t + KEY_TILE) for t in range(0, keys, KEY_TILE)]
     low = jnp.full((8, rows), -3e38, F32)
+    zero = jnp.zeros((8, rows), F32)
 
     def fold(tile):
         return tile.reshape(tile.shape[0] // 8, 8, rows)
 
-    def one_key_head(c):
-        for i in range(8):
-            here = slice(i * block, (i + 1) * block)
-            ref, first = (kv_refs[i], 2 * c * HD) if i < 7 else (kv_refs[7 + c], 0)
-            k_ref[here, :] = ref[:, first : first + HD]
-            v_ref[here, :] = ref[:, first + HD : first + 2 * HD]
-        dk_ref[...] = jnp.zeros_like(dk_ref)
-        dv_ref[...] = jnp.zeros_like(dv_ref)
-        empty = v_ref[:, :1].astype(F32) > 0.5 * EMPTY
-        bias_ref[...] = jnp.broadcast_to(jnp.where(empty, NEG, 0.0), bias_ref.shape)
-        kt_ref[...] = k_ref[...].T
-
-        def scores(buffer, q, part, top):
-            bias = jnp.concatenate([bias_ref[part, :]] * (rows // HD), axis=1)
-            s = contract_last(k_ref[part, :], q) + bias
-            s_ref[buffer, part, :] = s
-            return jnp.maximum(top, jnp.max(fold(s), axis=0))
-
-        def one_head(h, top, here, there, last=False):
-            at = c * HALF + h
-            q = qg_ref[:, columns(at)]
-            g = qg_ref[:, columns(QH + at)]
-            top = jnp.max(top, axis=0, keepdims=True)
-            total = jnp.zeros((8, rows), F32)
-            cross = jnp.zeros((8, rows), F32)
-            for part in parts:
-                dp = contract_last(v_ref[part, :], g)
-                e = jnp.exp2((s_ref[here, part, :] - top) * unit)
-                s_ref[here, part, :] = e
-                p_ref[part, :] = dp
-                total = total + jnp.sum(fold(e), axis=0)
-                cross = cross + jnp.sum(fold(e * dp), axis=0)
+    for i in range(8):
+        here = slice(i * block, (i + 1) * block)
+        for c in range(KVH):
+            cols = slice(2 * c * HD, 2 * (c + 1) * HD)
+            kv_ref[here, cols] = kv_refs[i][:, cols] if i < 7 else kv_refs[7 + c][...]
+    dk_ref[...] = jnp.zeros_like(dk_ref)
+    dv_ref[...] = jnp.zeros_like(dv_ref)
+    for c in range(KVH):
+        empty = kv_ref[:, (2 * c + 1) * HD : (2 * c + 1) * HD + 1].astype(F32) > 0.5 * EMPTY
+        bias_ref[c] = jnp.broadcast_to(jnp.where(empty, NEG, 0.0), (keys, HD))
+        kt_ref[c] = kv_ref[:, 2 * c * HD : (2 * c + 1) * HD].T
+
+    def key_head(h):
+        return int(h >= HALF) if isinstance(h, int) else (h >= HALF).astype(jnp.int32)
+
+    def scores(h, part, top):
+        c = key_head(h)
+        bias = jnp.concatenate([bias_ref[c, part, :]] * (rows // HD), axis=1)
+        x = contract_last(kv_ref[part, columns(2 * c)], qg_ref[:, columns(h)]) + bias
+        x_ref[part, :] = x
+        return jnp.maximum(top, jnp.max(fold(x), axis=0))
+
+    def weights(h, part, top, total, cross):
+        dp = contract_last(kv_ref[part, columns(2 * key_head(h) + 1)], qg_ref[:, columns(QH + h)])
+        e = jnp.exp2((x_ref[part, :] - top) * unit)
+        y_ref[part, :] = e
+        p_ref[part, :] = dp
+        return total + jnp.sum(fold(e), axis=0), cross + jnp.sum(fold(e * dp), axis=0)
+
+    def gradients(h, part, q, g, share, row_dot, dqt):
+        c = key_head(h)
+        p = y_ref[part, :] * share
+        ds = (p * (p_ref[part, :] - row_dot)).astype(BF)
+        dv_ref[c, part, :] += dot(p.astype(BF), g)
+        dk_ref[c, part, :] += dot(ds, q)
+        return dqt + dot(kt_ref[c, :, part], ds)
+
+    def step(i, top, total, cross):
+        known = not isinstance(i, int)
+        has_gradients = known or i >= 0
+        has_weights = known or 0 <= i + 1 < QH
+        has_scores = known or i + 2 < QH
+        top = jnp.max(top, axis=0, keepdims=True)
+        if has_gradients:
             share = 1.0 / jnp.sum(total, axis=0, keepdims=True)
             row_dot = jnp.sum(cross, axis=0, keepdims=True) * share
-            dqt = jnp.zeros((HD, rows), F32)
-            next_top = low
-            if not last:
-                next_q = qg_ref[:, columns(at + 1)]
-            for part in parts:
-                if not last:
-                    next_top = scores(there, next_q, part, next_top)
-                p = s_ref[here, part, :] * share
-                ds = (p * (p_ref[part, :] - row_dot)).astype(BF)
-                dv_ref[part, :] += dot(p.astype(BF), g)
-                dk_ref[part, :] += dot(ds, q)
-                dqt += dot(kt_ref[:, part], ds)
-            dq_ref[:, columns(at)] = (dqt * scale).T.astype(BF)
-            return next_top
-
-        def two_heads(i, top):
-            top = one_head(2 * i, top, 0, 1)
-            return one_head(2 * i + 1, top, 1, 0)
-
-        first_q = qg_ref[:, columns(c * HALF)]
-        top = low
+            q, g = qg_ref[:, columns(i)], qg_ref[:, columns(QH + i)]
+        dqt = jnp.zeros((HD, rows), F32)
+        next_top, next_total, next_cross = low, zero, zero
         for part in parts:
-            top = scores(0, first_q, part, top)
-        top = lax.fori_loop(0, HALF // 2 - 1, two_heads, top)
-        top = one_head(HALF - 2, top, 0, 1)
-        one_head(HALF - 1, top, 1, 0, last=True)
-        for i in range(8):
-            here = slice(i * block, (i + 1) * block)
+            if has_gradients:
+                dqt = gradients(i, part, q, g, share, row_dot, dqt)
+            if has_weights:
+                next_total, next_cross = weights(i + 1, part, top, next_total, next_cross)
+            if has_scores:
+                next_top = scores(i + 2, part, next_top)
+        if has_gradients:
+            dq_ref[:, columns(i)] = (dqt * scale).T.astype(BF)
+        return next_top, next_total, next_cross
+
+    state = step(-1, *step(-2, low, zero, zero))
+    state = lax.fori_loop(0, QH - 2, lambda i, state: step(i, *state), state)
+    step(QH - 1, *step(QH - 2, *state))
+
+    for i in range(8):
+        here = slice(i * block, (i + 1) * block)
+        for c in range(KVH):
             ref, first = (dkv_refs[i], 2 * c * HD) if i < 7 else (dkv_refs[7 + c], 0)
-            ref[:, first : first + HD] = (dk_ref[here, :] * scale).astype(BF)
-            ref[:, first + HD : first + 2 * HD] = dv_ref[here, :].astype(BF)
-
-    for c in range(KVH):
-        one_key_head(c)
-
-
-def unpack_q_kernel(head_ref, group_ref, dq_ref, out_ref):
+            ref[:, first : first + HD] = (dk_ref[c, here, :] * scale).astype(BF)
+            ref[:, first + HD : first + 2 * HD] = dv_ref[c, here, :].astype(BF)
+
+
+def unpack_q_kernel(head_ref, group_ref, dq_ref, out_ref, taker_ref):
     taker = taker_of(group_ref, dq_ref.shape[0])
+    taker_ref[...] = taker
     for slot in range(QH):
         place = place_of(head_ref[slot])
         out_ref[:, slot * HD : (slot + 1) * HD] = dot(taker, dq_ref[:, columns(place)]).astype(BF)
 
 
-def unpack_kv_kernel(group_ref, dkv_ref, dk_ref, dv_ref):
-    taker = taker_of(group_ref, dkv_ref.shape[0])
+def unpack_kv_kernel(taker_ref, dkv_ref, dk_ref, dv_ref):
+    rows = dot(taker_ref[...], dkv_ref[...]).astype(BF)
     for c in range(KVH):
         cols = slice(c * HD, (c + 1) * HD)
-        dk_ref[:, cols] = dot(taker, dkv_ref[:, 2 * c * HD : (2 * c + 1) * HD]).astype(BF)
-        dv_ref[:, cols] = dot(taker, dkv_ref[:, (2 * c + 1) * HD : (2 * c + 2) * HD]).astype(BF)
-
-
-def ring_steps(axis):
+        dk_ref[:, cols] = rows[:, 2 * c * HD : (2 * c + 1) * HD]
+        dv_ref[:, cols] = rows[:, (2 * c + 1) * HD : (2 * c + 2) * HD]
+
+
+def step_by(axis, distance):
     size = lax.axis_size(axis)
-    up = [(i, (i + 1) % size) for i in range(size)]
-    down = [(i, (i - 1) % size) for i in range(size)]
-    return lambda x: lax.ppermute(x, axis, up), lambda x: lax.ppermute(x, axis, down)
+    pairs = [(i, (i + distance) % size) for i in range(size)]
+    return lambda x: lax.ppermute(x, axis, pairs)
 
 
 def gather_column(block):
-    up, down = ring_steps(COLUMN)
+    up, down = step_by(COLUMN, 1), step_by(COLUMN, -1)
     half = block.shape[1] // 2
     below = above = block
     blocks = [block]
-    for _ in range(3):
+    for i in range(3):
+        if i == 2:
+            far = [
+                step_by(COLUMN, 2)(below[:, :half]),
+                step_by(COLUMN, -2)(above[:, half:]),
+            ]
         below, above = up(below), down(above)
         blocks += [below, above]
-    return blocks + [up(below[:, :half]), down(above[:, half:])]
+    return blocks + far
 
 
 def scatter_column(blocks):
-    up, down = ring_steps(COLUMN)
+    up, down = step_by(COLUMN, 1), step_by(COLUMN, -1)
 
     def plus(*terms):
         return sum(term.astype(F32) for term in terms).astype(BF)
 
     own, to_below, to_above = blocks[0], blocks[1:7:2], blocks[2:7:2]
     zeros = jnp.zeros_like(blocks[7])
-    rising = plus(to_above[2], jnp.concatenate([up(blocks[7]), zeros], axis=1))
-    falling = plus(to_below[2], jnp.concatenate([zeros, down(blocks[8])], axis=1))
-    for i in (1, 0):
-        rising, falling = plus(to_above[i], up(rising)), plus(to_below[i], down(falling))
+    far_up = jnp.concatenate([step_by(COLUMN, 2)(blocks[7]), zeros], axis=1)
+    far_down = jnp.concatenate([zeros, step_by(COLUMN, -2)(blocks[8])], axis=1)
+    rising = plus(to_above[1], up(to_above[2]), far_up)
+    falling = plus(to_below[1], down(to_below[2]), far_down)
+    rising, falling = plus(to_above[0], up(rising)), plus(to_below[0], down(falling))
     return plus(own, up(rising), down(falling))
 
 
@@ -277,14 +286,14 @@
         (*blocks, struct(slots, width_q)),
         inputs=1 + len(all_kv),
         scratch=[
-            pltpu.VMEM((all_keys, HD), BF),
-            pltpu.VMEM((all_keys, HD), BF),
-            pltpu.VMEM((2, all_keys, slots), F32),
+            pltpu.VMEM((all_keys, width_kv), BF),
             pltpu.VMEM((all_keys, slots), F32),
-            pltpu.VMEM((all_keys, HD), F32),
-            pltpu.VMEM((all_keys, HD), F32),
-            pltpu.VMEM((all_keys, HD), F32),
-            pltpu.VMEM((HD, all_keys), BF),
+            pltpu.VMEM((all_keys, slots), F32),
+            pltpu.VMEM((all_keys, slots), F32),
+            pltpu.VMEM((KVH, all_keys, HD), F32),
+            pltpu.VMEM((KVH, all_keys, HD), F32),
+            pltpu.VMEM((KVH, all_keys, HD), F32),
+            pltpu.VMEM((KVH, HD, all_keys), BF),
         ],
         cost=pl.CostEstimate(
             flops=10 * HD * pairs,
@@ -296,12 +305,12 @@
     kv_total = scatter_column(grad_kv)
     back_q = over_plane(grad_q)
     back_kv = over_plane(kv_total)
-    out_q = call(unpack_q_kernel, "unpack_q", struct(rows, width_q), scalars=1, inputs=2)(
-        head_slot, row_group, back_q
-    )
+    out_q, taker = call(
+        unpack_q_kernel, "unpack_q", (struct(rows, width_q), struct(rows, slots)), scalars=1, inputs=2
+    )(head_slot, row_group, back_q)
     out_k, out_v = call(
         unpack_kv_kernel, "unpack_kv", (struct(rows, KVH * HD), struct(rows, KVH * HD)), inputs=2
-    )(row_group, back_kv)
+    )(taker, back_kv)
     return out_q, out_k, out_v
 
 

time: 156 us -> 151 us (0.968)
  waiting for transfers between devices: 49.5 us -> 47.3 us
  Pallas kernels: 40.9 us -> 39.1 us
    ppermute x16, waiting for transfers between devices: 33.8 us -> 29.6 us  [step_by(): return lambda x: lax.ppermute(x, axis, pairs)]
    all_to_all x4, starting transfers between devices: 34.5 us -> 31.4 us  [over_plane(): return lax.all_to_all(array, PLANE, split_axis=0, concat_axis=0, tiled=True)]
    ppermute x16, starting transfers between devices: 23.3 us -> 25.9 us  [step_by(): return lambda x: lax.ppermute(x, axis, pairs)]
    all_to_all x4, waiting for transfers between devices: 15.7 us -> 17.7 us  [over_plane(): return lax.all_to_all(array, PLANE, split_axis=0, concat_axis=0, tiled=True)]
    pallas_call x1, Pallas kernels: 30.7 us -> 29.1 us  [per_device(): call(attend_kernel, 'attend', (*blocks, struct(slots, width_q)), inputs=1...]
    convert_element_type x6 -> x4, other arithmetic: 3.29 us -> 2.24 us  [plus(): return sum((term.astype(F32) for term in terms)).astype(BF)]
  transfers between devices with their start and end apart: 20 -> 20, of which waited for: 12 -> 9; matrix products, arithmetic and copies ran while one was open for 3% -> 2% of each run, Pallas kernels for 4% -> 4%
where the time goes in v4:
time: 151 us; the launch traced here: 150 us
  starting transfers between devices  57.3 us (38%)
  waiting for transfers between devices  47.3 us (31%)
  Pallas kernels  39.1 us (26%)
  other arithmetic  3.04 us (2%)
  local copies, waits for them, and re-layouts  2.79 us (2%)
    all_to_all x4, starting transfers between devices, over_plane(): return lax.all_to_all(array, PLANE, split_axis=0, concat_axis=0, tiled=True)  31.4 us
    ppermute x16, waiting for transfers between devices, step_by(): return lambda x: lax.ppermute(x, axis, pairs)  29.6 us
    pallas_call x1, Pallas kernels, per_device(): call(attend_kernel, 'attend', (*blocks, struct(slots, width_q)), inputs=1...  29.1 us
    ppermute x16, starting transfers between devices, step_by(): return lambda x: lax.ppermute(x, axis, pairs)  25.9 us
    all_to_all x4, waiting for transfers between devices, over_plane(): return lax.all_to_all(array, PLANE, split_axis=0, concat_axis=0, tiled=True)  17.7 us
    pallas_call x1, Pallas kernels, per_device(): call(pack_qg_kernel, 'pack_qg', struct(slots, 2 * width_q), scalars=1, in...  3.58 us
  transfers between devices with their start and end apart: 20, of which 9 were waited for; matrix products, arithmetic and copies ran while one was open for 2% of the time, Pallas kernels for 4%

profile of v4, /device:TPU:1, one launch (start us, length us, event | category | flops | bytes accessed | tf_op | source)
XLA Modules:
  0.0 150.4 jit_solution(10904383532273051249)
XLA Ops:
  0.6 1.9 %pack_kv.1 = bf16[256,512]{1,0:T(8,128)(2,1)} custom-call(s32[1,128]{1,0:T(1,128)} %bitcast.19, bf16[128,256]{1,0:T(8,128)(2,1)} %key_ref.1, bf16[128,256]{1,0:T(8,128)(2,1)} %value_ref.1), custom_call_target="tpu_custom_call" | custom-call | tf_op jit(solution)/shard_map/pack_kv/pallas_call | solution.py:273
  2.5 8.6 %all-to-all-start.1 = ((bf16[32,8,512]{2,1,0:T(8,128)(2,1)}), bf16[32,8,512]{2,1,0:T(8,128)(2,1)S(1)}, u32[]{:S(2)}, u32[]{:S(2)}) async-start(bf16[32,8,512]{2,1,0:T(8,128)(2,1)} %bitcast.15), calls=%async_computation.1 | async-start | bytes 524288 | tf_op jit(solution)/shard_map/all_to_all | solution.py:271
  11.1 3.6 %pack_qg.1 = bf16[256,4096]{1,0:T(8,128)(2,1)} custom-call(s32[16]{0:T(128)} %head_ref.3, s32[1,128]{1,0:T(1,128)} %bitcast.20, bf16[128,2048]{1,0:T(8,128)(2,1)} %query_ref.1, bf16[128,2048]{1,0:T(8,128)(2,1)} %grad_ref.1), custom_call_target="tpu_custom_call" | custom-call | tf_op jit(solution)/shard_map/pack_qg/pallas_call | solution.py:276
  14.7 5.3 %all-to-all-done.1 = bf16[32,8,512]{2,1,0:T(8,128)(2,1)S(1)} async-done(((bf16[32,8,512]{2,1,0:T(8,128)(2,1)}), bf16[32,8,512]{2,1,0:T(8,128)(2,1)S(1)}, u32[]{:S(2)}, u32[]{:S(2)}) %all-to-all-start.1) | async-done | bytes 262176 | tf_op jit(solution)/shard_map/all_to_all | solution.py:271
  20.0 4.1 %all-to-all-start = ((bf16[32,8,4096]{2,1,0:T(8,128)(2,1)}), bf16[32,8,4096]{2,1,0:T(8,128)(2,1)S(1)}, u32[]{:S(2)}, u32[]{:S(2)}) async-start(bf16[32,8,4096]{2,1,0:T(8,128)(2,1)} %bitcast.10), calls=%async_computation | async-start | bytes 4194304 | tf_op jit(solution)/shard_map/all_to_all | solution.py:271
  24.2 5.7 %collective-permute-start.1 = (bf16[256,512]{1,0:T(8,128)(2,1)S(1)}, bf16[256,512]{1,0:T(8,128)(2,1)S(1)}, u32[]{:S(2)}, u32[]{:S(2)}) collective-permute-start(bf16[256,512]{1,0:T(8,128)(2,1)S(1)} %bitcast.16), channel_id=1, source_target_pairs={{0,196},{4,0},{64,4},{68,64},{128,68},{132,128},{192,132},{196,192... | collective-permute-start | bytes 786440 | tf_op jit(solution)/shard_map/ppermute | solution.py:206
  29.8 5.5 %collective-permute-done.1.refs_3_ = bf16[256,512]{1,0:T(8,128)(2,1)S(1)} collective-permute-done((bf16[256,512]{1,0:T(8,128)(2,1)S(1)}, bf16[256,512]{1,0:T(8,128)(2,1)S(1)}, u32[]{:S(2)}, u32[]{:S(2)}) %collective-permute-start.1) | collective-permute-done | bytes 262176 | tf_op jit(solution)/shard_map/ppermute | solution.py:206
  35.3 3.4 %collective-permute-start.3 = (bf16[256,512]{1,0:T(8,128)(2,1)S(1)}, bf16[256,512]{1,0:T(8,128)(2,1)S(1)}, u32[]{:S(2)}, u32[]{:S(2)}) collective-permute-start(bf16[256,512]{1,0:T(8,128)(2,1)S(1)} %collective-permute-done.1.refs_3_), channel_id=1, source_target_pairs={{0,196},{4,0},{64,4},{68,64},{128,68},{132,128},{192,132},{196,192... | collective-permute-start | bytes 786440 | tf_op jit(solution)/shard_map/ppermute | solution.py:206
  38.7 4.5 %collective-permute-done.3.refs_5_ = bf16[256,512]{1,0:T(8,128)(2,1)S(1)} collective-permute-done((bf16[256,512]{1,0:T(8,128)(2,1)S(1)}, bf16[256,512]{1,0:T(8,128)(2,1)S(1)}, u32[]{:S(2)}, u32[]{:S(2)}) %collective-permute-start.3) | collective-permute-done | bytes 262176 | tf_op jit(solution)/shard_map/ppermute | solution.py:206
  43.3 3.4 %collective-permute-start.5 = (bf16[256,512]{1,0:T(8,128)(2,1)S(1)}, bf16[256,512]{1,0:T(8,128)(2,1)S(1)}, u32[]{:S(2)}, u32[]{:S(2)}) collective-permute-start(bf16[256,512]{1,0:T(8,128)(2,1)S(1)} %collective-permute-done.3.refs_5_), channel_id=1, source_target_pairs={{0,196},{4,0},{64,4},{68,64},{128,68},{132,128},{192,132},{196,192... | collective-permute-start | bytes 786440 | tf_op jit(solution)/shard_map/ppermute | solution.py:206
  46.7 1.3 collective-permute-start.7
  48.0 1.4 collective-permute-start.6
  49.4 4.3 %collective-permute-done.7.refs_9_ = bf16[256,256]{1,0:T(8,128)(2,1)S(1)} collective-permute-done((bf16[256,256]{1,0:T(8,128)(2,1)S(1)}, bf16[256,256]{1,0:T(8,128)(2,1)S(1)}, u32[]{:S(2)}, u32[]{:S(2)}) %collective-permute-start.7) | collective-permute-done | bytes 131104 | tf_op jit(solution)/shard_map/ppermute | solution.py:206
  53.7 4.5 %collective-permute-done.6.refs_8_ = bf16[256,256]{1,0:T(8,128)(2,1)S(1)} collective-permute-done((bf16[256,256]{1,0:T(8,128)(2,1)S(1)}, bf16[256,256]{1,0:T(8,128)(2,1)S(1)}, u32[]{:S(2)}, u32[]{:S(2)}) %collective-permute-start.6) | collective-permute-done | bytes 131104 | tf_op jit(solution)/shard_map/ppermute | solution.py:206
  59.5 0.7 copy-done.1
  60.3 29.1 %attend.1 = (bf16[256,512]{1,0:T(8,128)(2,1)}, bf16[256,512]{1,0:T(8,128)(2,1)}, bf16[256,512]{1,0:T(8,128)(2,1)}, bf16[256,512]{1,0:T(8,128)(2,1)}, bf16[256,51...) custom-call(bf16[256,4096]{1,0:T(8,128)(2,1)} %bitcast.12, ...), custom_call_target="tpu_custom_call" | custom-call | flops 10737418240 | bytes 7340032 | tf_op jit(solution)/shard_map/attend/pallas_call | solution.py:283
  89.4 0.9 collective-permute-start.8
  90.3 2.5 %collective-permute-start.12 = (bf16[256,512]{1,0:T(8,128)(2,1)}, bf16[256,512]{1,0:T(8,128)(2,1)S(1)}, u32[]{:S(2)}, u32[]{:S(2)}) collective-permute-start(bf16[256,512]{1,0:T(8,128)(2,1)} %get-tuple-element.27), channel_id=1, source_target_pairs={{0,196},{4,0},{64,4},{68,64},{128,68},{132,128},{192,132},{196,192... | collective-permute-start | bytes 786440 | tf_op jit(solution)/shard_map/ppermute | solution.py:206
  92.8 1.7 %collective-permute-start.13 = (bf16[256,256]{1,0:T(8,128)(2,1)}, bf16[256,256]{1,0:T(8,128)(2,1)S(1)}, u32[]{:S(2)}, u32[]{:S(2)}) collective-permute-start(bf16[256,256]{1,0:T(8,128)(2,1)} %get-tuple-element.28), channel_id=1, source_target_pairs={{0,192},{4,196},{64,0},{68,4},{128,64},{132,68},{192,128},{196,132... | collective-permute-start | bytes 393224 | tf_op jit(solution)/shard_map/ppermute | solution.py:206
  94.5 4.8 %collective-permute-done.9 = bf16[256,256]{1,0:T(8,128)(2,1)S(1)} collective-permute-done((bf16[256,256]{1,0:T(8,128)(2,1)}, bf16[256,256]{1,0:T(8,128)(2,1)S(1)}, u32[]{:S(2)}, u32[]{:S(2)}) %collective-permute-start.9) | collective-permute-done | bytes 131104 | tf_op jit(solution)/shard_map/ppermute | solution.py:206
  99.3 1.0 add_convert_fusion.4
  100.3 2.2 %collective-permute-start.10 = (bf16[256,512]{1,0:T(8,128)(2,1)S(1)}, bf16[256,512]{1,0:T(8,128)(2,1)S(1)}, u32[]{:S(2)}, u32[]{:S(2)}) collective-permute-start(bf16[256,512]{1,0:T(8,128)(2,1)S(1)} %add_convert_fusion.4), channel_id=1, source_target_pairs={{0,4},{4,64},{64,68},{68,128},{128,132},{132,192},{192,196},{196,0... | collective-permute-start | bytes 786440 | tf_op jit(solution)/shard_map/ppermute | solution.py:206
  102.6 1.1 add_convert_fusion.2
  104.3 13.4 %all-to-all-start.2 = ((bf16[32,8,2048]{2,1,0:T(8,128)(2,1)}), bf16[32,8,2048]{2,1,0:T(8,128)(2,1)S(1)}, u32[]{:S(2)}, u32[]{:S(2)}) async-start(bf16[32,8,2048]{2,1,0:T(8,128)(2,1)} %bitcast.14), calls=%async_computation.2 | async-start | bytes 2097152 | tf_op jit(solution)/shard_map/all_to_all | solution.py:271
  118.0 2.7 %collective-permute-start.15 = (bf16[256,512]{1,0:T(8,128)(2,1)S(1)}, bf16[256,512]{1,0:T(8,128)(2,1)S(1)}, u32[]{:S(2)}, u32[]{:S(2)}) collective-permute-start(bf16[256,512]{1,0:T(8,128)(2,1)S(1)} %add_convert_fusion.1), channel_id=1, source_target_pairs={{0,196},{4,0},{64,4},{68,64},{128,68},{132,128},{192,132},{196,192... | collective-permute-start | bytes 786440 | tf_op jit(solution)/shard_map/ppermute | solution.py:206
  120.7 6.1 %collective-permute-done.11 = bf16[256,512]{1,0:T(8,128)(2,1)S(1)} collective-permute-done((bf16[256,512]{1,0:T(8,128)(2,1)S(1)}, bf16[256,512]{1,0:T(8,128)(2,1)S(1)}, u32[]{:S(2)}, u32[]{:S(2)}) %collective-permute-start.11) | collective-permute-done | bytes 262176 | tf_op jit(solution)/shard_map/ppermute | solution.py:206
  126.8 0.8 fusion
  127.5 6.2 %all-to-all-done.2 = bf16[32,8,2048]{2,1,0:T(8,128)(2,1)S(1)} async-done(((bf16[32,8,2048]{2,1,0:T(8,128)(2,1)}), bf16[32,8,2048]{2,1,0:T(8,128)(2,1)S(1)}, u32[]{:S(2)}, u32[]{:S(2)}) %all-to-all-start.2) | async-done | bytes 1048608 | tf_op jit(solution)/shard_map/all_to_all | solution.py:271
  133.7 5.3 %all-to-all-start.3 = ((bf16[32,8,512]{2,1,0:T(8,128)(2,1)}), bf16[32,8,512]{2,1,0:T(8,128)(2,1)S(1)}, u32[]{:S(2)}, u32[]{:S(2)}) async-start(bf16[32,8,512]{2,1,0:T(8,128)(2,1)} %fusion), calls=%async_computation.3 | async-start | bytes 524288 | tf_op jit(solution)/shard_map/all_to_all | solution.py:271
  139.0 2.7 %unpack_q.1 = (bf16[128,2048]{1,0:T(8,128)(2,1)}, bf16[128,256]{1,0:T(8,128)(2,1)}) custom-call(s32[16]{0:T(128)} %head_ref.3, s32[1,128]{1,0:T(1,128)} %bitcast.21, bf16[256,2048]{1,0:T(8,128)(2,1)} %bitcast.11), custom_call_target="tpu_custom_call" | custom-call | tf_op jit(solution)/shard_map/unpack_q/pallas_call | solution.py:308
  141.7 6.2 %all-to-all-done.3 = bf16[32,8,512]{2,1,0:T(8,128)(2,1)S(1)} async-done(((bf16[32,8,512]{2,1,0:T(8,128)(2,1)}), bf16[32,8,512]{2,1,0:T(8,128)(2,1)S(1)}, u32[]{:S(2)}, u32[]{:S(2)}) %all-to-all-start.3) | async-done | bytes 262176 | tf_op jit(solution)/shard_map/all_to_all | solution.py:271
  148.6 1.8 %unpack_kv.1 = (bf16[128,256]{1,0:T(8,128)(2,1)}, bf16[128,256]{1,0:T(8,128)(2,1)}) custom-call(bf16[128,256]{1,0:T(8,128)(2,1)} %get-tuple-element.19.taker_ref, bf16[256,512]{1,0:T(8,128)(2,1)} %bitcast.13), custom_call_target="tpu_custom_call" | custom-call | tf_op jit(solution)/shard_map/unpack_kv/pallas_call | solution.py:311
  (48 shorter events, 2.9 us)
Async XLA Ops:
  2.5 17.5 %all-to-all-start.1 = ((bf16[32,8,512]{2,1,0:T(8,128)(2,1)}), bf16[32,8,512]{2,1,0:T(8,128)(2,1)S(1)}, u32[]{:S(2)}, u32[]{:S(2)}) async-start(bf16[32,8,512]{2,1,0:T(8,128)(2,1)} %bitcast.15), calls=%async_computation.1 | async-start | bytes 524288 | tf_op jit(solution)/shard_map/all_to_all | solution.py:271
  20.0 9.8 %copy-start.5 = (bf16[32,8,512]{2,1,0:T(8,128)(2,1)}, bf16[32,8,512]{2,1,0:T(8,128)(2,1)S(1)}, u32[]{:S(2)}) copy-start(bf16[32,8,512]{2,1,0:T(8,128)(2,1)S(1)} %all-to-all-done.1) | copy-start | bytes 786436
  20.0 38.8 %all-to-all-start = ((bf16[32,8,4096]{2,1,0:T(8,128)(2,1)}), bf16[32,8,4096]{2,1,0:T(8,128)(2,1)S(1)}, u32[]{:S(2)}, u32[]{:S(2)}) async-start(bf16[32,8,4096]{2,1,0:T(8,128)(2,1)} %bitcast.10), calls=%async_computation | async-start | bytes 4194304 | tf_op jit(solution)/shard_map/all_to_all | solution.py:271
  24.2 11.1 %collective-permute-start.1 = (bf16[256,512]{1,0:T(8,128)(2,1)S(1)}, bf16[256,512]{1,0:T(8,128)(2,1)S(1)}, u32[]{:S(2)}, u32[]{:S(2)}) collective-permute-start(bf16[256,512]{1,0:T(8,128)(2,1)S(1)} %bitcast.16), channel_id=1, source_target_pairs={{0,196},{4,0},{64,4},{68,64},{128,68},{132,128},{192,132},{196,192... | collective-permute-start | bytes 786440 | tf_op jit(solution)/shard_map/ppermute | solution.py:206
  29.8 8.9 %collective-permute-start = (bf16[256,512]{1,0:T(8,128)(2,1)S(1)}, bf16[256,512]{1,0:T(8,128)(2,1)S(1)}, u32[]{:S(2)}, u32[]{:S(2)}) collective-permute-start(bf16[256,512]{1,0:T(8,128)(2,1)S(1)} %bitcast.17), channel_id=1, source_target_pairs={{0,4},{4,64},{64,68},{68,128},{128,132},{132,192},{192,196},{196,0... | collective-permute-start | bytes 786440 | tf_op jit(solution)/shard_map/ppermute | solution.py:206
  35.3 23.6 %copy-start.9 = (bf16[256,512]{1,0:T(8,128)(2,1)}, bf16[256,512]{1,0:T(8,128)(2,1)S(1)}, u32[]{:S(2)}) copy-start(bf16[256,512]{1,0:T(8,128)(2,1)S(1)} %collective-permute-done.1.refs_3_) | copy-start | bytes 786436
  35.3 8.0 %collective-permute-start.3 = (bf16[256,512]{1,0:T(8,128)(2,1)S(1)}, bf16[256,512]{1,0:T(8,128)(2,1)S(1)}, u32[]{:S(2)}, u32[]{:S(2)}) collective-permute-start(bf16[256,512]{1,0:T(8,128)(2,1)S(1)} %collective-permute-done.1.refs_3_), channel_id=1, source_target_pairs={{0,196},{4,0},{64,4},{68,64},{128,68},{132,128},{192,132},{196,192... | collective-permute-start | bytes 786440 | tf_op jit(solution)/shard_map/ppermute | solution.py:206
  38.7 20.2 %copy-start.10 = (bf16[256,512]{1,0:T(8,128)(2,1)}, bf16[256,512]{1,0:T(8,128)(2,1)S(1)}, u32[]{:S(2)}) copy-start(bf16[256,512]{1,0:T(8,128)(2,1)S(1)} %collective-permute-done.refs_2_) | copy-start | bytes 786436
  38.7 8.0 %collective-permute-start.2 = (bf16[256,512]{1,0:T(8,128)(2,1)S(1)}, bf16[256,512]{1,0:T(8,128)(2,1)S(1)}, u32[]{:S(2)}, u32[]{:S(2)}) collective-permute-start(bf16[256,512]{1,0:T(8,128)(2,1)S(1)} %collective-permute-done.refs_2_), channel_id=1, source_target_pairs={{0,4},{4,64},{64,68},{68,128},{128,132},{132,192},{192,196},{196,0... | collective-permute-start | bytes 786440 | tf_op jit(solution)/shard_map/ppermute | solution.py:206
  43.3 15.6 %copy-start.7 = (bf16[256,512]{1,0:T(8,128)(2,1)}, bf16[256,512]{1,0:T(8,128)(2,1)S(1)}, u32[]{:S(2)}) copy-start(bf16[256,512]{1,0:T(8,128)(2,1)S(1)} %collective-permute-done.3.refs_5_) | copy-start | bytes 786436
  43.3 14.9 %collective-permute-start.5 = (bf16[256,512]{1,0:T(8,128)(2,1)S(1)}, bf16[256,512]{1,0:T(8,128)(2,1)S(1)}, u32[]{:S(2)}, u32[]{:S(2)}) collective-permute-start(bf16[256,512]{1,0:T(8,128)(2,1)S(1)} %collective-permute-done.3.refs_5_), channel_id=1, source_target_pairs={{0,196},{4,0},{64,4},{68,64},{128,68},{132,128},{192,132},{196,192... | collective-permute-start | bytes 786440 | tf_op jit(solution)/shard_map/ppermute | solution.py:206
  46.7 12.2 %copy-start.8 = (bf16[256,512]{1,0:T(8,128)(2,1)}, bf16[256,512]{1,0:T(8,128)(2,1)S(1)}, u32[]{:S(2)}) copy-start(bf16[256,512]{1,0:T(8,128)(2,1)S(1)} %collective-permute-done.2.refs_4_) | copy-start | bytes 786436
  46.7 12.2 %collective-permute-start.4 = (bf16[256,512]{1,0:T(8,128)(2,1)S(1)}, bf16[256,512]{1,0:T(8,128)(2,1)}, u32[]{:S(2)}, u32[]{:S(2)}) collective-permute-start(bf16[256,512]{1,0:T(8,128)(2,1)S(1)} %collective-permute-done.2.refs_4_), channel_id=1, source_target_pairs={{0,4},{4,64},{64,68},{68,128},{128,132},{132,192},{192,196},{196,0... | collective-permute-start | bytes 786440 | tf_op jit(solution)/shard_map/ppermute | solution.py:206
  46.7 7.0 %collective-permute-start.7 = (bf16[256,256]{1,0:T(8,128)(2,1)S(1)}, bf16[256,256]{1,0:T(8,128)(2,1)S(1)}, u32[]{:S(2)}, u32[]{:S(2)}) collective-permute-start(bf16[256,256]{1,0:T(8,128)(2,1)S(1)} %slice.9), channel_id=1, source_target_pairs={{0,192},{4,196},{64,0},{68,4},{128,64},{132,68},{192,128},{196,132... | collective-permute-start | bytes 393224 | tf_op jit(solution)/shard_map/ppermute | solution.py:206
  48.0 10.1 %collective-permute-start.6 = (bf16[256,256]{1,0:T(8,128)(2,1)S(1)}, bf16[256,256]{1,0:T(8,128)(2,1)S(1)}, u32[]{:S(2)}, u32[]{:S(2)}) collective-permute-start(bf16[256,256]{1,0:T(8,128)(2,1)S(1)} %slice.8), channel_id=1, source_target_pairs={{0,64},{4,68},{64,128},{68,132},{128,192},{132,196},{192,0},{196,4... | collective-permute-start | bytes 393224 | tf_op jit(solution)/shard_map/ppermute | solution.py:206
  53.7 5.2 %copy-start.12 = (bf16[256,256]{1,0:T(8,128)(2,1)}, bf16[256,256]{1,0:T(8,128)(2,1)S(1)}, u32[]{:S(2)}) copy-start(bf16[256,256]{1,0:T(8,128)(2,1)S(1)} %collective-permute-done.7.refs_9_) | copy-start | bytes 393220
  58.9 1.4 copy-start.1
  89.4 28.3 %copy-start.4 = (bf16[256,512]{1,0:T(8,128)(2,1)S(1)}, bf16[256,512]{1,0:T(8,128)(2,1)}, u32[]{:S(2)}) copy-start(bf16[256,512]{1,0:T(8,128)(2,1)} %get-tuple-element.21) | copy-start | bytes 786436
  89.4 9.9 %collective-permute-start.8 = (bf16[256,512]{1,0:T(8,128)(2,1)}, bf16[256,512]{1,0:T(8,128)(2,1)S(1)}, u32[]{:S(2)}, u32[]{:S(2)}) collective-permute-start(bf16[256,512]{1,0:T(8,128)(2,1)} %get-tuple-element.23), channel_id=1, source_target_pairs={{0,4},{4,64},{64,68},{68,128},{128,132},{132,192},{192,196},{196,0... | collective-permute-start | bytes 786440 | tf_op jit(solution)/shard_map/ppermute | solution.py:206
  90.3 9.0 %collective-permute-start.9 = (bf16[256,256]{1,0:T(8,128)(2,1)}, bf16[256,256]{1,0:T(8,128)(2,1)S(1)}, u32[]{:S(2)}, u32[]{:S(2)}) collective-permute-start(bf16[256,256]{1,0:T(8,128)(2,1)} %get-tuple-element.24), channel_id=1, source_target_pairs={{0,64},{4,68},{64,128},{68,132},{128,192},{132,196},{192,0},{196,4... | collective-permute-start | bytes 393224 | tf_op jit(solution)/shard_map/ppermute | solution.py:206
  90.3 12.2 %collective-permute-start.12 = (bf16[256,512]{1,0:T(8,128)(2,1)}, bf16[256,512]{1,0:T(8,128)(2,1)S(1)}, u32[]{:S(2)}, u32[]{:S(2)}) collective-permute-start(bf16[256,512]{1,0:T(8,128)(2,1)} %get-tuple-element.27), channel_id=1, source_target_pairs={{0,196},{4,0},{64,4},{68,64},{128,68},{132,128},{192,132},{196,192... | collective-permute-start | bytes 786440 | tf_op jit(solution)/shard_map/ppermute | solution.py:206
  92.8 9.7 %collective-permute-start.13 = (bf16[256,256]{1,0:T(8,128)(2,1)}, bf16[256,256]{1,0:T(8,128)(2,1)S(1)}, u32[]{:S(2)}, u32[]{:S(2)}) collective-permute-start(bf16[256,256]{1,0:T(8,128)(2,1)} %get-tuple-element.28), channel_id=1, source_target_pairs={{0,192},{4,196},{64,0},{68,4},{128,64},{132,68},{192,128},{196,132... | collective-permute-start | bytes 393224 | tf_op jit(solution)/shard_map/ppermute | solution.py:206
  100.3 17.6 %copy-start.3 = (bf16[256,512]{1,0:T(8,128)(2,1)S(1)}, bf16[256,512]{1,0:T(8,128)(2,1)}, u32[]{:S(2)}) copy-start(bf16[256,512]{1,0:T(8,128)(2,1)} %get-tuple-element.25) | copy-start | bytes 786436
  100.3 17.4 %collective-permute-start.10 = (bf16[256,512]{1,0:T(8,128)(2,1)S(1)}, bf16[256,512]{1,0:T(8,128)(2,1)S(1)}, u32[]{:S(2)}, u32[]{:S(2)}) collective-permute-start(bf16[256,512]{1,0:T(8,128)(2,1)S(1)} %add_convert_fusion.4), channel_id=1, source_target_pairs={{0,4},{4,64},{64,68},{68,128},{128,132},{132,192},{192,196},{196,0... | collective-permute-start | bytes 786440 | tf_op jit(solution)/shard_map/ppermute | solution.py:206
  102.6 24.2 %copy-start.6 = (bf16[256,512]{1,0:T(8,128)(2,1)S(1)}, bf16[256,512]{1,0:T(8,128)(2,1)}, u32[]{:S(2)}) copy-start(bf16[256,512]{1,0:T(8,128)(2,1)} %get-tuple-element.20) | copy-start | bytes 786436
  103.6 14.2 %collective-permute-start.14 = (bf16[256,512]{1,0:T(8,128)(2,1)S(1)}, bf16[256,512]{1,0:T(8,128)(2,1)S(1)}, u32[]{:S(2)}, u32[]{:S(2)}) collective-permute-start(bf16[256,512]{1,0:T(8,128)(2,1)S(1)} %add_convert_fusion.2), channel_id=1, source_target_pairs={{0,196},{4,0},{64,4},{68,64},{128,68},{132,128},{192,132},{196,192... | collective-permute-start | bytes 786440 | tf_op jit(solution)/shard_map/ppermute | solution.py:206
  104.3 29.5 %all-to-all-start.2 = ((bf16[32,8,2048]{2,1,0:T(8,128)(2,1)}), bf16[32,8,2048]{2,1,0:T(8,128)(2,1)S(1)}, u32[]{:S(2)}, u32[]{:S(2)}) async-start(bf16[32,8,2048]{2,1,0:T(8,128)(2,1)} %bitcast.14), calls=%async_computation.2 | async-start | bytes 2097152 | tf_op jit(solution)/shard_map/all_to_all | solution.py:271
  117.8 9.0 %collective-permute-start.11 = (bf16[256,512]{1,0:T(8,128)(2,1)S(1)}, bf16[256,512]{1,0:T(8,128)(2,1)S(1)}, u32[]{:S(2)}, u32[]{:S(2)}) collective-permute-start(bf16[256,512]{1,0:T(8,128)(2,1)S(1)} %add_convert_fusion.3), channel_id=1, source_target_pairs={{0,4},{4,64},{64,68},{68,128},{128,132},{132,192},{192,196},{196,0... | collective-permute-start | bytes 786440 | tf_op jit(solution)/shard_map/ppermute | solution.py:206
  118.0 8.8 %collective-permute-start.15 = (bf16[256,512]{1,0:T(8,128)(2,1)S(1)}, bf16[256,512]{1,0:T(8,128)(2,1)S(1)}, u32[]{:S(2)}, u32[]{:S(2)}) collective-permute-start(bf16[256,512]{1,0:T(8,128)(2,1)S(1)} %add_convert_fusion.1), channel_id=1, source_target_pairs={{0,196},{4,0},{64,4},{68,64},{128,68},{132,128},{192,132},{196,192... | collective-permute-start | bytes 786440 | tf_op jit(solution)/shard_map/ppermute | solution.py:206
  133.7 5.3 %copy-start = (bf16[32,8,2048]{2,1,0:T(8,128)(2,1)}, bf16[32,8,2048]{2,1,0:T(8,128)(2,1)S(1)}, u32[]{:S(2)}) copy-start(bf16[32,8,2048]{2,1,0:T(8,128)(2,1)S(1)} %all-to-all-done.2) | copy-start | bytes 3145732
  133.7 14.2 %all-to-all-start.3 = ((bf16[32,8,512]{2,1,0:T(8,128)(2,1)}), bf16[32,8,512]{2,1,0:T(8,128)(2,1)S(1)}, u32[]{:S(2)}, u32[]{:S(2)}) async-start(bf16[32,8,512]{2,1,0:T(8,128)(2,1)} %fusion), calls=%async_computation.3 | async-start | bytes 524288 | tf_op jit(solution)/shard_map/all_to_all | solution.py:271
  147.9 0.7 copy-start.2
  (2 other events, 1.4 us)

commit v5 on v4

--- a/solution.py
+++ b/solution.py
@@ -21,8 +21,9 @@
 COLUMN = ("zh", "zl")
 BF = jnp.bfloat16
 F32 = jnp.float32
-KEY_TILE = 512
-VMEM = 60 * 1024 * 1024
+KEY_TILE = 2048
+CHUNK = 64
+MIB = 1024 * 1024
 
 
 def contract_last(left, right):
@@ -98,54 +99,73 @@
 
 
 def attend_kernel(*refs):
-    qg_ref, kv_refs, dkv_refs, dq_ref = refs[0], refs[1:10], refs[10:19], refs[19]
-    kv_ref, x_ref, y_ref, p_ref, dk_ref, dv_ref, bias_ref, kt_ref = refs[20:]
+    source_refs, dkv_refs, dq_ref = refs[:10], refs[10:19], refs[19]
+    qg_ref, kv_ref, x_ref, y_ref, p_ref, dk_ref, dv_ref, bias_ref, kt_ref, sems = refs[20:]
     keys = kv_ref.shape[0]
     rows = qg_ref.shape[0]
     block = keys // 8
     scale = HD ** (-0.5)
     unit = scale * math.log2(math.e)
     parts = [slice(t, t + KEY_TILE) for t in range(0, keys, KEY_TILE)]
+    chunks = range(0, KEY_TILE, CHUNK)
     low = jnp.full((8, rows), -3e38, F32)
     zero = jnp.zeros((8, rows), F32)
 
     def fold(tile):
         return tile.reshape(tile.shape[0] // 8, 8, rows)
 
-    for i in range(8):
-        here = slice(i * block, (i + 1) * block)
-        for c in range(KVH):
-            cols = slice(2 * c * HD, 2 * (c + 1) * HD)
-            kv_ref[here, cols] = kv_refs[i][:, cols] if i < 7 else kv_refs[7 + c][...]
+    targets = [kv_ref.at[i * block : (i + 1) * block, :] for i in range(7)]
+    targets += [kv_ref.at[7 * block :, : 2 * HD], kv_ref.at[7 * block :, 2 * HD :], qg_ref]
+    fetches = [
+        pltpu.make_async_copy(source, target, sems.at[i])
+        for i, (source, target) in enumerate(zip(source_refs, targets))
+    ]
+    for fetch in fetches:
+        fetch.start()
     dk_ref[...] = jnp.zeros_like(dk_ref)
     dv_ref[...] = jnp.zeros_like(dv_ref)
+    for fetch in fetches[:9]:
+        fetch.wait()
     for c in range(KVH):
         empty = kv_ref[:, (2 * c + 1) * HD : (2 * c + 1) * HD + 1].astype(F32) > 0.5 * EMPTY
         bias_ref[c] = jnp.broadcast_to(jnp.where(empty, NEG, 0.0), (keys, HD))
         kt_ref[c] = kv_ref[:, 2 * c * HD : (2 * c + 1) * HD].T
+    fetches[9].wait()
 
     def key_head(h):
         return int(h >= HALF) if isinstance(h, int) else (h >= HALF).astype(jnp.int32)
 
     def scores(h, part, top):
         c = key_head(h)
-        bias = jnp.concatenate([bias_ref[c, part, :]] * (rows // HD), axis=1)
-        x = contract_last(kv_ref[part, columns(2 * c)], qg_ref[:, columns(h)]) + bias
-        x_ref[part, :] = x
-        return jnp.maximum(top, jnp.max(fold(x), axis=0))
+        x = contract_last(kv_ref[part, columns(2 * c)], qg_ref[:, columns(h)])
+        for u in chunks:
+            here = slice(part.start + u, part.start + u + CHUNK)
+            biased = x[u : u + CHUNK] + jnp.concatenate([bias_ref[c, here, :]] * (rows // HD), axis=1)
+            x_ref[here, :] = biased
+            top = jnp.maximum(top, jnp.max(fold(biased), axis=0))
+        return top
 
     def weights(h, part, top, total, cross):
         dp = contract_last(kv_ref[part, columns(2 * key_head(h) + 1)], qg_ref[:, columns(QH + h)])
-        e = jnp.exp2((x_ref[part, :] - top) * unit)
-        y_ref[part, :] = e
-        p_ref[part, :] = dp
-        return total + jnp.sum(fold(e), axis=0), cross + jnp.sum(fold(e * dp), axis=0)
+        for u in chunks:
+            here = slice(part.start + u, part.start + u + CHUNK)
+            e = jnp.exp2((x_ref[here, :] - top) * unit)
+            y_ref[here, :] = e
+            p_ref[here, :] = dp[u : u + CHUNK]
+            total = total + jnp.sum(fold(e), axis=0)
+            cross = cross + jnp.sum(fold(e * dp[u : u + CHUNK]), axis=0)
+        return total, cross
 
     def gradients(h, part, q, g, share, row_dot, dqt):
         c = key_head(h)
-        p = y_ref[part, :] * share
-        ds = (p * (p_ref[part, :] - row_dot)).astype(BF)
-        dv_ref[c, part, :] += dot(p.astype(BF), g)
+        p, ds = [], []
+        for u in chunks:
+            here = slice(part.start + u, part.start + u + CHUNK)
+            attend = y_ref[here, :] * share
+            p.append(attend.astype(BF))
+            ds.append((attend * (p_ref[here, :] - row_dot)).astype(BF))
+        ds = jnp.concatenate(ds, axis=0)
+        dv_ref[c, part, :] += dot(jnp.concatenate(p, axis=0), g)
         dk_ref[c, part, :] += dot(ds, q)
         return dqt + dot(kt_ref[c, :, part], ds)
 
@@ -242,16 +262,18 @@
     return jax.ShapeDtypeStruct(shape, BF)
 
 
-def call(kernel, name, out_shape, scalars=0, inputs=1, scratch=(), cost=None):
+def call(kernel, name, out_shape, scalars=0, inputs=1, far=0, scratch=(), vmem=16, cost=None):
     whole = pl.BlockSpec(memory_space=pltpu.VMEM)
     many = isinstance(out_shape, tuple)
     return pl.pallas_call(
         kernel,
         out_shape=out_shape,
-        in_specs=[pl.BlockSpec(memory_space=pltpu.SMEM)] * scalars + [whole] * inputs,
+        in_specs=[pl.BlockSpec(memory_space=pltpu.SMEM)] * scalars
+        + [whole] * inputs
+        + [pl.BlockSpec(memory_space=pltpu.HBM)] * far,
         out_specs=(whole,) * len(out_shape) if many else whole,
         scratch_shapes=scratch,
-        compiler_params=pltpu.CompilerParams(vmem_limit_bytes=VMEM),
+        compiler_params=pltpu.CompilerParams(vmem_limit_bytes=vmem * MIB),
         cost_estimate=cost,
         name=name,
     )
@@ -270,10 +292,12 @@
     def over_plane(array):
         return lax.all_to_all(array, PLANE, split_axis=0, concat_axis=0, tiled=True)
 
-    sent_kv = call(pack_kv_kernel, "pack_kv", struct(slots, width_kv), inputs=3)(row_group, keys, values)
+    sent_kv = call(pack_kv_kernel, "pack_kv", struct(slots, width_kv), inputs=3, vmem=60)(row_group, keys, values)
     home_kv = over_plane(sent_kv)
     all_kv = gather_column(home_kv)
-    sent_qg = call(pack_qg_kernel, "pack_qg", struct(slots, 2 * width_q), scalars=1, inputs=3)(
+    sent_qg = call(
+        pack_qg_kernel, "pack_qg", struct(slots, 2 * width_q), scalars=1, inputs=3, vmem=60
+    )(
         head_slot, row_group, queries, grad_out
     )
     home_qg = over_plane(sent_qg)
@@ -284,8 +308,11 @@
         attend_kernel,
         "attend",
         (*blocks, struct(slots, width_q)),
-        inputs=1 + len(all_kv),
+        inputs=0,
+        far=10,
+        vmem=40,
         scratch=[
+            pltpu.VMEM((slots, 2 * width_q), BF),
             pltpu.VMEM((all_keys, width_kv), BF),
             pltpu.VMEM((all_keys, slots), F32),
             pltpu.VMEM((all_keys, slots), F32),
@@ -294,13 +321,14 @@
             pltpu.VMEM((KVH, all_keys, HD), F32),
             pltpu.VMEM((KVH, all_keys, HD), F32),
             pltpu.VMEM((KVH, HD, all_keys), BF),
+            pltpu.SemaphoreType.DMA((10,)),
         ],
         cost=pl.CostEstimate(
             flops=10 * HD * pairs,
             bytes_accessed=2 * (3 * slots * width_q + 2 * all_keys * width_kv),
             transcendentals=pairs,
         ),
-    )(home_qg, *all_kv)
+    )(*all_kv, home_qg)
 
     kv_total = scatter_column(grad_kv)
     back_q = over_plane(grad_q)

time: 151 us -> 150 us (level)
  local copies, waits for them, and re-layouts: 2.79 us -> 8.45 us
  Pallas kernels: 39.1 us -> 34.5 us
  other arithmetic: 3.04 us -> 1.09 us
    unnamed x28, local copies, waits for them, and re-layouts: 2.77 us -> 8.43 us
    pallas_call x2, Pallas kernels: 31 us -> 28.1 us  [the longest x1 26.2 us: per_device(): call(attend_kernel, 'attend', (*blocks, struct(slots, width_q)), inputs=0...]
    convert_element_type x4, other arithmetic: 2.24 us -> 0.29 us  [plus(): return sum((term.astype(F32) for term in terms)).astype(BF)]
  transfers between devices with their start and end apart: 20 -> 20, of which waited for: 9 -> 9; matrix products, arithmetic and copies ran while one was open for 2% -> 1% of each run, Pallas kernels for 4% -> 4%
where the time goes in v5:
time: 150 us; the launch traced here: 149 us
  starting transfers between devices  57.6 us (38%)
  waiting for transfers between devices  47 us (31%)
  Pallas kernels  34.5 us (23%)
  local copies, waits for them, and re-layouts  8.45 us (6%)
    all_to_all x4, starting transfers between devices, over_plane(): return lax.all_to_all(array, PLANE, split_axis=0, concat_axis=0, tiled=True)  31.2 us
    ppermute x16, waiting for transfers between devices, step_by(): return lambda x: lax.ppermute(x, axis, pairs)  28.7 us
    ppermute x16, starting transfers between devices, step_by(): return lambda x: lax.ppermute(x, axis, pairs)  26.4 us
    pallas_call x1, Pallas kernels, per_device(): call(attend_kernel, 'attend', (*blocks, struct(slots, width_q)), inputs=0...  26.2 us
    all_to_all x4, waiting for transfers between devices, over_plane(): return lax.all_to_all(array, PLANE, split_axis=0, concat_axis=0, tiled=True)  18.4 us
    unnamed x28, local copies, waits for them, and re-layouts  8.43 us
    pallas_call x1, Pallas kernels, per_device(): call(pack_qg_kernel, 'pack_qg', struct(slots, 2 * width_q), scalars=1, in...  3.58 us
  transfers between devices with their start and end apart: 20, of which 9 were waited for; matrix products, arithmetic and copies ran while one was open for 1% of the time, Pallas kernels for 4%

profile of v5, /device:TPU:1, one launch (start us, length us, event | category | flops | bytes accessed | tf_op | source)
XLA Modules:
  0.0 149.4 jit_solution(13299039342758104859)
XLA Ops:
  0.6 1.9 %pack_kv.1 = bf16[256,512]{1,0:T(8,128)(2,1)} custom-call(s32[1,128]{1,0:T(1,128)} %bitcast.16, bf16[128,256]{1,0:T(8,128)(2,1)} %key_ref.1, bf16[128,256]{1,0:T(8,128)(2,1)} %value_ref.1), custom_call_target="tpu_custom_call" | custom-call | tf_op jit(solution)/shard_map/pack_kv/pallas_call | solution.py:295
  2.5 8.6 %all-to-all-start = ((bf16[32,8,512]{2,1,0:T(8,128)(2,1)}), bf16[32,8,512]{2,1,0:T(8,128)(2,1)S(1)}, u32[]{:S(2)}, u32[]{:S(2)}) async-start(bf16[32,8,512]{2,1,0:T(8,128)(2,1)} %bitcast.20), calls=%async_computation | async-start | bytes 524288 | tf_op jit(solution)/shard_map/all_to_all | solution.py:293
  11.1 3.6 %pack_qg.1 = bf16[256,4096]{1,0:T(8,128)(2,1)} custom-call(s32[16]{0:T(128)} %head_ref.3, s32[1,128]{1,0:T(1,128)} %bitcast.17, bf16[128,2048]{1,0:T(8,128)(2,1)} %query_ref.1, bf16[128,2048]{1,0:T(8,128)(2,1)} %grad_ref.1), custom_call_target="tpu_custom_call" | custom-call | tf_op jit(solution)/shard_map/pack_qg/pallas_call | solution.py:298
  14.7 5.3 %all-to-all-done = bf16[32,8,512]{2,1,0:T(8,128)(2,1)S(1)} async-done(((bf16[32,8,512]{2,1,0:T(8,128)(2,1)}), bf16[32,8,512]{2,1,0:T(8,128)(2,1)S(1)}, u32[]{:S(2)}, u32[]{:S(2)}) %all-to-all-start) | async-done | bytes 262176 | tf_op jit(solution)/shard_map/all_to_all | solution.py:293
  20.0 4.1 %all-to-all-start.1 = ((bf16[32,8,4096]{2,1,0:T(8,128)(2,1)}), bf16[32,8,4096]{2,1,0:T(8,128)(2,1)S(1)}, u32[]{:S(2)}, u32[]{:S(2)}) async-start(bf16[32,8,4096]{2,1,0:T(8,128)(2,1)} %bitcast.19), calls=%async_computation.1 | async-start | bytes 4194304 | tf_op jit(solution)/shard_map/all_to_all | solution.py:293
  24.2 5.7 %collective-permute-start.1 = (bf16[256,512]{1,0:T(8,128)(2,1)S(1)}, bf16[256,512]{1,0:T(8,128)(2,1)S(1)}, u32[]{:S(2)}, u32[]{:S(2)}) collective-permute-start(bf16[256,512]{1,0:T(8,128)(2,1)S(1)} %bitcast.13), channel_id=1, source_target_pairs={{0,196},{4,0},{64,4},{68,64},{128,68},{132,128},{192,132},{196,192... | collective-permute-start | bytes 786440 | tf_op jit(solution)/shard_map/ppermute | solution.py:226
  29.8 5.5 %collective-permute-done.1.refs_2_ = bf16[256,512]{1,0:T(8,128)(2,1)S(1)} collective-permute-done((bf16[256,512]{1,0:T(8,128)(2,1)S(1)}, bf16[256,512]{1,0:T(8,128)(2,1)S(1)}, u32[]{:S(2)}, u32[]{:S(2)}) %collective-permute-start.1) | collective-permute-done | bytes 262176 | tf_op jit(solution)/shard_map/ppermute | solution.py:226
  35.3 3.4 %collective-permute-start.3 = (bf16[256,512]{1,0:T(8,128)(2,1)S(1)}, bf16[256,512]{1,0:T(8,128)(2,1)S(1)}, u32[]{:S(2)}, u32[]{:S(2)}) collective-permute-start(bf16[256,512]{1,0:T(8,128)(2,1)S(1)} %collective-permute-done.1.refs_2_), channel_id=1, source_target_pairs={{0,196},{4,0},{64,4},{68,64},{128,68},{132,128},{192,132},{196,192... | collective-permute-start | bytes 786440 | tf_op jit(solution)/shard_map/ppermute | solution.py:226
  39.4 3.8 %collective-permute-done.3.refs_4_ = bf16[256,512]{1,0:T(8,128)(2,1)S(1)} collective-permute-done((bf16[256,512]{1,0:T(8,128)(2,1)S(1)}, bf16[256,512]{1,0:T(8,128)(2,1)S(1)}, u32[]{:S(2)}, u32[]{:S(2)}) %collective-permute-start.3) | collective-permute-done | bytes 262176 | tf_op jit(solution)/shard_map/ppermute | solution.py:226
  43.3 3.4 %collective-permute-start.5 = (bf16[256,512]{1,0:T(8,128)(2,1)S(1)}, bf16[256,512]{1,0:T(8,128)(2,1)S(1)}, u32[]{:S(2)}, u32[]{:S(2)}) collective-permute-start(bf16[256,512]{1,0:T(8,128)(2,1)S(1)} %collective-permute-done.3.refs_4_), channel_id=1, source_target_pairs={{0,196},{4,0},{64,4},{68,64},{128,68},{132,128},{192,132},{196,192... | collective-permute-start | bytes 786440 | tf_op jit(solution)/shard_map/ppermute | solution.py:226
  46.7 1.3 collective-permute-start.7
  48.0 1.4 collective-permute-start.6
  49.4 4.2 %collective-permute-done.7.refs_8_ = bf16[256,256]{1,0:T(8,128)(2,1)S(1)} collective-permute-done((bf16[256,256]{1,0:T(8,128)(2,1)S(1)}, bf16[256,256]{1,0:T(8,128)(2,1)S(1)}, u32[]{:S(2)}, u32[]{:S(2)}) %collective-permute-start.7) | collective-permute-done | bytes 131104 | tf_op jit(solution)/shard_map/ppermute | solution.py:226
  53.6 4.6 %collective-permute-done.6.refs_7_ = bf16[256,256]{1,0:T(8,128)(2,1)S(1)} collective-permute-done((bf16[256,256]{1,0:T(8,128)(2,1)S(1)}, bf16[256,256]{1,0:T(8,128)(2,1)S(1)}, u32[]{:S(2)}, u32[]{:S(2)}) %collective-permute-start.6) | collective-permute-done | bytes 131104 | tf_op jit(solution)/shard_map/ppermute | solution.py:226
  60.3 0.9 copy-done.1
  61.2 0.9 copy-done.5
  62.2 0.9 copy-done.7
  63.1 0.9 copy-done.9
  64.1 0.9 copy-done.11
  65.9 26.2 %attend.1 = (bf16[256,512]{1,0:T(8,128)(2,1)S(1)}, bf16[256,512]{1,0:T(8,128)(2,1)S(1)}, bf16[256,512]{1,0:T(8,128)(2,1)S(1)}, bf16[256,512]{1,0:T(8,128)(2,1)S(...) custom-call(bf16[256,512]{1,0:T(8,128)(2,1)S(1)} %bitcast.15, ...), custom_call_target="tpu_custom_call" | custom-call | flops 10737418240 | bytes 7340032 | tf_op jit(solution)/shard_map/attend/pallas_call | solution.py:307
  93.0 2.5 %collective-permute-start.12 = (bf16[256,512]{1,0:T(8,128)(2,1)S(1)}, bf16[256,512]{1,0:T(8,128)(2,1)S(1)}, u32[]{:S(2)}, u32[]{:S(2)}) collective-permute-start(bf16[256,512]{1,0:T(8,128)(2,1)S(1)} %get-tuple-element.27), channel_id=1, source_target_pairs={{0,196},{4,0},{64,4},{68,64},{128,68},{132,128},{192,132},{196,192... | collective-permute-start | bytes 786440 | tf_op jit(solution)/shard_map/ppermute | solution.py:226
  95.5 1.7 %collective-permute-start.13 = (bf16[256,256]{1,0:T(8,128)(2,1)S(1)}, bf16[256,256]{1,0:T(8,128)(2,1)S(1)}, u32[]{:S(2)}, u32[]{:S(2)}) collective-permute-start(bf16[256,256]{1,0:T(8,128)(2,1)S(1)} %get-tuple-element.28), channel_id=1, source_target_pairs={{0,192},{4,196},{64,0},{68,4},{128,64},{132,68},{192,128},{196,132... | collective-permute-start | bytes 393224 | tf_op jit(solution)/shard_map/ppermute | solution.py:226
  97.2 4.5 %collective-permute-done.9 = bf16[256,256]{1,0:T(8,128)(2,1)S(1)} collective-permute-done((bf16[256,256]{1,0:T(8,128)(2,1)S(1)}, bf16[256,256]{1,0:T(8,128)(2,1)S(1)}, u32[]{:S(2)}, u32[]{:S(2)}) %collective-permute-start.9) | collective-permute-done | bytes 131104 | tf_op jit(solution)/shard_map/ppermute | solution.py:226
  101.8 2.3 %collective-permute-start.10 = (bf16[256,512]{1,0:T(8,128)(2,1)S(1)}, bf16[256,512]{1,0:T(8,128)(2,1)S(1)}, u32[]{:S(2)}, u32[]{:S(2)}) collective-permute-start(bf16[256,512]{1,0:T(8,128)(2,1)S(1)} %add_convert_fusion.4), channel_id=1, source_target_pairs={{0,4},{4,64},{64,68},{68,128},{128,132},{132,192},{192,196},{196,0... | collective-permute-start | bytes 786440 | tf_op jit(solution)/shard_map/ppermute | solution.py:226
  104.2 1.0 collective-permute-start.14
  105.2 13.2 %all-to-all-start.2 = ((bf16[32,8,2048]{2,1,0:T(8,128)(2,1)}), bf16[32,8,2048]{2,1,0:T(8,128)(2,1)S(1)}, u32[]{:S(2)}, u32[]{:S(2)}) async-start(bf16[32,8,2048]{2,1,0:T(8,128)(2,1)} %bitcast.5), calls=%async_computation.2 | async-start | bytes 2097152 | tf_op jit(solution)/shard_map/all_to_all | solution.py:293
  118.8 2.6 %collective-permute-start.15 = (bf16[256,512]{1,0:T(8,128)(2,1)S(1)}, bf16[256,512]{1,0:T(8,128)(2,1)S(1)}, u32[]{:S(2)}, u32[]{:S(2)}) collective-permute-start(bf16[256,512]{1,0:T(8,128)(2,1)S(1)} %add_convert_fusion.1), channel_id=1, source_target_pairs={{0,196},{4,0},{64,4},{68,64},{128,68},{132,128},{192,132},{196,192... | collective-permute-start | bytes 786440 | tf_op jit(solution)/shard_map/ppermute | solution.py:226
  121.4 6.1 %collective-permute-done.11 = bf16[256,512]{1,0:T(8,128)(2,1)S(1)} collective-permute-done((bf16[256,512]{1,0:T(8,128)(2,1)S(1)}, bf16[256,512]{1,0:T(8,128)(2,1)S(1)}, u32[]{:S(2)}, u32[]{:S(2)}) %collective-permute-start.11) | collective-permute-done | bytes 262176 | tf_op jit(solution)/shard_map/ppermute | solution.py:226
  128.3 6.1 %all-to-all-done.2 = bf16[32,8,2048]{2,1,0:T(8,128)(2,1)S(1)} async-done(((bf16[32,8,2048]{2,1,0:T(8,128)(2,1)}), bf16[32,8,2048]{2,1,0:T(8,128)(2,1)S(1)}, u32[]{:S(2)}, u32[]{:S(2)}) %all-to-all-start.2) | async-done | bytes 1048608 | tf_op jit(solution)/shard_map/all_to_all | solution.py:293
  134.4 5.3 %all-to-all-start.3 = ((bf16[32,8,512]{2,1,0:T(8,128)(2,1)}), bf16[32,8,512]{2,1,0:T(8,128)(2,1)S(1)}, u32[]{:S(2)}, u32[]{:S(2)}) async-start(bf16[32,8,512]{2,1,0:T(8,128)(2,1)} %fusion), calls=%async_computation.3 | async-start | bytes 524288 | tf_op jit(solution)/shard_map/all_to_all | solution.py:293
  139.7 2.0 %unpack_q.1 = (bf16[128,2048]{1,0:T(8,128)(2,1)}, bf16[128,256]{1,0:T(8,128)(2,1)S(1)}) custom-call(s32[16]{0:T(128)S(1)} %copy-done.3, s32[1,128]{1,0:T(1,128)S(1)} %bitcast.18, bf16[256,2048]{1,0:T(8,128)(2,1)S(1)} %bitcast.10), custom_call_target="tpu_custom_call" | custom-call | tf_op jit(solution)/shard_map/unpack_q/pallas_call | solution.py:336
  141.7 6.9 %all-to-all-done.3 = bf16[32,8,512]{2,1,0:T(8,128)(2,1)S(1)} async-done(((bf16[32,8,512]{2,1,0:T(8,128)(2,1)}), bf16[32,8,512]{2,1,0:T(8,128)(2,1)S(1)}, u32[]{:S(2)}, u32[]{:S(2)}) %all-to-all-start.3) | async-done | bytes 262176 | tf_op jit(solution)/shard_map/all_to_all | solution.py:293
  (48 shorter events, 6.8 us)
Async XLA Ops:
  2.5 17.5 %all-to-all-start = ((bf16[32,8,512]{2,1,0:T(8,128)(2,1)}), bf16[32,8,512]{2,1,0:T(8,128)(2,1)S(1)}, u32[]{:S(2)}, u32[]{:S(2)}) async-start(bf16[32,8,512]{2,1,0:T(8,128)(2,1)} %bitcast.20), calls=%async_computation | async-start | bytes 524288 | tf_op jit(solution)/shard_map/all_to_all | solution.py:293
  20.0 40.2 %all-to-all-start.1 = ((bf16[32,8,4096]{2,1,0:T(8,128)(2,1)}), bf16[32,8,4096]{2,1,0:T(8,128)(2,1)S(1)}, u32[]{:S(2)}, u32[]{:S(2)}) async-start(bf16[32,8,4096]{2,1,0:T(8,128)(2,1)} %bitcast.19), calls=%async_computation.1 | async-start | bytes 4194304 | tf_op jit(solution)/shard_map/all_to_all | solution.py:293
  24.2 11.1 %collective-permute-start.1 = (bf16[256,512]{1,0:T(8,128)(2,1)S(1)}, bf16[256,512]{1,0:T(8,128)(2,1)S(1)}, u32[]{:S(2)}, u32[]{:S(2)}) collective-permute-start(bf16[256,512]{1,0:T(8,128)(2,1)S(1)} %bitcast.13), channel_id=1, source_target_pairs={{0,196},{4,0},{64,4},{68,64},{128,68},{132,128},{192,132},{196,192... | collective-permute-start | bytes 786440 | tf_op jit(solution)/shard_map/ppermute | solution.py:226
  29.8 8.9 %collective-permute-start = (bf16[256,512]{1,0:T(8,128)(2,1)S(1)}, bf16[256,512]{1,0:T(8,128)(2,1)S(1)}, u32[]{:S(2)}, u32[]{:S(2)}) collective-permute-start(bf16[256,512]{1,0:T(8,128)(2,1)S(1)} %bitcast.14), channel_id=1, source_target_pairs={{0,4},{4,64},{64,68},{68,128},{128,132},{132,192},{192,196},{196,0... | collective-permute-start | bytes 786440 | tf_op jit(solution)/shard_map/ppermute | solution.py:226
  35.3 25.0 %copy-start.4 = (bf16[256,512]{1,0:T(8,128)(2,1)}, bf16[256,512]{1,0:T(8,128)(2,1)S(1)}, u32[]{:S(2)}) copy-start(bf16[256,512]{1,0:T(8,128)(2,1)S(1)} %collective-permute-done.1.refs_2_) | copy-start | bytes 786436
  35.3 8.0 %collective-permute-start.3 = (bf16[256,512]{1,0:T(8,128)(2,1)S(1)}, bf16[256,512]{1,0:T(8,128)(2,1)S(1)}, u32[]{:S(2)}, u32[]{:S(2)}) collective-permute-start(bf16[256,512]{1,0:T(8,128)(2,1)S(1)} %collective-permute-done.1.refs_2_), channel_id=1, source_target_pairs={{0,196},{4,0},{64,4},{68,64},{128,68},{132,128},{192,132},{196,192... | collective-permute-start | bytes 786440 | tf_op jit(solution)/shard_map/ppermute | solution.py:226
  38.7 8.0 %collective-permute-start.2 = (bf16[256,512]{1,0:T(8,128)(2,1)S(1)}, bf16[256,512]{1,0:T(8,128)(2,1)S(1)}, u32[]{:S(2)}, u32[]{:S(2)}) collective-permute-start(bf16[256,512]{1,0:T(8,128)(2,1)S(1)} %collective-permute-done.refs_1_), channel_id=1, source_target_pairs={{0,4},{4,64},{64,68},{68,128},{128,132},{132,192},{192,196},{196,0... | collective-permute-start | bytes 786440 | tf_op jit(solution)/shard_map/ppermute | solution.py:226
  43.3 15.6 %collective-permute-start.5 = (bf16[256,512]{1,0:T(8,128)(2,1)S(1)}, bf16[256,512]{1,0:T(8,128)(2,1)S(1)}, u32[]{:S(2)}, u32[]{:S(2)}) collective-permute-start(bf16[256,512]{1,0:T(8,128)(2,1)S(1)} %collective-permute-done.3.refs_4_), channel_id=1, source_target_pairs={{0,196},{4,0},{64,4},{68,64},{128,68},{132,128},{192,132},{196,192... | collective-permute-start | bytes 786440 | tf_op jit(solution)/shard_map/ppermute | solution.py:226
  46.7 13.6 %copy-start = (bf16[256,512]{1,0:T(8,128)(2,1)}, bf16[256,512]{1,0:T(8,128)(2,1)S(1)}, u32[]{:S(2)}) copy-start(bf16[256,512]{1,0:T(8,128)(2,1)S(1)} %collective-permute-done.2.refs_3_) | copy-start | bytes 786436
  46.7 12.9 %collective-permute-start.4 = (bf16[256,512]{1,0:T(8,128)(2,1)S(1)}, bf16[256,512]{1,0:T(8,128)(2,1)S(1)}, u32[]{:S(2)}, u32[]{:S(2)}) collective-permute-start(bf16[256,512]{1,0:T(8,128)(2,1)S(1)} %collective-permute-done.2.refs_3_), channel_id=1, source_target_pairs={{0,4},{4,64},{64,68},{68,128},{128,132},{132,192},{192,196},{196,0... | collective-permute-start | bytes 786440 | tf_op jit(solution)/shard_map/ppermute | solution.py:226
  46.7 6.9 %collective-permute-start.7 = (bf16[256,256]{1,0:T(8,128)(2,1)S(1)}, bf16[256,256]{1,0:T(8,128)(2,1)S(1)}, u32[]{:S(2)}, u32[]{:S(2)}) collective-permute-start(bf16[256,256]{1,0:T(8,128)(2,1)S(1)} %slice.9), channel_id=1, source_target_pairs={{0,192},{4,196},{64,0},{68,4},{128,64},{132,68},{192,128},{196,132... | collective-permute-start | bytes 393224 | tf_op jit(solution)/shard_map/ppermute | solution.py:226
  48.0 10.2 %collective-permute-start.6 = (bf16[256,256]{1,0:T(8,128)(2,1)S(1)}, bf16[256,256]{1,0:T(8,128)(2,1)S(1)}, u32[]{:S(2)}, u32[]{:S(2)}) collective-permute-start(bf16[256,256]{1,0:T(8,128)(2,1)S(1)} %slice.8), channel_id=1, source_target_pairs={{0,64},{4,68},{64,128},{68,132},{128,192},{132,196},{192,0},{196,4... | collective-permute-start | bytes 393224 | tf_op jit(solution)/shard_map/ppermute | solution.py:226
  58.8 0.7 copy-start.8
  59.6 0.7 copy-start.10
  60.3 1.0 copy-start.1
  61.2 0.9 copy-start.5
  62.2 0.9 copy-start.7
  63.1 0.9 copy-start.9
  64.1 0.9 copy-start.11
  65.0 0.9 copy-start.13
  92.1 9.6 %collective-permute-start.8 = (bf16[256,512]{1,0:T(8,128)(2,1)S(1)}, bf16[256,512]{1,0:T(8,128)(2,1)S(1)}, u32[]{:S(2)}, u32[]{:S(2)}) collective-permute-start(bf16[256,512]{1,0:T(8,128)(2,1)S(1)} %get-tuple-element.23), channel_id=1, source_target_pairs={{0,4},{4,64},{64,68},{68,128},{128,132},{132,192},{192,196},{196,0... | collective-permute-start | bytes 786440 | tf_op jit(solution)/shard_map/ppermute | solution.py:226
  93.0 8.7 %collective-permute-start.9 = (bf16[256,256]{1,0:T(8,128)(2,1)S(1)}, bf16[256,256]{1,0:T(8,128)(2,1)S(1)}, u32[]{:S(2)}, u32[]{:S(2)}) collective-permute-start(bf16[256,256]{1,0:T(8,128)(2,1)S(1)} %get-tuple-element.24), channel_id=1, source_target_pairs={{0,64},{4,68},{64,128},{68,132},{128,192},{132,196},{192,0},{196,4... | collective-permute-start | bytes 393224 | tf_op jit(solution)/shard_map/ppermute | solution.py:226
  93.0 11.1 %collective-permute-start.12 = (bf16[256,512]{1,0:T(8,128)(2,1)S(1)}, bf16[256,512]{1,0:T(8,128)(2,1)S(1)}, u32[]{:S(2)}, u32[]{:S(2)}) collective-permute-start(bf16[256,512]{1,0:T(8,128)(2,1)S(1)} %get-tuple-element.27), channel_id=1, source_target_pairs={{0,196},{4,0},{64,4},{68,64},{128,68},{132,128},{192,132},{196,192... | collective-permute-start | bytes 786440 | tf_op jit(solution)/shard_map/ppermute | solution.py:226
  95.5 8.6 %collective-permute-start.13 = (bf16[256,256]{1,0:T(8,128)(2,1)S(1)}, bf16[256,256]{1,0:T(8,128)(2,1)S(1)}, u32[]{:S(2)}, u32[]{:S(2)}) collective-permute-start(bf16[256,256]{1,0:T(8,128)(2,1)S(1)} %get-tuple-element.28), channel_id=1, source_target_pairs={{0,192},{4,196},{64,0},{68,4},{128,64},{132,68},{192,128},{196,132... | collective-permute-start | bytes 393224 | tf_op jit(solution)/shard_map/ppermute | solution.py:226
  101.8 16.6 %collective-permute-start.10 = (bf16[256,512]{1,0:T(8,128)(2,1)S(1)}, bf16[256,512]{1,0:T(8,128)(2,1)S(1)}, u32[]{:S(2)}, u32[]{:S(2)}) collective-permute-start(bf16[256,512]{1,0:T(8,128)(2,1)S(1)} %add_convert_fusion.4), channel_id=1, source_target_pairs={{0,4},{4,64},{64,68},{68,128},{128,132},{132,192},{192,196},{196,0... | collective-permute-start | bytes 786440 | tf_op jit(solution)/shard_map/ppermute | solution.py:226
  104.2 14.5 %collective-permute-start.14 = (bf16[256,512]{1,0:T(8,128)(2,1)S(1)}, bf16[256,512]{1,0:T(8,128)(2,1)S(1)}, u32[]{:S(2)}, u32[]{:S(2)}) collective-permute-start(bf16[256,512]{1,0:T(8,128)(2,1)S(1)} %add_convert_fusion.2), channel_id=1, source_target_pairs={{0,196},{4,0},{64,4},{68,64},{128,68},{132,128},{192,132},{196,192... | collective-permute-start | bytes 786440 | tf_op jit(solution)/shard_map/ppermute | solution.py:226
  105.2 29.2 %all-to-all-start.2 = ((bf16[32,8,2048]{2,1,0:T(8,128)(2,1)}), bf16[32,8,2048]{2,1,0:T(8,128)(2,1)S(1)}, u32[]{:S(2)}, u32[]{:S(2)}) async-start(bf16[32,8,2048]{2,1,0:T(8,128)(2,1)} %bitcast.5), calls=%async_computation.2 | async-start | bytes 2097152 | tf_op jit(solution)/shard_map/all_to_all | solution.py:293
  118.4 21.3 %copy-start.2 = (s32[128,1]{0,1:T(1,128)S(1)}, s32[128,1]{0,1:T(1,128)}, u32[]{:S(2)}) copy-start(s32[128,1]{0,1:T(1,128)} %param.10) | copy-start | bytes 1540
  118.4 21.3 %copy-start.3 = (s32[16]{0:T(128)S(1)}, s32[16]{0:T(128)}, u32[]{:S(2)}) copy-start(s32[16]{0:T(128)} %head_ref.3) | copy-start | bytes 196
  118.5 9.0 %collective-permute-start.11 = (bf16[256,512]{1,0:T(8,128)(2,1)S(1)}, bf16[256,512]{1,0:T(8,128)(2,1)S(1)}, u32[]{:S(2)}, u32[]{:S(2)}) collective-permute-start(bf16[256,512]{1,0:T(8,128)(2,1)S(1)} %add_convert_fusion.3), channel_id=1, source_target_pairs={{0,4},{4,64},{64,68},{68,128},{128,132},{132,192},{192,196},{196,0... | collective-permute-start | bytes 786440 | tf_op jit(solution)/shard_map/ppermute | solution.py:226
  118.8 8.7 %collective-permute-start.15 = (bf16[256,512]{1,0:T(8,128)(2,1)S(1)}, bf16[256,512]{1,0:T(8,128)(2,1)S(1)}, u32[]{:S(2)}, u32[]{:S(2)}) collective-permute-start(bf16[256,512]{1,0:T(8,128)(2,1)S(1)} %add_convert_fusion.1), channel_id=1, source_target_pairs={{0,196},{4,0},{64,4},{68,64},{128,68},{132,128},{192,132},{196,192... | collective-permute-start | bytes 786440 | tf_op jit(solution)/shard_map/ppermute | solution.py:226
  134.4 14.2 %all-to-all-start.3 = ((bf16[32,8,512]{2,1,0:T(8,128)(2,1)}), bf16[32,8,512]{2,1,0:T(8,128)(2,1)S(1)}, u32[]{:S(2)}, u32[]{:S(2)}) async-start(bf16[32,8,512]{2,1,0:T(8,128)(2,1)} %fusion), calls=%async_computation.3 | async-start | bytes 524288 | tf_op jit(solution)/shard_map/all_to_all | solution.py:293
  (2 other events, 1.3 us)

commit v6 on v5

--- a/solution.py
+++ b/solution.py
@@ -310,7 +310,7 @@
         (*blocks, struct(slots, width_q)),
         inputs=0,
         far=10,
-        vmem=40,
+        vmem=60,
         scratch=[
             pltpu.VMEM((slots, 2 * width_q), BF),
             pltpu.VMEM((all_keys, width_kv), BF),

time: 150 us -> 148 us (0.987)
  local copies, waits for them, and re-layouts: 8.45 us -> 2.09 us
  other arithmetic: 1.09 us -> 3.06 us
  Pallas kernels: 34.5 us -> 36.1 us
    unnamed x28, local copies, waits for them, and re-layouts: 8.43 us -> 2.07 us
    convert_element_type x4, other arithmetic: 0.29 us -> 2.25 us  [plus(): return sum((term.astype(F32) for term in terms)).astype(BF)]
    pallas_call x1, Pallas kernels: 26.2 us -> 27.8 us  [per_device(): call(attend_kernel, 'attend', (*blocks, struct(slots, width_q)), inputs=0...]
  transfers between devices with their start and end apart: 20 -> 20, of which waited for: 9 -> 9; matrix products, arithmetic and copies ran while one was open for 1% -> 2% of each run, Pallas kernels for 4% -> 4%
where the time goes in v6:
time: 148 us; the launch traced here: 147 us
  starting transfers between devices  57.2 us (39%)
  waiting for transfers between devices  48 us (32%)
  Pallas kernels  36.1 us (24%)
  other arithmetic  3.06 us (2%)
  local copies, waits for them, and re-layouts  2.09 us (1%)
    all_to_all x4, starting transfers between devices, over_plane(): return lax.all_to_all(array, PLANE, split_axis=0, concat_axis=0, tiled=True)  31.3 us
    ppermute x16, waiting for transfers between devices, step_by(): return lambda x: lax.ppermute(x, axis, pairs)  29.7 us
    pallas_call x1, Pallas kernels, per_device(): call(attend_kernel, 'attend', (*blocks, struct(slots, width_q)), inputs=0...  27.8 us
    ppermute x16, starting transfers between devices, step_by(): return lambda x: lax.ppermute(x, axis, pairs)  25.9 us
    all_to_all x4, waiting for transfers between devices, over_plane(): return lax.all_to_all(array, PLANE, split_axis=0, concat_axis=0, tiled=True)  18.3 us
    pallas_call x1, Pallas kernels, per_device(): call(pack_qg_kernel, 'pack_qg', struct(slots, 2 * width_q), scalars=1, in...  3.59 us
  transfers between devices with their start and end apart: 20, of which 9 were waited for; matrix products, arithmetic and copies ran while one was open for 2% of the time, Pallas kernels for 4%

profile of v6, /device:TPU:1, one launch (start us, length us, event | category | flops | bytes accessed | tf_op | source)
XLA Modules:
  0.0 147.3 jit_solution(15900521971277138703)
XLA Ops:
  0.6 1.9 %pack_kv.1 = bf16[256,512]{1,0:T(8,128)(2,1)} custom-call(s32[1,128]{1,0:T(1,128)} %bitcast.12, bf16[128,256]{1,0:T(8,128)(2,1)} %key_ref.1, bf16[128,256]{1,0:T(8,128)(2,1)} %value_ref.1), custom_call_target="tpu_custom_call" | custom-call | tf_op jit(solution)/shard_map/pack_kv/pallas_call | solution.py:295
  2.5 8.6 %all-to-all-start = ((bf16[32,8,512]{2,1,0:T(8,128)(2,1)}), bf16[32,8,512]{2,1,0:T(8,128)(2,1)S(1)}, u32[]{:S(2)}, u32[]{:S(2)}) async-start(bf16[32,8,512]{2,1,0:T(8,128)(2,1)} %bitcast.18), calls=%async_computation | async-start | bytes 524288 | tf_op jit(solution)/shard_map/all_to_all | solution.py:293
  11.1 3.6 %pack_qg.1 = bf16[256,4096]{1,0:T(8,128)(2,1)} custom-call(s32[16]{0:T(128)} %head_ref.3, s32[1,128]{1,0:T(1,128)} %bitcast.13, bf16[128,2048]{1,0:T(8,128)(2,1)} %query_ref.1, bf16[128,2048]{1,0:T(8,128)(2,1)} %grad_ref.1), custom_call_target="tpu_custom_call" | custom-call | tf_op jit(solution)/shard_map/pack_qg/pallas_call | solution.py:298
  14.7 5.3 %all-to-all-done = bf16[32,8,512]{2,1,0:T(8,128)(2,1)S(1)} async-done(((bf16[32,8,512]{2,1,0:T(8,128)(2,1)}), bf16[32,8,512]{2,1,0:T(8,128)(2,1)S(1)}, u32[]{:S(2)}, u32[]{:S(2)}) %all-to-all-start) | async-done | bytes 262176 | tf_op jit(solution)/shard_map/all_to_all | solution.py:293
  20.0 4.1 %all-to-all-start.1 = ((bf16[32,8,4096]{2,1,0:T(8,128)(2,1)}), bf16[32,8,4096]{2,1,0:T(8,128)(2,1)S(1)}, u32[]{:S(2)}, u32[]{:S(2)}) async-start(bf16[32,8,4096]{2,1,0:T(8,128)(2,1)} %bitcast.15), calls=%async_computation.1 | async-start | bytes 4194304 | tf_op jit(solution)/shard_map/all_to_all | solution.py:293
  24.2 5.7 %collective-permute-start.1 = (bf16[256,512]{1,0:T(8,128)(2,1)S(1)}, bf16[256,512]{1,0:T(8,128)(2,1)S(1)}, u32[]{:S(2)}, u32[]{:S(2)}) collective-permute-start(bf16[256,512]{1,0:T(8,128)(2,1)S(1)} %bitcast.19), channel_id=1, source_target_pairs={{0,196},{4,0},{64,4},{68,64},{128,68},{132,128},{192,132},{196,192... | collective-permute-start | bytes 786440 | tf_op jit(solution)/shard_map/ppermute | solution.py:226
  29.8 5.5 %collective-permute-done.1.refs_2_ = bf16[256,512]{1,0:T(8,128)(2,1)S(1)} collective-permute-done((bf16[256,512]{1,0:T(8,128)(2,1)S(1)}, bf16[256,512]{1,0:T(8,128)(2,1)S(1)}, u32[]{:S(2)}, u32[]{:S(2)}) %collective-permute-start.1) | collective-permute-done | bytes 262176 | tf_op jit(solution)/shard_map/ppermute | solution.py:226
  35.3 3.4 %collective-permute-start.3 = (bf16[256,512]{1,0:T(8,128)(2,1)S(1)}, bf16[256,512]{1,0:T(8,128)(2,1)S(1)}, u32[]{:S(2)}, u32[]{:S(2)}) collective-permute-start(bf16[256,512]{1,0:T(8,128)(2,1)S(1)} %collective-permute-done.1.refs_2_), channel_id=1, source_target_pairs={{0,196},{4,0},{64,4},{68,64},{128,68},{132,128},{192,132},{196,192... | collective-permute-start | bytes 786440 | tf_op jit(solution)/shard_map/ppermute | solution.py:226
  38.7 4.5 %collective-permute-done.3.refs_4_ = bf16[256,512]{1,0:T(8,128)(2,1)S(1)} collective-permute-done((bf16[256,512]{1,0:T(8,128)(2,1)S(1)}, bf16[256,512]{1,0:T(8,128)(2,1)S(1)}, u32[]{:S(2)}, u32[]{:S(2)}) %collective-permute-start.3) | collective-permute-done | bytes 262176 | tf_op jit(solution)/shard_map/ppermute | solution.py:226
  43.3 3.4 %collective-permute-start.5 = (bf16[256,512]{1,0:T(8,128)(2,1)S(1)}, bf16[256,512]{1,0:T(8,128)(2,1)S(1)}, u32[]{:S(2)}, u32[]{:S(2)}) collective-permute-start(bf16[256,512]{1,0:T(8,128)(2,1)S(1)} %collective-permute-done.3.refs_4_), channel_id=1, source_target_pairs={{0,196},{4,0},{64,4},{68,64},{128,68},{132,128},{192,132},{196,192... | collective-permute-start | bytes 786440 | tf_op jit(solution)/shard_map/ppermute | solution.py:226
  46.7 1.3 collective-permute-start.7
  48.0 1.4 collective-permute-start.6
  49.4 4.3 %collective-permute-done.7.refs_8_ = bf16[256,256]{1,0:T(8,128)(2,1)S(1)} collective-permute-done((bf16[256,256]{1,0:T(8,128)(2,1)S(1)}, bf16[256,256]{1,0:T(8,128)(2,1)S(1)}, u32[]{:S(2)}, u32[]{:S(2)}) %collective-permute-start.7) | collective-permute-done | bytes 131104 | tf_op jit(solution)/shard_map/ppermute | solution.py:226
  53.7 4.5 %collective-permute-done.6.refs_7_ = bf16[256,256]{1,0:T(8,128)(2,1)S(1)} collective-permute-done((bf16[256,256]{1,0:T(8,128)(2,1)S(1)}, bf16[256,256]{1,0:T(8,128)(2,1)S(1)}, u32[]{:S(2)}, u32[]{:S(2)}) %collective-permute-start.6) | collective-permute-done | bytes 131104 | tf_op jit(solution)/shard_map/ppermute | solution.py:226
  59.5 0.7 copy-done.2
  60.3 27.8 %attend.1 = (bf16[256,512]{1,0:T(8,128)(2,1)}, bf16[256,512]{1,0:T(8,128)(2,1)}, bf16[256,512]{1,0:T(8,128)(2,1)}, bf16[256,512]{1,0:T(8,128)(2,1)}, bf16[256,51...) custom-call(bf16[256,512]{1,0:T(8,128)(2,1)} %bitcast.21, ...), custom_call_target="tpu_custom_call" | custom-call | flops 10737418240 | bytes 7340032 | tf_op jit(solution)/shard_map/attend/pallas_call | solution.py:307
  88.1 0.9 collective-permute-start.8
  89.0 2.5 %collective-permute-start.12 = (bf16[256,512]{1,0:T(8,128)(2,1)}, bf16[256,512]{1,0:T(8,128)(2,1)S(1)}, u32[]{:S(2)}, u32[]{:S(2)}) collective-permute-start(bf16[256,512]{1,0:T(8,128)(2,1)} %get-tuple-element.27), channel_id=1, source_target_pairs={{0,196},{4,0},{64,4},{68,64},{128,68},{132,128},{192,132},{196,192... | collective-permute-start | bytes 786440 | tf_op jit(solution)/shard_map/ppermute | solution.py:226
  91.5 1.7 %collective-permute-start.13 = (bf16[256,256]{1,0:T(8,128)(2,1)}, bf16[256,256]{1,0:T(8,128)(2,1)S(1)}, u32[]{:S(2)}, u32[]{:S(2)}) collective-permute-start(bf16[256,256]{1,0:T(8,128)(2,1)} %get-tuple-element.28), channel_id=1, source_target_pairs={{0,192},{4,196},{64,0},{68,4},{128,64},{132,68},{192,128},{196,132... | collective-permute-start | bytes 393224 | tf_op jit(solution)/shard_map/ppermute | solution.py:226
  93.2 4.8 %collective-permute-done.9 = bf16[256,256]{1,0:T(8,128)(2,1)S(1)} collective-permute-done((bf16[256,256]{1,0:T(8,128)(2,1)}, bf16[256,256]{1,0:T(8,128)(2,1)S(1)}, u32[]{:S(2)}, u32[]{:S(2)}) %collective-permute-start.9) | collective-permute-done | bytes 131104 | tf_op jit(solution)/shard_map/ppermute | solution.py:226
  98.0 1.0 add_convert_fusion.4
  99.1 2.2 %collective-permute-start.10 = (bf16[256,512]{1,0:T(8,128)(2,1)S(1)}, bf16[256,512]{1,0:T(8,128)(2,1)S(1)}, u32[]{:S(2)}, u32[]{:S(2)}) collective-permute-start(bf16[256,512]{1,0:T(8,128)(2,1)S(1)} %add_convert_fusion.4), channel_id=1, source_target_pairs={{0,4},{4,64},{64,68},{68,128},{128,132},{132,192},{192,196},{196,0... | collective-permute-start | bytes 786440 | tf_op jit(solution)/shard_map/ppermute | solution.py:226
  101.2 1.1 add_convert_fusion.2
  103.0 13.3 %all-to-all-start.2 = ((bf16[32,8,2048]{2,1,0:T(8,128)(2,1)}), bf16[32,8,2048]{2,1,0:T(8,128)(2,1)S(1)}, u32[]{:S(2)}, u32[]{:S(2)}) async-start(bf16[32,8,2048]{2,1,0:T(8,128)(2,1)} %bitcast.17), calls=%async_computation.2 | async-start | bytes 2097152 | tf_op jit(solution)/shard_map/all_to_all | solution.py:293
  116.6 2.7 %collective-permute-start.15 = (bf16[256,512]{1,0:T(8,128)(2,1)S(1)}, bf16[256,512]{1,0:T(8,128)(2,1)S(1)}, u32[]{:S(2)}, u32[]{:S(2)}) collective-permute-start(bf16[256,512]{1,0:T(8,128)(2,1)S(1)} %add_convert_fusion.1), channel_id=1, source_target_pairs={{0,196},{4,0},{64,4},{68,64},{128,68},{132,128},{192,132},{196,192... | collective-permute-start | bytes 786440 | tf_op jit(solution)/shard_map/ppermute | solution.py:226
  119.3 6.1 %collective-permute-done.11 = bf16[256,512]{1,0:T(8,128)(2,1)S(1)} collective-permute-done((bf16[256,512]{1,0:T(8,128)(2,1)S(1)}, bf16[256,512]{1,0:T(8,128)(2,1)S(1)}, u32[]{:S(2)}, u32[]{:S(2)}) %collective-permute-start.11) | collective-permute-done | bytes 262176 | tf_op jit(solution)/shard_map/ppermute | solution.py:226
  125.4 0.8 fusion
  126.2 6.1 %all-to-all-done.2 = bf16[32,8,2048]{2,1,0:T(8,128)(2,1)S(1)} async-done(((bf16[32,8,2048]{2,1,0:T(8,128)(2,1)}), bf16[32,8,2048]{2,1,0:T(8,128)(2,1)S(1)}, u32[]{:S(2)}, u32[]{:S(2)}) %all-to-all-start.2) | async-done | bytes 1048608 | tf_op jit(solution)/shard_map/all_to_all | solution.py:293
  132.3 5.3 %all-to-all-start.3 = ((bf16[32,8,512]{2,1,0:T(8,128)(2,1)}), bf16[32,8,512]{2,1,0:T(8,128)(2,1)S(1)}, u32[]{:S(2)}, u32[]{:S(2)}) async-start(bf16[32,8,512]{2,1,0:T(8,128)(2,1)} %fusion), calls=%async_computation.3 | async-start | bytes 524288 | tf_op jit(solution)/shard_map/all_to_all | solution.py:293
  137.6 2.0 %unpack_q.1 = (bf16[128,2048]{1,0:T(8,128)(2,1)}, bf16[128,256]{1,0:T(8,128)(2,1)S(1)}) custom-call(s32[16]{0:T(128)S(1)} %copy-done.1, s32[1,128]{1,0:T(1,128)S(1)} %bitcast.14, bf16[256,2048]{1,0:T(8,128)(2,1)S(1)} %bitcast.10), custom_call_target="tpu_custom_call" | custom-call | tf_op jit(solution)/shard_map/unpack_q/pallas_call | solution.py:336
  139.6 6.9 %all-to-all-done.3 = bf16[32,8,512]{2,1,0:T(8,128)(2,1)S(1)} async-done(((bf16[32,8,512]{2,1,0:T(8,128)(2,1)}), bf16[32,8,512]{2,1,0:T(8,128)(2,1)S(1)}, u32[]{:S(2)}, u32[]{:S(2)}) %all-to-all-start.3) | async-done | bytes 262176 | tf_op jit(solution)/shard_map/all_to_all | solution.py:293
  146.5 0.8 unpack_kv.1
  (48 shorter events, 2.3 us)
Async XLA Ops:
  2.5 17.5 %all-to-all-start = ((bf16[32,8,512]{2,1,0:T(8,128)(2,1)}), bf16[32,8,512]{2,1,0:T(8,128)(2,1)S(1)}, u32[]{:S(2)}, u32[]{:S(2)}) async-start(bf16[32,8,512]{2,1,0:T(8,128)(2,1)} %bitcast.18), calls=%async_computation | async-start | bytes 524288 | tf_op jit(solution)/shard_map/all_to_all | solution.py:293
  20.0 9.8 %copy-start.5 = (bf16[32,8,512]{2,1,0:T(8,128)(2,1)}, bf16[32,8,512]{2,1,0:T(8,128)(2,1)S(1)}, u32[]{:S(2)}) copy-start(bf16[32,8,512]{2,1,0:T(8,128)(2,1)S(1)} %all-to-all-done) | copy-start | bytes 786436
  20.0 38.8 %all-to-all-start.1 = ((bf16[32,8,4096]{2,1,0:T(8,128)(2,1)}), bf16[32,8,4096]{2,1,0:T(8,128)(2,1)S(1)}, u32[]{:S(2)}, u32[]{:S(2)}) async-start(bf16[32,8,4096]{2,1,0:T(8,128)(2,1)} %bitcast.15), calls=%async_computation.1 | async-start | bytes 4194304 | tf_op jit(solution)/shard_map/all_to_all | solution.py:293
  24.2 11.1 %collective-permute-start.1 = (bf16[256,512]{1,0:T(8,128)(2,1)S(1)}, bf16[256,512]{1,0:T(8,128)(2,1)S(1)}, u32[]{:S(2)}, u32[]{:S(2)}) collective-permute-start(bf16[256,512]{1,0:T(8,128)(2,1)S(1)} %bitcast.19), channel_id=1, source_target_pairs={{0,196},{4,0},{64,4},{68,64},{128,68},{132,128},{192,132},{196,192... | collective-permute-start | bytes 786440 | tf_op jit(solution)/shard_map/ppermute | solution.py:226
  29.8 8.9 %collective-permute-start = (bf16[256,512]{1,0:T(8,128)(2,1)S(1)}, bf16[256,512]{1,0:T(8,128)(2,1)S(1)}, u32[]{:S(2)}, u32[]{:S(2)}) collective-permute-start(bf16[256,512]{1,0:T(8,128)(2,1)S(1)} %bitcast.20), channel_id=1, source_target_pairs={{0,4},{4,64},{64,68},{68,128},{128,132},{132,192},{192,196},{196,0... | collective-permute-start | bytes 786440 | tf_op jit(solution)/shard_map/ppermute | solution.py:226
  35.3 23.6 %copy-start.9 = (bf16[256,512]{1,0:T(8,128)(2,1)}, bf16[256,512]{1,0:T(8,128)(2,1)S(1)}, u32[]{:S(2)}) copy-start(bf16[256,512]{1,0:T(8,128)(2,1)S(1)} %collective-permute-done.1.refs_2_) | copy-start | bytes 786436
  35.3 8.0 %collective-permute-start.3 = (bf16[256,512]{1,0:T(8,128)(2,1)S(1)}, bf16[256,512]{1,0:T(8,128)(2,1)S(1)}, u32[]{:S(2)}, u32[]{:S(2)}) collective-permute-start(bf16[256,512]{1,0:T(8,128)(2,1)S(1)} %collective-permute-done.1.refs_2_), channel_id=1, source_target_pairs={{0,196},{4,0},{64,4},{68,64},{128,68},{132,128},{192,132},{196,192... | collective-permute-start | bytes 786440 | tf_op jit(solution)/shard_map/ppermute | solution.py:226
  38.7 20.2 %copy-start.10 = (bf16[256,512]{1,0:T(8,128)(2,1)}, bf16[256,512]{1,0:T(8,128)(2,1)S(1)}, u32[]{:S(2)}) copy-start(bf16[256,512]{1,0:T(8,128)(2,1)S(1)} %collective-permute-done.refs_1_) | copy-start | bytes 786436
  38.7 8.0 %collective-permute-start.2 = (bf16[256,512]{1,0:T(8,128)(2,1)S(1)}, bf16[256,512]{1,0:T(8,128)(2,1)S(1)}, u32[]{:S(2)}, u32[]{:S(2)}) collective-permute-start(bf16[256,512]{1,0:T(8,128)(2,1)S(1)} %collective-permute-done.refs_1_), channel_id=1, source_target_pairs={{0,4},{4,64},{64,68},{68,128},{128,132},{132,192},{192,196},{196,0... | collective-permute-start | bytes 786440 | tf_op jit(solution)/shard_map/ppermute | solution.py:226
  43.3 15.6 %copy-start.7 = (bf16[256,512]{1,0:T(8,128)(2,1)}, bf16[256,512]{1,0:T(8,128)(2,1)S(1)}, u32[]{:S(2)}) copy-start(bf16[256,512]{1,0:T(8,128)(2,1)S(1)} %collective-permute-done.3.refs_4_) | copy-start | bytes 786436
  43.3 14.9 %collective-permute-start.5 = (bf16[256,512]{1,0:T(8,128)(2,1)S(1)}, bf16[256,512]{1,0:T(8,128)(2,1)S(1)}, u32[]{:S(2)}, u32[]{:S(2)}) collective-permute-start(bf16[256,512]{1,0:T(8,128)(2,1)S(1)} %collective-permute-done.3.refs_4_), channel_id=1, source_target_pairs={{0,196},{4,0},{64,4},{68,64},{128,68},{132,128},{192,132},{196,192... | collective-permute-start | bytes 786440 | tf_op jit(solution)/shard_map/ppermute | solution.py:226
  46.7 12.2 %copy-start.8 = (bf16[256,512]{1,0:T(8,128)(2,1)}, bf16[256,512]{1,0:T(8,128)(2,1)S(1)}, u32[]{:S(2)}) copy-start(bf16[256,512]{1,0:T(8,128)(2,1)S(1)} %collective-permute-done.2.refs_3_) | copy-start | bytes 786436
  46.7 12.2 %collective-permute-start.4 = (bf16[256,512]{1,0:T(8,128)(2,1)S(1)}, bf16[256,512]{1,0:T(8,128)(2,1)}, u32[]{:S(2)}, u32[]{:S(2)}) collective-permute-start(bf16[256,512]{1,0:T(8,128)(2,1)S(1)} %collective-permute-done.2.refs_3_), channel_id=1, source_target_pairs={{0,4},{4,64},{64,68},{68,128},{128,132},{132,192},{192,196},{196,0... | collective-permute-start | bytes 786440 | tf_op jit(solution)/shard_map/ppermute | solution.py:226
  46.7 7.0 %collective-permute-start.7 = (bf16[256,256]{1,0:T(8,128)(2,1)S(1)}, bf16[256,256]{1,0:T(8,128)(2,1)S(1)}, u32[]{:S(2)}, u32[]{:S(2)}) collective-permute-start(bf16[256,256]{1,0:T(8,128)(2,1)S(1)} %slice.9), channel_id=1, source_target_pairs={{0,192},{4,196},{64,0},{68,4},{128,64},{132,68},{192,128},{196,132... | collective-permute-start | bytes 393224 | tf_op jit(solution)/shard_map/ppermute | solution.py:226
  48.0 10.1 %collective-permute-start.6 = (bf16[256,256]{1,0:T(8,128)(2,1)S(1)}, bf16[256,256]{1,0:T(8,128)(2,1)S(1)}, u32[]{:S(2)}, u32[]{:S(2)}) collective-permute-start(bf16[256,256]{1,0:T(8,128)(2,1)S(1)} %slice.8), channel_id=1, source_target_pairs={{0,64},{4,68},{64,128},{68,132},{128,192},{132,196},{192,0},{196,4... | collective-permute-start | bytes 393224 | tf_op jit(solution)/shard_map/ppermute | solution.py:226
  53.7 5.2 %copy-start.12 = (bf16[256,256]{1,0:T(8,128)(2,1)}, bf16[256,256]{1,0:T(8,128)(2,1)S(1)}, u32[]{:S(2)}) copy-start(bf16[256,256]{1,0:T(8,128)(2,1)S(1)} %collective-permute-done.7.refs_8_) | copy-start | bytes 393220
  58.9 1.4 copy-start.2
  88.1 28.3 %copy-start.4 = (bf16[256,512]{1,0:T(8,128)(2,1)S(1)}, bf16[256,512]{1,0:T(8,128)(2,1)}, u32[]{:S(2)}) copy-start(bf16[256,512]{1,0:T(8,128)(2,1)} %get-tuple-element.21) | copy-start | bytes 786436
  88.1 9.9 %collective-permute-start.8 = (bf16[256,512]{1,0:T(8,128)(2,1)}, bf16[256,512]{1,0:T(8,128)(2,1)S(1)}, u32[]{:S(2)}, u32[]{:S(2)}) collective-permute-start(bf16[256,512]{1,0:T(8,128)(2,1)} %get-tuple-element.23), channel_id=1, source_target_pairs={{0,4},{4,64},{64,68},{68,128},{128,132},{132,192},{192,196},{196,0... | collective-permute-start | bytes 786440 | tf_op jit(solution)/shard_map/ppermute | solution.py:226
  89.0 9.0 %collective-permute-start.9 = (bf16[256,256]{1,0:T(8,128)(2,1)}, bf16[256,256]{1,0:T(8,128)(2,1)S(1)}, u32[]{:S(2)}, u32[]{:S(2)}) collective-permute-start(bf16[256,256]{1,0:T(8,128)(2,1)} %get-tuple-element.24), channel_id=1, source_target_pairs={{0,64},{4,68},{64,128},{68,132},{128,192},{132,196},{192,0},{196,4... | collective-permute-start | bytes 393224 | tf_op jit(solution)/shard_map/ppermute | solution.py:226
  89.0 12.2 %collective-permute-start.12 = (bf16[256,512]{1,0:T(8,128)(2,1)}, bf16[256,512]{1,0:T(8,128)(2,1)S(1)}, u32[]{:S(2)}, u32[]{:S(2)}) collective-permute-start(bf16[256,512]{1,0:T(8,128)(2,1)} %get-tuple-element.27), channel_id=1, source_target_pairs={{0,196},{4,0},{64,4},{68,64},{128,68},{132,128},{192,132},{196,192... | collective-permute-start | bytes 786440 | tf_op jit(solution)/shard_map/ppermute | solution.py:226
  91.5 9.7 %collective-permute-start.13 = (bf16[256,256]{1,0:T(8,128)(2,1)}, bf16[256,256]{1,0:T(8,128)(2,1)S(1)}, u32[]{:S(2)}, u32[]{:S(2)}) collective-permute-start(bf16[256,256]{1,0:T(8,128)(2,1)} %get-tuple-element.28), channel_id=1, source_target_pairs={{0,192},{4,196},{64,0},{68,4},{128,64},{132,68},{192,128},{196,132... | collective-permute-start | bytes 393224 | tf_op jit(solution)/shard_map/ppermute | solution.py:226
  99.0 17.5 %copy-start.3 = (bf16[256,512]{1,0:T(8,128)(2,1)S(1)}, bf16[256,512]{1,0:T(8,128)(2,1)}, u32[]{:S(2)}) copy-start(bf16[256,512]{1,0:T(8,128)(2,1)} %get-tuple-element.25) | copy-start | bytes 786436
  99.1 17.3 %collective-permute-start.10 = (bf16[256,512]{1,0:T(8,128)(2,1)S(1)}, bf16[256,512]{1,0:T(8,128)(2,1)S(1)}, u32[]{:S(2)}, u32[]{:S(2)}) collective-permute-start(bf16[256,512]{1,0:T(8,128)(2,1)S(1)} %add_convert_fusion.4), channel_id=1, source_target_pairs={{0,4},{4,64},{64,68},{68,128},{128,132},{132,192},{192,196},{196,0... | collective-permute-start | bytes 786440 | tf_op jit(solution)/shard_map/ppermute | solution.py:226
  101.2 24.2 %copy-start.6 = (bf16[256,512]{1,0:T(8,128)(2,1)S(1)}, bf16[256,512]{1,0:T(8,128)(2,1)}, u32[]{:S(2)}) copy-start(bf16[256,512]{1,0:T(8,128)(2,1)} %get-tuple-element.20) | copy-start | bytes 786436
  102.3 14.2 %collective-permute-start.14 = (bf16[256,512]{1,0:T(8,128)(2,1)S(1)}, bf16[256,512]{1,0:T(8,128)(2,1)S(1)}, u32[]{:S(2)}, u32[]{:S(2)}) collective-permute-start(bf16[256,512]{1,0:T(8,128)(2,1)S(1)} %add_convert_fusion.2), channel_id=1, source_target_pairs={{0,196},{4,0},{64,4},{68,64},{128,68},{132,128},{192,132},{196,192... | collective-permute-start | bytes 786440 | tf_op jit(solution)/shard_map/ppermute | solution.py:226
  103.0 29.4 %all-to-all-start.2 = ((bf16[32,8,2048]{2,1,0:T(8,128)(2,1)}), bf16[32,8,2048]{2,1,0:T(8,128)(2,1)S(1)}, u32[]{:S(2)}, u32[]{:S(2)}) async-start(bf16[32,8,2048]{2,1,0:T(8,128)(2,1)} %bitcast.17), calls=%async_computation.2 | async-start | bytes 2097152 | tf_op jit(solution)/shard_map/all_to_all | solution.py:293
  116.3 21.3 %copy-start = (s32[128,1]{0,1:T(1,128)S(1)}, s32[128,1]{0,1:T(1,128)}, u32[]{:S(2)}) copy-start(s32[128,1]{0,1:T(1,128)} %param.10) | copy-start | bytes 1540
  116.3 21.3 %copy-start.1 = (s32[16]{0:T(128)S(1)}, s32[16]{0:T(128)}, u32[]{:S(2)}) copy-start(s32[16]{0:T(128)} %head_ref.3) | copy-start | bytes 196
  116.4 9.0 %collective-permute-start.11 = (bf16[256,512]{1,0:T(8,128)(2,1)S(1)}, bf16[256,512]{1,0:T(8,128)(2,1)S(1)}, u32[]{:S(2)}, u32[]{:S(2)}) collective-permute-start(bf16[256,512]{1,0:T(8,128)(2,1)S(1)} %add_convert_fusion.3), channel_id=1, source_target_pairs={{0,4},{4,64},{64,68},{68,128},{128,132},{132,192},{192,196},{196,0... | collective-permute-start | bytes 786440 | tf_op jit(solution)/shard_map/ppermute | solution.py:226
  116.6 8.8 %collective-permute-start.15 = (bf16[256,512]{1,0:T(8,128)(2,1)S(1)}, bf16[256,512]{1,0:T(8,128)(2,1)S(1)}, u32[]{:S(2)}, u32[]{:S(2)}) collective-permute-start(bf16[256,512]{1,0:T(8,128)(2,1)S(1)} %add_convert_fusion.1), channel_id=1, source_target_pairs={{0,196},{4,0},{64,4},{68,64},{128,68},{132,128},{192,132},{196,192... | collective-permute-start | bytes 786440 | tf_op jit(solution)/shard_map/ppermute | solution.py:226
  132.3 14.2 %all-to-all-start.3 = ((bf16[32,8,512]{2,1,0:T(8,128)(2,1)}), bf16[32,8,512]{2,1,0:T(8,128)(2,1)S(1)}, u32[]{:S(2)}, u32[]{:S(2)}) async-start(bf16[32,8,512]{2,1,0:T(8,128)(2,1)} %fusion), calls=%async_computation.3 | async-start | bytes 524288 | tf_op jit(solution)/shard_map/all_to_all | solution.py:293
  (2 other events, 1.4 us)

commit v7 on v6

--- a/solution.py
+++ b/solution.py
@@ -310,7 +310,7 @@
         (*blocks, struct(slots, width_q)),
         inputs=0,
         far=10,
-        vmem=60,
+        vmem=57,
         scratch=[
             pltpu.VMEM((slots, 2 * width_q), BF),
             pltpu.VMEM((all_keys, width_kv), BF),

time: 148 us -> 148 us (level)
  no operation moved by 1% of the time
where the time goes in v7:
time: 148 us; the launch traced here: 147 us
  starting transfers between devices  57.2 us (39%)
  waiting for transfers between devices  48 us (32%)
  Pallas kernels  36.1 us (24%)
  other arithmetic  3.06 us (2%)
  local copies, waits for them, and re-layouts  2.09 us (1%)
    all_to_all x4, starting transfers between devices, over_plane(): return lax.all_to_all(array, PLANE, split_axis=0, concat_axis=0, tiled=True)  31.3 us
    ppermute x16, waiting for transfers between devices, step_by(): return lambda x: lax.ppermute(x, axis, pairs)  29.7 us
    pallas_call x1, Pallas kernels, per_device(): call(attend_kernel, 'attend', (*blocks, struct(slots, width_q)), inputs=0...  27.8 us
    ppermute x16, starting transfers between devices, step_by(): return lambda x: lax.ppermute(x, axis, pairs)  25.9 us
    all_to_all x4, waiting for transfers between devices, over_plane(): return lax.all_to_all(array, PLANE, split_axis=0, concat_axis=0, tiled=True)  18.3 us
    pallas_call x1, Pallas kernels, per_device(): call(pack_qg_kernel, 'pack_qg', struct(slots, 2 * width_q), scalars=1, in...  3.58 us
  transfers between devices with their start and end apart: 20, of which 9 were waited for; matrix products, arithmetic and copies ran while one was open for 2% of the time, Pallas kernels for 4%

profile of v7, /device:TPU:1, one launch (start us, length us, event | category | flops | bytes accessed | tf_op | source)
XLA Modules:
  0.0 147.3 jit_solution(15900521971277138703)
XLA Ops:
  0.6 1.9 %pack_kv.1 = bf16[256,512]{1,0:T(8,128)(2,1)} custom-call(s32[1,128]{1,0:T(1,128)} %bitcast.12, bf16[128,256]{1,0:T(8,128)(2,1)} %key_ref.1, bf16[128,256]{1,0:T(8,128)(2,1)} %value_ref.1), custom_call_target="tpu_custom_call" | custom-call | tf_op jit(solution)/shard_map/pack_kv/pallas_call | solution.py:295
  2.5 8.6 %all-to-all-start = ((bf16[32,8,512]{2,1,0:T(8,128)(2,1)}), bf16[32,8,512]{2,1,0:T(8,128)(2,1)S(1)}, u32[]{:S(2)}, u32[]{:S(2)}) async-start(bf16[32,8,512]{2,1,0:T(8,128)(2,1)} %bitcast.18), calls=%async_computation | async-start | bytes 524288 | tf_op jit(solution)/shard_map/all_to_all | solution.py:293
  11.1 3.6 %pack_qg.1 = bf16[256,4096]{1,0:T(8,128)(2,1)} custom-call(s32[16]{0:T(128)} %head_ref.3, s32[1,128]{1,0:T(1,128)} %bitcast.13, bf16[128,2048]{1,0:T(8,128)(2,1)} %query_ref.1, bf16[128,2048]{1,0:T(8,128)(2,1)} %grad_ref.1), custom_call_target="tpu_custom_call" | custom-call | tf_op jit(solution)/shard_map/pack_qg/pallas_call | solution.py:298
  14.7 5.3 %all-to-all-done = bf16[32,8,512]{2,1,0:T(8,128)(2,1)S(1)} async-done(((bf16[32,8,512]{2,1,0:T(8,128)(2,1)}), bf16[32,8,512]{2,1,0:T(8,128)(2,1)S(1)}, u32[]{:S(2)}, u32[]{:S(2)}) %all-to-all-start) | async-done | bytes 262176 | tf_op jit(solution)/shard_map/all_to_all | solution.py:293
  20.0 4.1 %all-to-all-start.1 = ((bf16[32,8,4096]{2,1,0:T(8,128)(2,1)}), bf16[32,8,4096]{2,1,0:T(8,128)(2,1)S(1)}, u32[]{:S(2)}, u32[]{:S(2)}) async-start(bf16[32,8,4096]{2,1,0:T(8,128)(2,1)} %bitcast.15), calls=%async_computation.1 | async-start | bytes 4194304 | tf_op jit(solution)/shard_map/all_to_all | solution.py:293
  24.2 5.7 %collective-permute-start.1 = (bf16[256,512]{1,0:T(8,128)(2,1)S(1)}, bf16[256,512]{1,0:T(8,128)(2,1)S(1)}, u32[]{:S(2)}, u32[]{:S(2)}) collective-permute-start(bf16[256,512]{1,0:T(8,128)(2,1)S(1)} %bitcast.19), channel_id=1, source_target_pairs={{0,196},{4,0},{64,4},{68,64},{128,68},{132,128},{192,132},{196,192... | collective-permute-start | bytes 786440 | tf_op jit(solution)/shard_map/ppermute | solution.py:226
  29.8 5.5 %collective-permute-done.1.refs_2_ = bf16[256,512]{1,0:T(8,128)(2,1)S(1)} collective-permute-done((bf16[256,512]{1,0:T(8,128)(2,1)S(1)}, bf16[256,512]{1,0:T(8,128)(2,1)S(1)}, u32[]{:S(2)}, u32[]{:S(2)}) %collective-permute-start.1) | collective-permute-done | bytes 262176 | tf_op jit(solution)/shard_map/ppermute | solution.py:226
  35.3 3.4 %collective-permute-start.3 = (bf16[256,512]{1,0:T(8,128)(2,1)S(1)}, bf16[256,512]{1,0:T(8,128)(2,1)S(1)}, u32[]{:S(2)}, u32[]{:S(2)}) collective-permute-start(bf16[256,512]{1,0:T(8,128)(2,1)S(1)} %collective-permute-done.1.refs_2_), channel_id=1, source_target_pairs={{0,196},{4,0},{64,4},{68,64},{128,68},{132,128},{192,132},{196,192... | collective-permute-start | bytes 786440 | tf_op jit(solution)/shard_map/ppermute | solution.py:226
  38.7 4.5 %collective-permute-done.3.refs_4_ = bf16[256,512]{1,0:T(8,128)(2,1)S(1)} collective-permute-done((bf16[256,512]{1,0:T(8,128)(2,1)S(1)}, bf16[256,512]{1,0:T(8,128)(2,1)S(1)}, u32[]{:S(2)}, u32[]{:S(2)}) %collective-permute-start.3) | collective-permute-done | bytes 262176 | tf_op jit(solution)/shard_map/ppermute | solution.py:226
  43.3 3.4 %collective-permute-start.5 = (bf16[256,512]{1,0:T(8,128)(2,1)S(1)}, bf16[256,512]{1,0:T(8,128)(2,1)S(1)}, u32[]{:S(2)}, u32[]{:S(2)}) collective-permute-start(bf16[256,512]{1,0:T(8,128)(2,1)S(1)} %collective-permute-done.3.refs_4_), channel_id=1, source_target_pairs={{0,196},{4,0},{64,4},{68,64},{128,68},{132,128},{192,132},{196,192... | collective-permute-start | bytes 786440 | tf_op jit(solution)/shard_map/ppermute | solution.py:226
  46.7 1.3 collective-permute-start.7
  48.0 1.4 collective-permute-start.6
  49.4 4.3 %collective-permute-done.7.refs_8_ = bf16[256,256]{1,0:T(8,128)(2,1)S(1)} collective-permute-done((bf16[256,256]{1,0:T(8,128)(2,1)S(1)}, bf16[256,256]{1,0:T(8,128)(2,1)S(1)}, u32[]{:S(2)}, u32[]{:S(2)}) %collective-permute-start.7) | collective-permute-done | bytes 131104 | tf_op jit(solution)/shard_map/ppermute | solution.py:226
  53.7 4.5 %collective-permute-done.6.refs_7_ = bf16[256,256]{1,0:T(8,128)(2,1)S(1)} collective-permute-done((bf16[256,256]{1,0:T(8,128)(2,1)S(1)}, bf16[256,256]{1,0:T(8,128)(2,1)S(1)}, u32[]{:S(2)}, u32[]{:S(2)}) %collective-permute-start.6) | collective-permute-done | bytes 131104 | tf_op jit(solution)/shard_map/ppermute | solution.py:226
  59.5 0.7 copy-done.2
  60.3 27.8 %attend.1 = (bf16[256,512]{1,0:T(8,128)(2,1)}, bf16[256,512]{1,0:T(8,128)(2,1)}, bf16[256,512]{1,0:T(8,128)(2,1)}, bf16[256,512]{1,0:T(8,128)(2,1)}, bf16[256,51...) custom-call(bf16[256,512]{1,0:T(8,128)(2,1)} %bitcast.21, ...), custom_call_target="tpu_custom_call" | custom-call | flops 10737418240 | bytes 7340032 | tf_op jit(solution)/shard_map/attend/pallas_call | solution.py:307
  88.1 0.9 collective-permute-start.8
  89.0 2.5 %collective-permute-start.12 = (bf16[256,512]{1,0:T(8,128)(2,1)}, bf16[256,512]{1,0:T(8,128)(2,1)S(1)}, u32[]{:S(2)}, u32[]{:S(2)}) collective-permute-start(bf16[256,512]{1,0:T(8,128)(2,1)} %get-tuple-element.27), channel_id=1, source_target_pairs={{0,196},{4,0},{64,4},{68,64},{128,68},{132,128},{192,132},{196,192... | collective-permute-start | bytes 786440 | tf_op jit(solution)/shard_map/ppermute | solution.py:226
  91.5 1.7 %collective-permute-start.13 = (bf16[256,256]{1,0:T(8,128)(2,1)}, bf16[256,256]{1,0:T(8,128)(2,1)S(1)}, u32[]{:S(2)}, u32[]{:S(2)}) collective-permute-start(bf16[256,256]{1,0:T(8,128)(2,1)} %get-tuple-element.28), channel_id=1, source_target_pairs={{0,192},{4,196},{64,0},{68,4},{128,64},{132,68},{192,128},{196,132... | collective-permute-start | bytes 393224 | tf_op jit(solution)/shard_map/ppermute | solution.py:226
  93.2 4.8 %collective-permute-done.9 = bf16[256,256]{1,0:T(8,128)(2,1)S(1)} collective-permute-done((bf16[256,256]{1,0:T(8,128)(2,1)}, bf16[256,256]{1,0:T(8,128)(2,1)S(1)}, u32[]{:S(2)}, u32[]{:S(2)}) %collective-permute-start.9) | collective-permute-done | bytes 131104 | tf_op jit(solution)/shard_map/ppermute | solution.py:226
  98.0 1.0 add_convert_fusion.4
  99.1 2.2 %collective-permute-start.10 = (bf16[256,512]{1,0:T(8,128)(2,1)S(1)}, bf16[256,512]{1,0:T(8,128)(2,1)S(1)}, u32[]{:S(2)}, u32[]{:S(2)}) collective-permute-start(bf16[256,512]{1,0:T(8,128)(2,1)S(1)} %add_convert_fusion.4), channel_id=1, source_target_pairs={{0,4},{4,64},{64,68},{68,128},{128,132},{132,192},{192,196},{196,0... | collective-permute-start | bytes 786440 | tf_op jit(solution)/shard_map/ppermute | solution.py:226
  101.2 1.1 add_convert_fusion.2
  103.0 13.3 %all-to-all-start.2 = ((bf16[32,8,2048]{2,1,0:T(8,128)(2,1)}), bf16[32,8,2048]{2,1,0:T(8,128)(2,1)S(1)}, u32[]{:S(2)}, u32[]{:S(2)}) async-start(bf16[32,8,2048]{2,1,0:T(8,128)(2,1)} %bitcast.17), calls=%async_computation.2 | async-start | bytes 2097152 | tf_op jit(solution)/shard_map/all_to_all | solution.py:293
  116.6 2.7 %collective-permute-start.15 = (bf16[256,512]{1,0:T(8,128)(2,1)S(1)}, bf16[256,512]{1,0:T(8,128)(2,1)S(1)}, u32[]{:S(2)}, u32[]{:S(2)}) collective-permute-start(bf16[256,512]{1,0:T(8,128)(2,1)S(1)} %add_convert_fusion.1), channel_id=1, source_target_pairs={{0,196},{4,0},{64,4},{68,64},{128,68},{132,128},{192,132},{196,192... | collective-permute-start | bytes 786440 | tf_op jit(solution)/shard_map/ppermute | solution.py:226
  119.3 6.1 %collective-permute-done.11 = bf16[256,512]{1,0:T(8,128)(2,1)S(1)} collective-permute-done((bf16[256,512]{1,0:T(8,128)(2,1)S(1)}, bf16[256,512]{1,0:T(8,128)(2,1)S(1)}, u32[]{:S(2)}, u32[]{:S(2)}) %collective-permute-start.11) | collective-permute-done | bytes 262176 | tf_op jit(solution)/shard_map/ppermute | solution.py:226
  125.4 0.8 fusion
  126.2 6.1 %all-to-all-done.2 = bf16[32,8,2048]{2,1,0:T(8,128)(2,1)S(1)} async-done(((bf16[32,8,2048]{2,1,0:T(8,128)(2,1)}), bf16[32,8,2048]{2,1,0:T(8,128)(2,1)S(1)}, u32[]{:S(2)}, u32[]{:S(2)}) %all-to-all-start.2) | async-done | bytes 1048608 | tf_op jit(solution)/shard_map/all_to_all | solution.py:293
  132.3 5.3 %all-to-all-start.3 = ((bf16[32,8,512]{2,1,0:T(8,128)(2,1)}), bf16[32,8,512]{2,1,0:T(8,128)(2,1)S(1)}, u32[]{:S(2)}, u32[]{:S(2)}) async-start(bf16[32,8,512]{2,1,0:T(8,128)(2,1)} %fusion), calls=%async_computation.3 | async-start | bytes 524288 | tf_op jit(solution)/shard_map/all_to_all | solution.py:293
  137.6 2.0 %unpack_q.1 = (bf16[128,2048]{1,0:T(8,128)(2,1)}, bf16[128,256]{1,0:T(8,128)(2,1)S(1)}) custom-call(s32[16]{0:T(128)S(1)} %copy-done.1, s32[1,128]{1,0:T(1,128)S(1)} %bitcast.14, bf16[256,2048]{1,0:T(8,128)(2,1)S(1)} %bitcast.10), custom_call_target="tpu_custom_call" | custom-call | tf_op jit(solution)/shard_map/unpack_q/pallas_call | solution.py:336
  139.6 6.9 %all-to-all-done.3 = bf16[32,8,512]{2,1,0:T(8,128)(2,1)S(1)} async-done(((bf16[32,8,512]{2,1,0:T(8,128)(2,1)}), bf16[32,8,512]{2,1,0:T(8,128)(2,1)S(1)}, u32[]{:S(2)}, u32[]{:S(2)}) %all-to-all-start.3) | async-done | bytes 262176 | tf_op jit(solution)/shard_map/all_to_all | solution.py:293
  146.5 0.8 unpack_kv.1
  (48 shorter events, 2.3 us)
Async XLA Ops:
  2.5 17.5 %all-to-all-start = ((bf16[32,8,512]{2,1,0:T(8,128)(2,1)}), bf16[32,8,512]{2,1,0:T(8,128)(2,1)S(1)}, u32[]{:S(2)}, u32[]{:S(2)}) async-start(bf16[32,8,512]{2,1,0:T(8,128)(2,1)} %bitcast.18), calls=%async_computation | async-start | bytes 524288 | tf_op jit(solution)/shard_map/all_to_all | solution.py:293
  20.0 9.8 %copy-start.5 = (bf16[32,8,512]{2,1,0:T(8,128)(2,1)}, bf16[32,8,512]{2,1,0:T(8,128)(2,1)S(1)}, u32[]{:S(2)}) copy-start(bf16[32,8,512]{2,1,0:T(8,128)(2,1)S(1)} %all-to-all-done) | copy-start | bytes 786436
  20.0 38.8 %all-to-all-start.1 = ((bf16[32,8,4096]{2,1,0:T(8,128)(2,1)}), bf16[32,8,4096]{2,1,0:T(8,128)(2,1)S(1)}, u32[]{:S(2)}, u32[]{:S(2)}) async-start(bf16[32,8,4096]{2,1,0:T(8,128)(2,1)} %bitcast.15), calls=%async_computation.1 | async-start | bytes 4194304 | tf_op jit(solution)/shard_map/all_to_all | solution.py:293
  24.2 11.1 %collective-permute-start.1 = (bf16[256,512]{1,0:T(8,128)(2,1)S(1)}, bf16[256,512]{1,0:T(8,128)(2,1)S(1)}, u32[]{:S(2)}, u32[]{:S(2)}) collective-permute-start(bf16[256,512]{1,0:T(8,128)(2,1)S(1)} %bitcast.19), channel_id=1, source_target_pairs={{0,196},{4,0},{64,4},{68,64},{128,68},{132,128},{192,132},{196,192... | collective-permute-start | bytes 786440 | tf_op jit(solution)/shard_map/ppermute | solution.py:226
  29.8 8.9 %collective-permute-start = (bf16[256,512]{1,0:T(8,128)(2,1)S(1)}, bf16[256,512]{1,0:T(8,128)(2,1)S(1)}, u32[]{:S(2)}, u32[]{:S(2)}) collective-permute-start(bf16[256,512]{1,0:T(8,128)(2,1)S(1)} %bitcast.20), channel_id=1, source_target_pairs={{0,4},{4,64},{64,68},{68,128},{128,132},{132,192},{192,196},{196,0... | collective-permute-start | bytes 786440 | tf_op jit(solution)/shard_map/ppermute | solution.py:226
  35.3 23.6 %copy-start.9 = (bf16[256,512]{1,0:T(8,128)(2,1)}, bf16[256,512]{1,0:T(8,128)(2,1)S(1)}, u32[]{:S(2)}) copy-start(bf16[256,512]{1,0:T(8,128)(2,1)S(1)} %collective-permute-done.1.refs_2_) | copy-start | bytes 786436
  35.3 8.0 %collective-permute-start.3 = (bf16[256,512]{1,0:T(8,128)(2,1)S(1)}, bf16[256,512]{1,0:T(8,128)(2,1)S(1)}, u32[]{:S(2)}, u32[]{:S(2)}) collective-permute-start(bf16[256,512]{1,0:T(8,128)(2,1)S(1)} %collective-permute-done.1.refs_2_), channel_id=1, source_target_pairs={{0,196},{4,0},{64,4},{68,64},{128,68},{132,128},{192,132},{196,192... | collective-permute-start | bytes 786440 | tf_op jit(solution)/shard_map/ppermute | solution.py:226
  38.7 20.2 %copy-start.10 = (bf16[256,512]{1,0:T(8,128)(2,1)}, bf16[256,512]{1,0:T(8,128)(2,1)S(1)}, u32[]{:S(2)}) copy-start(bf16[256,512]{1,0:T(8,128)(2,1)S(1)} %collective-permute-done.refs_1_) | copy-start | bytes 786436
  38.7 8.0 %collective-permute-start.2 = (bf16[256,512]{1,0:T(8,128)(2,1)S(1)}, bf16[256,512]{1,0:T(8,128)(2,1)S(1)}, u32[]{:S(2)}, u32[]{:S(2)}) collective-permute-start(bf16[256,512]{1,0:T(8,128)(2,1)S(1)} %collective-permute-done.refs_1_), channel_id=1, source_target_pairs={{0,4},{4,64},{64,68},{68,128},{128,132},{132,192},{192,196},{196,0... | collective-permute-start | bytes 786440 | tf_op jit(solution)/shard_map/ppermute | solution.py:226
  43.3 15.6 %copy-start.7 = (bf16[256,512]{1,0:T(8,128)(2,1)}, bf16[256,512]{1,0:T(8,128)(2,1)S(1)}, u32[]{:S(2)}) copy-start(bf16[256,512]{1,0:T(8,128)(2,1)S(1)} %collective-permute-done.3.refs_4_) | copy-start | bytes 786436
  43.3 14.9 %collective-permute-start.5 = (bf16[256,512]{1,0:T(8,128)(2,1)S(1)}, bf16[256,512]{1,0:T(8,128)(2,1)S(1)}, u32[]{:S(2)}, u32[]{:S(2)}) collective-permute-start(bf16[256,512]{1,0:T(8,128)(2,1)S(1)} %collective-permute-done.3.refs_4_), channel_id=1, source_target_pairs={{0,196},{4,0},{64,4},{68,64},{128,68},{132,128},{192,132},{196,192... | collective-permute-start | bytes 786440 | tf_op jit(solution)/shard_map/ppermute | solution.py:226
  46.7 12.2 %copy-start.8 = (bf16[256,512]{1,0:T(8,128)(2,1)}, bf16[256,512]{1,0:T(8,128)(2,1)S(1)}, u32[]{:S(2)}) copy-start(bf16[256,512]{1,0:T(8,128)(2,1)S(1)} %collective-permute-done.2.refs_3_) | copy-start | bytes 786436
  46.7 12.2 %collective-permute-start.4 = (bf16[256,512]{1,0:T(8,128)(2,1)S(1)}, bf16[256,512]{1,0:T(8,128)(2,1)}, u32[]{:S(2)}, u32[]{:S(2)}) collective-permute-start(bf16[256,512]{1,0:T(8,128)(2,1)S(1)} %collective-permute-done.2.refs_3_), channel_id=1, source_target_pairs={{0,4},{4,64},{64,68},{68,128},{128,132},{132,192},{192,196},{196,0... | collective-permute-start | bytes 786440 | tf_op jit(solution)/shard_map/ppermute | solution.py:226
  46.7 7.0 %collective-permute-start.7 = (bf16[256,256]{1,0:T(8,128)(2,1)S(1)}, bf16[256,256]{1,0:T(8,128)(2,1)S(1)}, u32[]{:S(2)}, u32[]{:S(2)}) collective-permute-start(bf16[256,256]{1,0:T(8,128)(2,1)S(1)} %slice.9), channel_id=1, source_target_pairs={{0,192},{4,196},{64,0},{68,4},{128,64},{132,68},{192,128},{196,132... | collective-permute-start | bytes 393224 | tf_op jit(solution)/shard_map/ppermute | solution.py:226
  48.0 10.1 %collective-permute-start.6 = (bf16[256,256]{1,0:T(8,128)(2,1)S(1)}, bf16[256,256]{1,0:T(8,128)(2,1)S(1)}, u32[]{:S(2)}, u32[]{:S(2)}) collective-permute-start(bf16[256,256]{1,0:T(8,128)(2,1)S(1)} %slice.8), channel_id=1, source_target_pairs={{0,64},{4,68},{64,128},{68,132},{128,192},{132,196},{192,0},{196,4... | collective-permute-start | bytes 393224 | tf_op jit(solution)/shard_map/ppermute | solution.py:226
  53.7 5.2 %copy-start.12 = (bf16[256,256]{1,0:T(8,128)(2,1)}, bf16[256,256]{1,0:T(8,128)(2,1)S(1)}, u32[]{:S(2)}) copy-start(bf16[256,256]{1,0:T(8,128)(2,1)S(1)} %collective-permute-done.7.refs_8_) | copy-start | bytes 393220
  58.9 1.4 copy-start.2
  88.1 28.3 %copy-start.4 = (bf16[256,512]{1,0:T(8,128)(2,1)S(1)}, bf16[256,512]{1,0:T(8,128)(2,1)}, u32[]{:S(2)}) copy-start(bf16[256,512]{1,0:T(8,128)(2,1)} %get-tuple-element.21) | copy-start | bytes 786436
  88.1 9.9 %collective-permute-start.8 = (bf16[256,512]{1,0:T(8,128)(2,1)}, bf16[256,512]{1,0:T(8,128)(2,1)S(1)}, u32[]{:S(2)}, u32[]{:S(2)}) collective-permute-start(bf16[256,512]{1,0:T(8,128)(2,1)} %get-tuple-element.23), channel_id=1, source_target_pairs={{0,4},{4,64},{64,68},{68,128},{128,132},{132,192},{192,196},{196,0... | collective-permute-start | bytes 786440 | tf_op jit(solution)/shard_map/ppermute | solution.py:226
  89.0 9.0 %collective-permute-start.9 = (bf16[256,256]{1,0:T(8,128)(2,1)}, bf16[256,256]{1,0:T(8,128)(2,1)S(1)}, u32[]{:S(2)}, u32[]{:S(2)}) collective-permute-start(bf16[256,256]{1,0:T(8,128)(2,1)} %get-tuple-element.24), channel_id=1, source_target_pairs={{0,64},{4,68},{64,128},{68,132},{128,192},{132,196},{192,0},{196,4... | collective-permute-start | bytes 393224 | tf_op jit(solution)/shard_map/ppermute | solution.py:226
  89.0 12.2 %collective-permute-start.12 = (bf16[256,512]{1,0:T(8,128)(2,1)}, bf16[256,512]{1,0:T(8,128)(2,1)S(1)}, u32[]{:S(2)}, u32[]{:S(2)}) collective-permute-start(bf16[256,512]{1,0:T(8,128)(2,1)} %get-tuple-element.27), channel_id=1, source_target_pairs={{0,196},{4,0},{64,4},{68,64},{128,68},{132,128},{192,132},{196,192... | collective-permute-start | bytes 786440 | tf_op jit(solution)/shard_map/ppermute | solution.py:226
  91.5 9.7 %collective-permute-start.13 = (bf16[256,256]{1,0:T(8,128)(2,1)}, bf16[256,256]{1,0:T(8,128)(2,1)S(1)}, u32[]{:S(2)}, u32[]{:S(2)}) collective-permute-start(bf16[256,256]{1,0:T(8,128)(2,1)} %get-tuple-element.28), channel_id=1, source_target_pairs={{0,192},{4,196},{64,0},{68,4},{128,64},{132,68},{192,128},{196,132... | collective-permute-start | bytes 393224 | tf_op jit(solution)/shard_map/ppermute | solution.py:226
  99.0 17.5 %copy-start.3 = (bf16[256,512]{1,0:T(8,128)(2,1)S(1)}, bf16[256,512]{1,0:T(8,128)(2,1)}, u32[]{:S(2)}) copy-start(bf16[256,512]{1,0:T(8,128)(2,1)} %get-tuple-element.25) | copy-start | bytes 786436
  99.1 17.3 %collective-permute-start.10 = (bf16[256,512]{1,0:T(8,128)(2,1)S(1)}, bf16[256,512]{1,0:T(8,128)(2,1)S(1)}, u32[]{:S(2)}, u32[]{:S(2)}) collective-permute-start(bf16[256,512]{1,0:T(8,128)(2,1)S(1)} %add_convert_fusion.4), channel_id=1, source_target_pairs={{0,4},{4,64},{64,68},{68,128},{128,132},{132,192},{192,196},{196,0... | collective-permute-start | bytes 786440 | tf_op jit(solution)/shard_map/ppermute | solution.py:226
  101.2 24.2 %copy-start.6 = (bf16[256,512]{1,0:T(8,128)(2,1)S(1)}, bf16[256,512]{1,0:T(8,128)(2,1)}, u32[]{:S(2)}) copy-start(bf16[256,512]{1,0:T(8,128)(2,1)} %get-tuple-element.20) | copy-start | bytes 786436
  102.3 14.2 %collective-permute-start.14 = (bf16[256,512]{1,0:T(8,128)(2,1)S(1)}, bf16[256,512]{1,0:T(8,128)(2,1)S(1)}, u32[]{:S(2)}, u32[]{:S(2)}) collective-permute-start(bf16[256,512]{1,0:T(8,128)(2,1)S(1)} %add_convert_fusion.2), channel_id=1, source_target_pairs={{0,196},{4,0},{64,4},{68,64},{128,68},{132,128},{192,132},{196,192... | collective-permute-start | bytes 786440 | tf_op jit(solution)/shard_map/ppermute | solution.py:226
  103.0 29.4 %all-to-all-start.2 = ((bf16[32,8,2048]{2,1,0:T(8,128)(2,1)}), bf16[32,8,2048]{2,1,0:T(8,128)(2,1)S(1)}, u32[]{:S(2)}, u32[]{:S(2)}) async-start(bf16[32,8,2048]{2,1,0:T(8,128)(2,1)} %bitcast.17), calls=%async_computation.2 | async-start | bytes 2097152 | tf_op jit(solution)/shard_map/all_to_all | solution.py:293
  116.3 21.3 %copy-start = (s32[128,1]{0,1:T(1,128)S(1)}, s32[128,1]{0,1:T(1,128)}, u32[]{:S(2)}) copy-start(s32[128,1]{0,1:T(1,128)} %param.10) | copy-start | bytes 1540
  116.3 21.3 %copy-start.1 = (s32[16]{0:T(128)S(1)}, s32[16]{0:T(128)}, u32[]{:S(2)}) copy-start(s32[16]{0:T(128)} %head_ref.3) | copy-start | bytes 196
  116.4 9.0 %collective-permute-start.11 = (bf16[256,512]{1,0:T(8,128)(2,1)S(1)}, bf16[256,512]{1,0:T(8,128)(2,1)S(1)}, u32[]{:S(2)}, u32[]{:S(2)}) collective-permute-start(bf16[256,512]{1,0:T(8,128)(2,1)S(1)} %add_convert_fusion.3), channel_id=1, source_target_pairs={{0,4},{4,64},{64,68},{68,128},{128,132},{132,192},{192,196},{196,0... | collective-permute-start | bytes 786440 | tf_op jit(solution)/shard_map/ppermute | solution.py:226
  116.6 8.8 %collective-permute-start.15 = (bf16[256,512]{1,0:T(8,128)(2,1)S(1)}, bf16[256,512]{1,0:T(8,128)(2,1)S(1)}, u32[]{:S(2)}, u32[]{:S(2)}) collective-permute-start(bf16[256,512]{1,0:T(8,128)(2,1)S(1)} %add_convert_fusion.1), channel_id=1, source_target_pairs={{0,196},{4,0},{64,4},{68,64},{128,68},{132,128},{192,132},{196,192... | collective-permute-start | bytes 786440 | tf_op jit(solution)/shard_map/ppermute | solution.py:226
  132.3 14.2 %all-to-all-start.3 = ((bf16[32,8,512]{2,1,0:T(8,128)(2,1)}), bf16[32,8,512]{2,1,0:T(8,128)(2,1)S(1)}, u32[]{:S(2)}, u32[]{:S(2)}) async-start(bf16[32,8,512]{2,1,0:T(8,128)(2,1)} %fusion), calls=%async_computation.3 | async-start | bytes 524288 | tf_op jit(solution)/shard_map/all_to_all | solution.py:293
  (2 other events, 1.4 us)
